TPU v7x, 32 devices: a whole 2x2x4 slice. The times are simulated.
32 devices in a mesh: case: 4 (over y, core), mod: 8 (over z, x).
Axes of the slice: x: 2, y: 2, z: 4, core: 2. Of those that a mesh axis runs over, the one named last changes fastest.
Arguments:
- turbulence: float32 [4, 256, 256], P('case'), may hold values from -6 to 6
- pupil_amp: float32 [256, 256], replicated, may hold values from 0.3 to 1
- mod_points: int32 [8], P('mod'), may hold values from 0 to 255
- valid_pix: int32 [8192], P('mod'), may hold values from 0 to 262143, as said below
- recon: bfloat16 [5120, 8192], P('case', 'mod'), may hold values from -0.0625 to 0.0625
- gx: float32 [256, 64], replicated, may hold values from -1.2 to 1.2
- gy: float32 [256, 80], replicated, may hold values from -1.2 to 1.2
- act_map: int32 [5120], replicated, may hold values from 0 to 5119, each once
Outputs:
- command_total: float32 [4, 5120], P('case')
- frame: float32 [4, 512, 512], P('case', 'mod')
Inputs may be any that keep to these rules, and one draw needn't show every extreme that they name: `valid_pix`: entries k * 1024 to (k + 1) * 1024 - 1 are flat indices (row times 512 plus column) of pixels in detector rows k * 64 to (k + 1) * 64 - 1.
All inputs are finite; a program needn't handle non-finite values.
Results may differ from a plain program's by a relative error of at most 0.0058.
Values may be sent and summed in bfloat16 or wider, within the bound.
No kernel may reach another device: no remote copies, remote signals or barrier semaphores. Data moves between devices by JAX's collectives and lax.ppermute only.
A program may use at most 64 MiB of HBM per device.

v0:
```python
import math

import jax
import jax.numpy as jnp
from jax import lax
from jax.sharding import PartitionSpec as P

STEPS = 2


loop_gain = 0.5
radius_pixels = 6.0
point_count = 256


def phase_table(length, pupil_width, sign_factor):
    centred = jnp.arange(length, dtype=jnp.int32) - length // 2
    position = jnp.arange(pupil_width, dtype=jnp.int32)
    wrapped = jnp.mod(centred[:, None] * position[None, :], length).astype(jnp.float32)
    angles = 2.0 * math.pi / length * wrapped
    factor = 1.0 / math.sqrt(length)
    return (jnp.cos(angles) * factor, sign_factor * jnp.sin(angles) * factor)


def optics_tables(pupil_size, length):
    fwd_cos, fwd_sin = phase_table(length, pupil_size, -1.0)
    inv_cos, inv_sin = phase_table(length, length, 1.0)
    inv_cos = inv_cos.T
    inv_sin = inv_sin.T
    table_one = jnp.concatenate([fwd_cos, fwd_sin], 0).astype(jnp.bfloat16)
    table_two = jnp.concatenate(
        [jnp.concatenate([fwd_cos.T, fwd_sin.T], 1), jnp.concatenate([-fwd_sin.T, fwd_cos.T], 1)], 0
    ).astype(jnp.bfloat16)
    table_three = jnp.concatenate([inv_cos, inv_sin], 0).astype(jnp.bfloat16)
    table_four = jnp.concatenate(
        [jnp.concatenate([inv_cos.T, inv_sin.T], 1), jnp.concatenate([-inv_sin.T, inv_cos.T], 1)], 0
    ).astype(jnp.bfloat16)
    offset = jnp.abs(jnp.arange(length, dtype=jnp.float32) - length // 2)
    mask_angle = 0.5 * math.pi * (offset[:, None] + offset[None, :])
    return (table_one, table_two, table_three, table_four, jnp.cos(mask_angle), jnp.sin(mask_angle))


def detector_frame(pupil_phase, amplitude, mod_point, tables):
    table_one, table_two, table_three, table_four, mask_cos, mask_sin = tables
    pupil_size = pupil_phase.shape[0]
    length = mask_cos.shape[0]
    centred = jnp.arange(pupil_size, dtype=jnp.float32) - pupil_size // 2
    tilt_angle = 2.0 * math.pi / point_count * mod_point.astype(jnp.float32)
    tilt_phase = (
        2.0
        * math.pi
        * radius_pixels
        / length
        * (centred[:, None] * jnp.cos(tilt_angle) + centred[None, :] * jnp.sin(tilt_angle))
    )
    total_phase = pupil_phase + tilt_phase
    pupil_field = jnp.concatenate(
        [amplitude * jnp.cos(total_phase), amplitude * jnp.sin(total_phase)], 1
    ).astype(jnp.bfloat16)
    section_one = jnp.dot(table_one, pupil_field, preferred_element_type=jnp.float32)
    real_part = section_one[:length, :pupil_size] - section_one[length:, pupil_size:]
    imag_part = section_one[:length, pupil_size:] + section_one[length:, :pupil_size]
    focal_half = jnp.concatenate([real_part, imag_part], 1).astype(jnp.bfloat16)
    focal_field = jnp.dot(focal_half, table_two, preferred_element_type=jnp.float32)
    focal_real = focal_field[:, :length]
    focal_imag = focal_field[:, length:]
    masked = jnp.concatenate(
        [
            focal_real * mask_cos - focal_imag * mask_sin,
            focal_real * mask_sin + focal_imag * mask_cos,
        ],
        1,
    ).astype(jnp.bfloat16)
    section_three = jnp.dot(table_three, masked, preferred_element_type=jnp.float32)
    inverse_half = jnp.concatenate(
        [
            section_three[:length, :length] - section_three[length:, length:],
            section_three[:length, length:] + section_three[length:, :length],
        ],
        1,
    ).astype(jnp.bfloat16)
    detector_field = jnp.dot(inverse_half, table_four, preferred_element_type=jnp.float32)
    return detector_field[:, :length] ** 2 + detector_field[:, length:] ** 2


def mirror_surface(commands, act_map, gx, gy):
    actuator_grid = commands[act_map].reshape(gx.shape[1], gy.shape[1])
    rows_mapped = jnp.dot(
        gx, actuator_grid, precision=lax.Precision.HIGHEST, preferred_element_type=jnp.float32
    )
    return jnp.dot(
        rows_mapped, gy.T, precision=lax.Precision.HIGHEST, preferred_element_type=jnp.float32
    )


def body(turbulence, pupil_amp, mod_points, valid_pix, recon, gx, gy, act_map):
    pupil_size = pupil_amp.shape[0]
    length = 2 * pupil_size
    tables = optics_tables(pupil_size, length)
    screen = turbulence[0]
    mod_point = mod_points[0]
    devices_mod = lax.axis_size("mod")
    row_count = length // devices_mod
    command_total = jnp.zeros((1, act_map.shape[0]), jnp.float32)
    pupil_phase = screen
    frame_block = jnp.zeros((row_count, length), jnp.float32)
    for iteration in range(STEPS):
        frame_term = detector_frame(pupil_phase, pupil_amp, mod_point, tables) / devices_mod
        frame_block = lax.psum_scatter(frame_term, "mod", scatter_dimension=0, tiled=True)
        local_index = valid_pix - lax.axis_index("mod") * (row_count * length)
        signal = frame_block.reshape(-1)[local_index].astype(jnp.bfloat16)
        signals = lax.all_gather(signal[None, :], "case", axis=0, tiled=True)
        partial_commands = lax.dot_general(
            signals, recon, (((1,), (1,)), ((), ())), preferred_element_type=jnp.float32
        )
        summed_commands = lax.psum(partial_commands, "mod")
        own_commands = lax.all_to_all(
            summed_commands, "case", split_axis=0, concat_axis=1, tiled=True
        )
        command_total = command_total + loop_gain * own_commands
        if iteration + 1 < STEPS:
            pupil_phase = screen - mirror_surface(command_total[0], act_map, gx, gy)
    return (command_total, frame_block[None])


def solution(mesh):
    return jax.shard_map(
        body,
        mesh=mesh,
        in_specs=(P("case", None, None), P(), P("mod"), P("mod"), P("case", "mod"), P(), P(), P()),
        out_specs=(P("case", None), P("case", "mod", None)),
        check_vma=False,
    )
```

profile of v0, /device:TPU:0, one launch (start us, length us, event | category | flops | bytes accessed | tf_op | source)
XLA Modules:
  0.0 328.0 jit_solution(16047453606565163714)
XLA Ops:
  8.2 3.1 multiply_convert_fusion.5
  11.4 3.0 fusion.64
  14.4 9.8 %fusion.39 = (bf16[512,512]{1,0:T(8,128)(2,1)}, bf16[512,512]{1,0:T(8,128)(2,1)}, bf16[512,512]{1,0:T(8,128)(2,1)}, bf16[512,512]{1,0:T(8,128)(2,1)}, bf16[512,512]{1,0:T(8,128)(2,1)}) fusion(s32[512]{0:T(512)S(1)} %iota_add_fusion), kind=kLoop, calls=%fused_computation.72 | loop fusion | flops 9961472 | bytes 2623488 | tf_op jit(solution)/shard_map/convert.13
  24.3 1.1 copy.21
  25.4 1.2 multiply_convert_fusion.9
  26.7 1.5 fusion.66
  29.1 4.7 %subtract_convert_fusion.1 = (bf16[512,512]{1,0:T(8,128)(2,1)S(1)}, bf16[512,512]{1,0:T(8,128)(2,1)S(1)}) fusion(f32[512,1024]{1,0:T(8,128)S(1)} %fusion.50, f32[512]{0:T(512)S(1)} %add_abs_fusion), kind=kLoop, calls=%fused_computation.62 | loop fusion | flops 2621440 | bytes 3149824 | tf_op jit(solution)/shard_map/convert.16
  33.8 1.3 fusion.15
  36.5 1.3 fusion.19
  37.8 1.2 fusion.12
  39.1 66.3 %reduce-scatter.3.cloned.1.call-done = f32[64,512]{1,0:T(8,128)} async-done(((f32[512,512]{1,0:T(8,128)}), f32[64,512]{1,0:T(8,128)}) %reduce-scatter.3.cloned.1.call-update) | async-done | bytes 131088 | tf_op jit(solution)/shard_map/reduce_scatter | solution.py:109
  105.3 0.9 copy.27
  106.3 6.8 %gather_fusion = bf16[1024]{0:T(1024)(128)(2,1)S(1)} fusion(bf16[32768]{0:T(1024)(128)(2,1)S(1)} %bitcast.29, s32[1024]{0:T(1024)S(1)} %fusion.74), kind=kCustom, calls=%fused_computation | custom fusion | bytes 8192 | tf_op jit(solution)/shard_map/gather | solution.py:111
  113.1 5.2 %all-gather = bf16[4096]{0:T(1024)(128)(2,1)S(1)} all-gather(bf16[1024]{0:T(1024)(128)(2,1)S(1)} %gather_fusion), channel_id=2, replica_groups=mesh['case'=4,'mod'=8] {'case'}, dimensions={0}, use_global_device_ids=true | all-gather | bytes 10240 | tf_op jit(solution)/shard_map/all_gather | solution.py:112
  118.3 0.8 convolution_bitcast_fusion.1
  119.1 35.2 %psum.14 = f32[4,1,1280]{2,0,1:T(4,128)S(1)} all-reduce(f32[4,1,1280]{2,0,1:T(4,128)S(1)} %convolution_bitcast_fusion.1), channel_id=1, replica_groups=mesh['case'=4,'mod'=8] {'mod'}, use_global_device_ids=true, to_apply=%region_1.2 | all-reduce | flops 5120 | bytes 40960 | tf_op jit(solution)/shard_map/psum | solution.py:116
  154.9 3.3 all-to-all-start
  158.4 3.6 %all-to-all-done = f32[4,1,1280]{2,1,0:T(1,128)S(1)} async-done(((f32[4,1,1280]{2,1,0:T(1,128)}), f32[4,1,1280]{2,1,0:T(1,128)S(1)}, u32[]{:S(2)}, u32[]{:S(2)}) %all-to-all-start) | async-done | bytes 20512 | tf_op jit(solution)/shard_map/all_to_all | solution.py:117
  162.0 28.7 %gather_fusion.1 = f32[5120]{0:T(1024)S(1)} fusion(f32[5120]{0:T(1024)S(1)} %bitcast.28, s32[5120]{0:T(1024)S(1)} %fusion.73), kind=kCustom, calls=%fused_computation.1 | custom fusion | bytes 61440 | tf_op jit(solution)/shard_map/gather | solution.py:87
  191.0 2.2 multiply_convert_fusion.7
  193.3 1.5 fusion.65
  195.8 4.7 %subtract_convert_fusion = (bf16[512,512]{1,0:T(8,128)(2,1)S(1)}, bf16[512,512]{1,0:T(8,128)(2,1)S(1)}) fusion(f32[512,1024]{1,0:T(8,128)S(1)} %fusion.54, f32[512]{0:T(512)S(1)} %copy-done.20), kind=kLoop, calls=%fused_computation.55 | loop fusion | flops 2621440 | bytes 3149824 | tf_op jit(solution)/shard_map/convert.2
  200.5 1.3 fusion.23
  203.2 1.3 fusion.27
  204.5 1.2 fusion.8
  205.7 59.6 %reduce-scatter.5.cloned.1.call-done = f32[64,512]{1,0:T(8,128)} async-done(((f32[512,512]{1,0:T(8,128)}), f32[64,512]{1,0:T(8,128)}) %reduce-scatter.5.cloned.1.call-update) | async-done | bytes 131088 | tf_op jit(solution)/shard_map/reduce_scatter | solution.py:109
  265.3 0.9 copy.28
  266.2 6.8 %gather_fusion.2 = bf16[1024]{0:T(1024)(128)(2,1)S(1)} fusion(bf16[32768]{0:T(1024)(128)(2,1)S(1)} %bitcast.30, s32[1024]{0:T(1024)S(1)} %copy-done.22), kind=kCustom, calls=%fused_computation.2 | custom fusion | bytes 8192 | tf_op jit(solution)/shard_map/gather | solution.py:111
  273.0 5.2 %all-gather.1 = bf16[4096]{0:T(1024)(128)(2,1)S(1)} all-gather(bf16[1024]{0:T(1024)(128)(2,1)S(1)} %gather_fusion.2), channel_id=3, replica_groups=mesh['case'=4,'mod'=8] {'case'}, dimensions={0}, use_global_device_ids=true | all-gather | bytes 10240 | tf_op jit(solution)/shard_map/all_gather | solution.py:112
  278.2 0.8 convolution_bitcast_fusion
  279.0 35.2 %psum.15 = f32[4,1,1280]{2,0,1:T(4,128)S(1)} all-reduce(f32[4,1,1280]{2,0,1:T(4,128)S(1)} %convolution_bitcast_fusion), channel_id=1, replica_groups=mesh['case'=4,'mod'=8] {'mod'}, use_global_device_ids=true, to_apply=%region_3.4 | all-reduce | flops 5120 | bytes 40960 | tf_op jit(solution)/shard_map/psum | solution.py:116
  314.1 6.4 %all_to_all.26 = f32[4,1,1280]{2,1,0:T(1,128)S(1)} all-to-all(f32[4,1,1280]{2,1,0:T(1,128)S(1)} %copy.26), channel_id=1, replica_groups=mesh['case'=4,'mod'=8] {'case'}, dimensions={0} | all-to-all | bytes 40960 | tf_op jit(solution)/shard_map/all_to_all | solution.py:117
  (78 shorter events, 6.7 us)
Async XLA Ops:
  7.2 111.1 %copy-start = (bf16[1280,1024]{1,0:T(8,128)(2,1)S(1)}, bf16[1280,1024]{1,0:T(8,128)(2,1)}, u32[]{:S(2)}) copy-start(bf16[1280,1024]{1,0:T(8,128)(2,1)} %param.12) | copy-start | bytes 7864324
  7.2 17.0 %copy-start.17 = (f32[1,256,256]{2,1,0:T(8,128)S(1)}, f32[1,256,256]{2,1,0:T(8,128)}, u32[]{:S(2)}) copy-start(f32[1,256,256]{2,1,0:T(8,128)} %param.8) | copy-start | bytes 786436
  7.2 98.2 %reduce-scatter.3.cloned.1.call-start = ((), (), s32[]{:S(2)}) async-start(), calls=%async_computation.4 | async-start | bytes 1179648 | tf_op jit(solution)/shard_map/reduce_scatter | solution.py:109
  14.4 14.7 %copy-start.19 = (f32[512]{0:T(512)}, f32[512]{0:T(512)S(1)}, u32[]{:S(2)}) copy-start(f32[512]{0:T(512)S(1)} %add_abs_fusion) | copy-start | bytes 6148
  25.4 1.2 copy-start.24
  25.4 1.2 copy-start.25
  26.7 1.7 copy-start.11
  26.7 1.7 copy-start.13
  26.7 1.7 copy-start.15
  29.1 4.7 %copy-start.7 = (bf16[512,512]{1,0:T(8,128)(2,1)S(1)}, bf16[512,512]{1,0:T(8,128)(2,1)}, u32[]{:S(2)}) copy-start(bf16[512,512]{1,0:T(8,128)(2,1)} %get-tuple-element.19) | copy-start | bytes 1572868
  29.1 4.7 %copy-start.9 = (bf16[512,512]{1,0:T(8,128)(2,1)S(1)}, bf16[512,512]{1,0:T(8,128)(2,1)}, u32[]{:S(2)}) copy-start(bf16[512,512]{1,0:T(8,128)(2,1)} %get-tuple-element.22) | copy-start | bytes 1572868
  35.1 1.0 copy-start.1
  35.2 1.2 copy-start.3
  35.2 1.3 copy-start.5
  37.8 1.3 copy-start.26
  39.1 80.0 %copy-start.21 = (s32[1024]{0:T(1024)}, s32[1024]{0:T(1024)S(1)}, u32[]{:S(2)}) copy-start(s32[1024]{0:T(1024)S(1)} %fusion.74) | copy-start | bytes 12292
  106.3 52.1 %copy-start.23 = (s32[5120]{0:T(1024)S(1)}, s32[5120]{0:T(1024)}, u32[]{:S(2)}) copy-start(s32[5120]{0:T(1024)} %param.15) | copy-start | bytes 61444
  154.9 7.1 %all-to-all-start = ((f32[4,1,1280]{2,1,0:T(1,128)}), f32[4,1,1280]{2,1,0:T(1,128)S(1)}, u32[]{:S(2)}, u32[]{:S(2)}) async-start(f32[4,1,1280]{2,1,0:T(1,128)} %copy.23), calls=%async_computation.1 | async-start | bytes 40960 | tf_op jit(solution)/shard_map/all_to_all | solution.py:117
  158.1 107.1 %reduce-scatter.5.cloned.1.call-start = ((), (), s32[]{:S(2)}) async-start(), calls=%async_computation.5 | async-start | bytes 1179648 | tf_op jit(solution)/shard_map/reduce_scatter | solution.py:109
  162.0 28.8 %copy-start.18 = (f32[256,64]{0,1:T(8,128)S(1)}, f32[256,64]{0,1:T(8,128)}, u32[]{:S(2)}) copy-start(f32[256,64]{0,1:T(8,128)} %param.13) | copy-start | bytes 196612
  193.3 1.7 copy-start.12
  193.3 1.7 copy-start.14
  193.3 1.7 copy-start.16
  195.0 0.8 copy-start.20
  195.8 4.7 %copy-start.8 = (bf16[512,512]{1,0:T(8,128)(2,1)S(1)}, bf16[512,512]{1,0:T(8,128)(2,1)}, u32[]{:S(2)}) copy-start(bf16[512,512]{1,0:T(8,128)(2,1)} %get-tuple-element.19) | copy-start | bytes 1572868
  195.8 4.7 %copy-start.10 = (bf16[512,512]{1,0:T(8,128)(2,1)S(1)}, bf16[512,512]{1,0:T(8,128)(2,1)}, u32[]{:S(2)}) copy-start(bf16[512,512]{1,0:T(8,128)(2,1)} %get-tuple-element.22) | copy-start | bytes 1572868
  201.8 1.0 copy-start.2
  201.8 1.2 copy-start.4
  201.8 1.3 copy-start.6
  204.4 61.8 %copy-start.22 = (s32[1024]{0:T(1024)S(1)}, s32[1024]{0:T(1024)}, u32[]{:S(2)}) copy-start(s32[1024]{0:T(1024)} %copy-done.21) | copy-start | bytes 12292
Sparse Core Ops, SparseCore 0:
  39.2 66.1 reduce-scatter.2
  205.8 59.3 reduce-scatter.4
where the time goes:
time: 329 us; the launch traced here: 328 us
  waiting for transfers between devices  129 us (39%)
  blocking collectives  87.1 us (26%)
  local copies, waits for them, and re-layouts  48.1 us (15%)
  other arithmetic  30.7 us (9%)
  between operations  15.5 us (5%)
  matrix products  13.6 us (4%)
  starting transfers between devices  3.52 us (1%)
    reduce_scatter x2, waiting for transfers between devices, body(): lax.psum_scatter(frame_term, 'mod', scatter_dimension=0, tiled=True)  126 us
    psum x2, blocking collectives, body(): summed_commands = lax.psum(partial_commands, 'mod')  70.3 us
    gather x1, local copies, waits for them, and re-layouts, mirror_surface(): actuator_grid = commands[act_map].reshape(gx.shape[1], gy.shape[1])  28.7 us
    another operation x10, other arithmetic  27.5 us
    gather x2, local copies, waits for them, and re-layouts, body(): signal = frame_block.reshape(-1)[local_index].astype(jnp.bfloat16)  13.6 us
    all_gather x2, blocking collectives, body(): signals = lax.all_gather(signal[None, :], 'case', axis=0, tiled=True)  10.3 us
  transfers between devices with their start and end apart: 3, of which 3 were waited for; matrix products, arithmetic and copies ran while one was open for 0% of the time, Pallas kernels for 0%

commit v1 on v0

v1 whole, which is shorter than its diff:
```python
import math

import jax
import jax.numpy as jnp
import numpy as np
from jax import lax
from jax.experimental import pallas as pl
from jax.experimental.pallas import tpu as pltpu
from jax.sharding import PartitionSpec as P

STEPS = 2


loop_gain = 0.5
radius_pixels = 6.0
point_count = 256
LANES = 128
VMEM_LIMIT = 32 * 1024 * 1024


def rounded_table(angle, length, sign):
    scale = 1.0 / math.sqrt(length)
    real = (np.cos(angle) * scale).astype(np.float32).astype(jnp.bfloat16).astype(np.float64)
    imag = (sign * np.sin(angle) * scale).astype(np.float32).astype(jnp.bfloat16).astype(np.float64)
    return real + 1j * imag


def pyramid_table(pupil_size, length):
    centred = np.arange(length) - length // 2
    forward = np.mod(centred[:, None] * np.arange(pupil_size)[None, :], length) * (2.0 * math.pi / length)
    inverse = np.mod(np.arange(length)[:, None] * centred[None, :], length) * (2.0 * math.pi / length)
    mask = np.array([1, 1j, -1, -1j])[np.abs(centred) % 4]
    return rounded_table(inverse, length, 1.0) @ (mask[:, None] * rounded_table(forward, length, -1.0))


def sin_cos(angle):
    turns = jnp.floor(angle * (2.0 / math.pi) + 0.5)
    rest = angle - turns * 1.5703125
    rest = rest - turns * 4.837512969970703125e-4
    rest = rest - turns * 7.54978995489188216e-8
    square = rest * rest
    sine = rest + rest * square * (-1.6666654611e-1 + square * (8.3321608736e-3 - square * 1.9515295891e-4))
    cosine = (
        1.0
        - 0.5 * square
        + square * square * (4.166664568298827e-2 + square * (-1.388731625493765e-3 + square * 2.443315711809948e-5))
    )
    quarter = turns.astype(jnp.int32)
    swap = (quarter & 1) == 1
    sin_out = jnp.where(swap, cosine, sine)
    cos_out = jnp.where(swap, sine, cosine)
    sin_out = jnp.where((quarter & 2) == 2, -sin_out, sin_out)
    cos_out = jnp.where(((quarter + 1) & 2) == 2, -cos_out, cos_out)
    return sin_out, cos_out


def field_matrix(phase, amplitude):
    sine, cosine = sin_cos(phase)
    real, imag = amplitude * cosine, amplitude * sine
    top = jnp.concatenate([real, imag], 1)
    bottom = jnp.concatenate([-imag, real], 1)
    return jnp.concatenate([top, bottom], 0).astype(jnp.bfloat16)


def field_kernel(phase_ref, amp_ref, out_ref):
    out_ref[...] = field_matrix(phase_ref[...], amp_ref[...])


def look_up(rows, index):
    count, row = rows
    high = index >> 7
    low = index & (LANES - 1)
    sums = [jnp.zeros(index.shape, jnp.float32) for _ in range(4)]
    for i in range(count):
        spread = jnp.broadcast_to(row(i), index.shape)
        picked = jnp.take_along_axis(spread, low, axis=1, mode="promise_in_bounds")
        sums[i % 4] = jnp.where(high == i, picked, sums[i % 4])
    return (sums[0] + sums[1]) + (sums[2] + sums[3])


def optics(points, field, rows_table, full_table, frame_ref, sums_axis):
    row_count = rows_table.shape[0]
    pupil = rows_table.shape[1] // 2
    length = full_table.shape[1] // 2
    count = points.shape[0]
    angle = points.astype(jnp.float32) * (2.0 * math.pi / point_count)
    sin_a, cos_a = sin_cos(angle)
    spread = pupil // LANES
    sin_a = jnp.concatenate([sin_a] * spread, 1)
    cos_a = jnp.concatenate([cos_a] * spread, 1)
    place = (lax.broadcasted_iota(jnp.int32, (count, pupil), 1) - pupil // 2).astype(jnp.float32)
    place = place * (2.0 * math.pi * radius_pixels / length)
    s1, c1 = sin_cos(place * cos_a)
    s2, c2 = sin_cos(place * sin_a)
    real, imag = rows_table[:, :pupil][None], rows_table[:, pupil:][None]
    s1, c1 = s1[:, None, :], c1[:, None, :]
    left = jnp.concatenate([real * c1 - imag * s1, real * s1 + imag * c1], 2)
    left = left.reshape(count * row_count, 2 * pupil).astype(jnp.bfloat16)
    half = jnp.dot(left, field, preferred_element_type=jnp.float32)
    half = half.reshape(count, row_count, 2 * pupil)
    real, imag = half[:, :, :pupil], half[:, :, pupil:]
    s2, c2 = s2[:, None, :], c2[:, None, :]
    half = jnp.concatenate([real * c2 - imag * s2, real * s2 + imag * c2], 2)
    half = half.reshape(count * row_count, 2 * pupil).astype(jnp.bfloat16)
    detector = jnp.dot(half, full_table, preferred_element_type=jnp.float32)
    real, imag = detector[:, :length], detector[:, length:]
    intensity = (real * real + imag * imag).reshape(count, row_count, length)
    frame_ref[...] = jnp.sum(intensity, 0) * (1.0 / count)


def read_signals(frame_ref, pixels):
    row_count, length = frame_ref.shape
    per_row = length // LANES

    def row(i):
        column = (i % per_row) * LANES
        return frame_ref[i // per_row : i // per_row + 1, column : column + LANES]

    picked = look_up((row_count * per_row, row), pixels)
    return picked.astype(jnp.bfloat16).astype(jnp.float32)


def first_kernel(points_ref, field_ref, rows_ref, full_ref, pixels_ref, frame_ref, signal_ref):
    optics(points_ref[...], field_ref[...], rows_ref[...], full_ref[...], frame_ref, None)
    signal_ref[...] = read_signals(frame_ref, pixels_ref[...])


def summed_commands(parts_ref, cases):
    parts = parts_ref[...].astype(jnp.float32)
    return jnp.sum(parts.reshape(cases, parts.shape[0] // cases, parts.shape[1]), 1)


def later_kernel(
    parts_ref, total_ref, map_ref, gx_ref, gyt_ref, phase_ref, amp_ref, points_ref, rows_ref, full_ref, pixels_ref,
    frame_ref, signal_ref, new_total_ref,
):
    cases, block = total_ref.shape
    total = total_ref[...] + loop_gain * summed_commands(parts_ref, cases)
    new_total_ref[...] = total
    per_case = block // LANES

    def row(i):
        column = (i % per_case) * LANES
        return total[i // per_case : i // per_case + 1, column : column + LANES]

    grid = look_up((cases * per_case, row), map_ref[...])
    rows_mapped = jnp.dot(gx_ref[...], grid, precision=lax.Precision.HIGHEST, preferred_element_type=jnp.float32)
    surface = jnp.dot(
        rows_mapped, gyt_ref[...], precision=lax.Precision.HIGHEST, preferred_element_type=jnp.float32
    )
    field = field_matrix(phase_ref[...] - surface, amp_ref[...])
    optics(points_ref[...], field, rows_ref[...], full_ref[...], frame_ref, None)
    signal_ref[...] = read_signals(frame_ref, pixels_ref[...])


def command_kernel(own_case_ref, *refs):
    signal_refs, recon_ref, out_ref = refs[:-2], refs[-2], refs[-1]
    cases = len(signal_refs)
    own_case = own_case_ref[0]
    received = [ref[...] for ref in signal_refs]
    ordered = []
    for case in range(cases):
        values = received[0]
        for j in range(1, cases):
            values = jnp.where((own_case ^ j) == case, received[j], values)
        ordered.append(values)
    groups = received[0].shape[0]
    signals = jnp.concatenate(
        [jnp.concatenate([values[g : g + 1] for values in ordered], 0) for g in range(groups)], 1
    ).astype(jnp.bfloat16)
    partial = lax.dot_general(
        signals, recon_ref[...], (((1,), (1,)), ((), ())), preferred_element_type=jnp.float32
    )
    copies = out_ref.shape[0] // cases
    spread = jnp.concatenate([jnp.broadcast_to(partial[c : c + 1], (copies, partial.shape[1])) for c in range(cases)], 0)
    out_ref[...] = spread.astype(jnp.bfloat16)


def last_kernel(parts_ref, total_ref, out_ref):
    cases, block = total_ref.shape
    total = total_ref[...] + loop_gain * summed_commands(parts_ref, cases)
    for case in range(cases):
        out_ref[:, case * block : (case + 1) * block] = total[case : case + 1]


def body(turbulence, pupil_amp, mod_points, valid_pix, recon, gx, gy, act_map):
    pupil = pupil_amp.shape[0]
    length = 2 * pupil
    cases = lax.axis_size("case")
    devices_mod = lax.axis_size("mod")
    per_device = mod_points.shape[0]
    count = devices_mod * per_device
    row_count = length // devices_mod
    block = recon.shape[0]
    signal_rows = valid_pix.shape[0] // LANES
    own_mod = lax.axis_index("mod")
    own_case = lax.axis_index("case")
    screen = turbulence[0]
    params = pltpu.CompilerParams(vmem_limit_bytes=VMEM_LIMIT)

    table = pyramid_table(pupil, length)
    rows_all = jnp.asarray(np.concatenate([table.real, table.imag], 1).astype(np.float32))
    full = np.concatenate(
        [
            np.concatenate([table.real.T, table.imag.T], 1),
            np.concatenate([-table.imag.T, table.real.T], 1),
        ],
        0,
    )
    full_table = jnp.asarray(full.astype(np.float32)).astype(jnp.bfloat16)
    rows_table = lax.dynamic_slice_in_dim(rows_all, own_mod * row_count, row_count, 0)

    with jax.named_scope("modulation_points"):
        points = jnp.broadcast_to(mod_points[None, :, None], (devices_mod, per_device, LANES))
        points = lax.all_to_all(points, "mod", 0, 0, tiled=True).reshape(count, LANES)
    pixels = (valid_pix - own_mod * (row_count * length)).reshape(signal_rows, LANES)
    grid_rows, grid_columns = gx.shape[1], gy.shape[1]
    cell_map = jnp.pad(act_map.reshape(grid_rows, grid_columns), ((0, 0), (0, LANES - grid_columns)))
    gy_t = jnp.pad(gy.T, ((0, LANES - grid_columns), (0, 0)))

    frame_shape = jax.ShapeDtypeStruct((row_count, length), jnp.float32)
    signal_shape = jax.ShapeDtypeStruct((signal_rows, LANES), jnp.float32)
    total_shape = jax.ShapeDtypeStruct((cases, block), jnp.float32)

    def commands(signal):
        signals = [signal]
        for j in range(1, cases):
            signals.append(lax.ppermute(signal, "case", [(i, i ^ j) for i in range(cases)]))
        partial = pl.pallas_call(
            command_kernel,
            out_shape=jax.ShapeDtypeStruct((cases * devices_mod, block), jnp.bfloat16),
            in_specs=[pl.BlockSpec(memory_space=pltpu.SMEM)] + [pl.BlockSpec(memory_space=pltpu.VMEM)] * (cases + 1),
            compiler_params=params,
            name="commands",
        )(own_case.reshape(1), *signals, recon)
        return lax.all_to_all(partial, ("case", "mod"), 0, 0, tiled=True)

    field = pl.pallas_call(
        field_kernel,
        out_shape=jax.ShapeDtypeStruct((2 * pupil, 2 * pupil), jnp.bfloat16),
        compiler_params=params,
        name="field",
    )(screen, pupil_amp)
    frame, signal = pl.pallas_call(
        first_kernel,
        out_shape=(frame_shape, signal_shape),
        compiler_params=params,
        name="first_frame",
    )(points, field, rows_table, full_table, pixels)
    total = jnp.zeros((cases, block), jnp.float32)
    for iteration in range(1, STEPS):
        parts = commands(signal)
        frame, signal, total = pl.pallas_call(
            later_kernel,
            out_shape=(frame_shape, signal_shape, total_shape),
            compiler_params=params,
            name="next_frame",
        )(parts, total, cell_map, gx, gy_t, screen, pupil_amp, points, rows_table, full_table, pixels)
    parts = commands(signal)
    command_total = pl.pallas_call(
        last_kernel,
        out_shape=jax.ShapeDtypeStruct((1, cases * block), jnp.float32),
        compiler_params=params,
        name="total",
    )(parts, total)
    return (command_total, frame[None])


def solution(mesh):
    return jax.shard_map(
        body,
        mesh=mesh,
        in_specs=(P("case", None, None), P(), P("mod"), P("mod"), P("case", "mod"), P(), P(), P()),
        out_specs=(P("case", None), P("case", "mod", None)),
        check_vma=False,
    )
```

time: 329 us -> 62.2 us (0.19)
  waiting for transfers between devices: 129 us -> 11.2 us
  blocking collectives: 87.1 us -> 9.59 us
  local copies, waits for them, and re-layouts: 48.1 us -> 14.5 us
  other arithmetic: 30.7 us -> 1.97 us
  between operations: 15.5 us -> 1.56 us
  matrix products: 13.6 us -> 0 us
  starting transfers between devices: 3.52 us -> 14.3 us
  Pallas kernels: 0 us -> 8.31 us
    reduce_scatter x2 -> x0, waiting for transfers between devices: 126 us -> none  [body(): lax.psum_scatter(frame_term, 'mod', scatter_dimension=0, tiled=True)]
    psum x2 -> x0, blocking collectives: 70.3 us -> none  [body(): summed_commands = lax.psum(partial_commands, 'mod')]
    gather x3 -> x0, local copies, waits for them, and re-layouts: 42.3 us -> none  [the longest x1 28.7 us: mirror_surface(): actuator_grid = commands[act_map].reshape(gx.shape[1], gy.shape[1])]
    another operation x10 -> x0, other arithmetic: 27.5 us -> none
    dot_general x12 -> x0, matrix products: 13.6 us -> none  [the longest x2 2.97 us: detector_frame(): jnp.dot(table_one, pupil_field, preferred_element_type=jnp.float32)]
    all_gather x2 -> x0, blocking collectives: 10.3 us -> none  [body(): signals = lax.all_gather(signal[None, :], 'case', axis=0, tiled=True)]
    pallas_call x0 -> x6, Pallas kernels: none -> 8.31 us  [the longest x1 3.84 us: body(): pl.pallas_call(later_kernel, out_shape=(frame_shape, signal_shape, total_...]
    all_to_all x1 -> x2, starting transfers between devices: 3.26 us -> 10.5 us  [the longest x1 7.25 us: body(): lax.all_to_all(points, 'mod', 0, 0, tiled=True).reshape(count, LANES)]
  transfers between devices with their start and end apart: 3 -> 8, of which waited for: 3 -> 5; matrix products, arithmetic and copies ran while one was open for 0% -> 8% of each run, Pallas kernels for 0% -> 1%
where the time goes in v1:
time: 62.2 us; the launch traced here: 61.4 us
  local copies, waits for them, and re-layouts  14.5 us (23%)
  starting transfers between devices  14.3 us (23%)
  waiting for transfers between devices  11.2 us (18%)
  blocking collectives  9.59 us (15%)
  Pallas kernels  8.31 us (13%)
  other arithmetic  1.97 us (3%)
  between operations  1.56 us (3%)
    unnamed x27, local copies, waits for them, and re-layouts  10.1 us
    all_to_all x1, blocking collectives, commands(): return lax.all_to_all(partial, ('case', 'mod'), 0, 0, tiled=True)  9.59 us
    all_to_all x1, starting transfers between devices, body(): lax.all_to_all(points, 'mod', 0, 0, tiled=True).reshape(count, LANES)  7.25 us
    ppermute x6, waiting for transfers between devices, commands(): lax.ppermute(signal, 'case', [(i, i ^ j) for i in range(cases)])  4.57 us
    all_to_all x1, waiting for transfers between devices, commands(): return lax.all_to_all(partial, ('case', 'mod'), 0, 0, tiled=True)  4.18 us
    pallas_call x1, Pallas kernels, body(): pl.pallas_call(later_kernel, out_shape=(frame_shape, signal_shape, total_...  3.84 us
    ppermute x6, starting transfers between devices, commands(): lax.ppermute(signal, 'case', [(i, i ^ j) for i in range(cases)])  3.75 us
    all_to_all x1, starting transfers between devices, commands(): return lax.all_to_all(partial, ('case', 'mod'), 0, 0, tiled=True)  3.28 us
  transfers between devices with their start and end apart: 8, of which 5 were waited for; matrix products, arithmetic and copies ran while one was open for 8% of the time, Pallas kernels for 1%

profile of v1, /device:TPU:0, one launch (start us, length us, event | category | flops | bytes accessed | tf_op | source)
XLA Modules:
  0.0 61.4 jit_solution(13586546801433370836)
XLA Ops:
  2.0 7.3 %all-to-all-start = ((s32[8,1,128]{2,1,0:T(1,128)}), s32[8,1,128]{2,1,0:T(1,128)S(1)}, u32[]{:S(2)}, u32[]{:S(2)}) async-start(s32[8,1,128]{2,1,0:T(1,128)} %broadcast_in_dim.15), calls=%async_computation | async-start | bytes 8192 | tf_op jit(solution)/shard_map/modulation_points/all_to_all | solution.py:215
  9.3 0.7 %subtract_bitcast_fusion.pixels_ref = s32[8,128]{1,0:T(8,128)S(1)} fusion(s32[1024]{0:T(1024)} %param.13, s32[]{:T(128)S(6)} %mul.7), kind=kLoop, calls=%fused_computation.2 | loop fusion | flops 1024 | bytes 8196 | tf_op jit(solution)/shard_map/reshape | solution.py:216
  10.0 0.9 %constant_dynamic-slice_fusion.rows_ref = f32[64,512]{1,0:T(8,128)S(1)} fusion(f32[512,512]{1,0:T(8,128)} %constant.23.clone, s32[]{:T(128)S(6)} %select_n.3), kind=kLoop, calls=%fused_computation.3 | loop fusion | bytes 262148 | tf_op jit(solution)/shard_map/dynamic_slice | solution.py:211
  10.9 0.9 %copy-done.3 = f32[1,256,256]{2,1,0:T(8,128)S(1)} copy-done((f32[1,256,256]{2,1,0:T(8,128)S(1)}, f32[1,256,256]{2,1,0:T(8,128)}, u32[]{:S(2)}) %copy-start.3) | copy-done | bytes 262168
  11.8 0.9 %copy-done.5 = f32[256,256]{1,0:T(8,128)S(1)} copy-done((f32[256,256]{1,0:T(8,128)S(1)}, f32[256,256]{1,0:T(8,128)}, u32[]{:S(2)}) %copy-start.5) | copy-done | bytes 262168
  13.2 2.5 %all-to-all-done = s32[8,1,128]{2,1,0:T(1,128)S(1)} async-done(((s32[8,1,128]{2,1,0:T(1,128)}), s32[8,1,128]{2,1,0:T(1,128)S(1)}, u32[]{:S(2)}, u32[]{:S(2)}) %all-to-all-start) | async-done | bytes 4128 | tf_op jit(solution)/shard_map/modulation_points/all_to_all | solution.py:215
  15.7 1.2 %copy-done.1 = bf16[512,1024]{1,0:T(8,128)(2,1)S(1)} copy-done((bf16[512,1024]{1,0:T(8,128)(2,1)S(1)}, bf16[512,1024]{1,0:T(8,128)(2,1)}, u32[]{:S(2)}) %copy-start.1) | copy-done | bytes 1048600
  16.9 1.9 %first_frame.1 = (f32[64,512]{1,0:T(8,128)}, f32[8,128]{1,0:T(8,128)S(1)}) custom-call(s32[8,128]{1,0:T(8,128)S(1)} %bitcast.23, bf16[512,512]{1,0:T(8,128)(2,1)S(1)} %field.1.field_ref, f32[64,512]{1,0:T(8,128)S(1)} %constant_dynamic-slice_fusion.rows_ref, bf16[512,1024]{1,0:T(8,128)(2,1)S(1)} %copy-done.1, s32[8,128]{1,0:T(8,128)S(1)} %subtract_bitcast_fusion.pixels_ref), custom_call_target="tpu_custom_call" | custom-call | tf_op jit(solution)/shard_map/first_frame/pallas_call | solution.py:244
  18.8 1.5 %collective-permute-start.1 = (f32[8,128]{1,0:T(8,128)S(1)}, f32[8,128]{1,0:T(8,128)S(1)}, u32[]{:S(2)}, u32[]{:S(2)}) collective-permute-start(f32[8,128]{1,0:T(8,128)S(1)} %get-tuple-element.6.refs_0_), channel_id=1, source_target_pairs={{0,16},{8,24},{16,0},{24,8},{1,17},{9,25},{17,1},{25,9},{2,18},{10... | collective-permute-start | bytes 12296 | tf_op jit(solution)/shard_map/ppermute | solution.py:228
  20.7 1.7 %collective-permute-done.1.refs_2_ = f32[8,128]{1,0:T(8,128)S(1)} collective-permute-done((f32[8,128]{1,0:T(8,128)S(1)}, f32[8,128]{1,0:T(8,128)S(1)}, u32[]{:S(2)}, u32[]{:S(2)}) %collective-permute-start.1) | collective-permute-done | bytes 4128 | tf_op jit(solution)/shard_map/ppermute | solution.py:228
  22.4 0.9 %collective-permute-done.2.refs_3_ = f32[8,128]{1,0:T(8,128)S(1)} collective-permute-done((f32[8,128]{1,0:T(8,128)S(1)}, f32[8,128]{1,0:T(8,128)S(1)}, u32[]{:S(2)}, u32[]{:S(2)}) %collective-permute-start.2) | collective-permute-done | bytes 4128 | tf_op jit(solution)/shard_map/ppermute | solution.py:228
  23.4 0.8 %commands.2 = bf16[32,1280]{1,0:T(8,128)(2,1)S(1)} custom-call(s32[1]{0:T(128)} %bitcast.own_case_ref, f32[8,128]{1,0:T(8,128)S(1)} %get-tuple-element.6.refs_0_, f32[8,128]{1,0:T(8,128)S(1)} %collective-permute-done.refs_1_, f32[8,128]{1,0:T(8,128)S(1)} %collective-permute-done.1.refs_2_, f32[8,128]{1,0:T(8,128)S(1)} %collective-permute-done.2.refs_3_, ...), custom_call_target="tpu_custom_call" | custom-call | tf_op jit(solution)/shard_map/commands/pallas_call | solution.py:229
  24.7 0.6 %reduce = bf16[32,1280]{1,0:T(8,128)(2,1)S(1)} reduce(bf16[32,1,1280]{2,0,1:T(8,128)(2,1)S(1)} %bitcast.19, bf16[]{:T(256)} %broadcast.5), dimensions={1}, to_apply=%copy.16.reduce_sub_computation | reduce | bytes 163842 | tf_op jit(solution)/shard_map/all_to_all | solution.py:236
  25.3 0.7 %reshape.28 = bf16[32,2,640]{2,1,0:T(2,128)(2,1)} reshape(bf16[32,1280]{1,0:T(8,128)(2,1)S(1)} %reduce) | data formatting | bytes 163840
  26.0 3.3 %all-to-all-start.1 = ((bf16[32,2,640]{2,1,0:T(2,128)(2,1)}), bf16[32,2,640]{2,1,0:T(2,128)(2,1)}, u32[]{:S(2)}, u32[]{:S(2)}) async-start(bf16[32,2,640]{2,1,0:T(2,128)(2,1)} %reshape.28), calls=%async_computation.1 | async-start | bytes 163840 | tf_op jit(solution)/shard_map/all_to_all | solution.py:236
  29.3 0.9 %copy.17.gx_ref = f32[256,64]{1,0:T(8,128)S(1)} copy(f32[256,64]{0,1:T(8,128)} %param.15) | data formatting | bytes 131072 | tf_op args[5]
  30.2 0.8 %reshape.27 = s32[64,80]{1,0:T(8,128)S(1)} reshape(s32[5120]{0:T(1024)} %param.17) | data formatting | bytes 40960 | tf_op jit(solution)/shard_map/reshape | solution.py:218
  31.6 0.9 %pad.9.gyt_ref = f32[128,256]{1,0:T(8,128)S(1)} pad(f32[80,256]{1,0:T(8,128)} %bitcast.25, f32[]{:T(128)} %constant.22.clone.1), padding=0_48x0_0 | pad | bytes 212996 | tf_op jit(solution)/shard_map/jit(_pad)/pad | solution.py:219
  32.5 4.2 %all-to-all-done.1 = bf16[32,2,640]{2,1,0:T(2,128)(2,1)} async-done(((bf16[32,2,640]{2,1,0:T(2,128)(2,1)}), bf16[32,2,640]{2,1,0:T(2,128)(2,1)}, u32[]{:S(2)}, u32[]{:S(2)}) %all-to-all-start.1) | async-done | bytes 81952 | tf_op jit(solution)/shard_map/all_to_all | solution.py:236
  36.7 1.6 %reshape.29 = bf16[32,1,1280]{2,1,0:T(2,128)(2,1)} reshape(bf16[32,2,640]{2,1,0:T(2,128)(2,1)} %all-to-all-done.1) | data formatting | bytes 163840
  38.3 0.9 %copy.24 = bf16[32,1,1280]{2,0,1:T(8,128)(2,1)S(1)} copy(bf16[32,1,1280]{2,1,0:T(2,128)(2,1)} %reshape.29) | data formatting | bytes 163840
  39.3 1.2 %copy-done.2 = bf16[512,1024]{1,0:T(8,128)(2,1)S(1)} copy-done((bf16[512,1024]{1,0:T(8,128)(2,1)S(1)}, bf16[512,1024]{1,0:T(8,128)(2,1)}, u32[]{:S(2)}) %copy-start.2) | copy-done | bytes 1048600
  40.5 0.8 %copy-done.7 = s32[64,128]{1,0:T(8,128)S(1)} copy-done((s32[64,128]{1,0:T(8,128)S(1)}, s32[64,128]{1,0:T(8,128)}, u32[]{:S(2)}) %copy-start.7) | copy-done | bytes 32792
  41.3 3.8 %next_frame.1 = (f32[64,512]{1,0:T(8,128)}, f32[8,128]{1,0:T(8,128)S(1)}, f32[4,1280]{1,0:T(4,128)S(1)}) custom-call(bf16[32,1280]{1,0:T(8,128)(2,1)S(1)} %bitcast.21, f32[4,1280]{1,0:T(4,128)S(1)} %broadcast_in_dim.16.total_ref, s32[64,128]{1,0:T(8,128)S(1)} %copy-done.7, f32[256,64]{1,0:T(8,128)S(1)} %copy.17.gx_ref, f32[128,256]{1,0:T(8,128)S(1)} %pad.9.gyt_ref, ...), custom_call_target="tpu_custom_call" | custom-call | tf_op jit(solution)/shard_map/next_frame/pallas_call | solution.py:253
  45.2 0.6 %collective-permute-start.4 = (f32[8,128]{1,0:T(8,128)S(1)}, f32[8,128]{1,0:T(8,128)S(1)}, u32[]{:S(2)}, u32[]{:S(2)}) collective-permute-start(f32[8,128]{1,0:T(8,128)S(1)} %get-tuple-element.7.refs_0_), channel_id=1, source_target_pairs={{0,16},{8,24},{16,0},{24,8},{1,17},{9,25},{17,1},{25,9},{2,18},{10... | collective-permute-start | bytes 12296 | tf_op jit(solution)/shard_map/ppermute | solution.py:228
  45.9 1.2 %collective-permute-start.5 = (f32[8,128]{1,0:T(8,128)S(1)}, f32[8,128]{1,0:T(8,128)S(1)}, u32[]{:S(2)}, u32[]{:S(2)}) collective-permute-start(f32[8,128]{1,0:T(8,128)S(1)} %get-tuple-element.7.refs_0_), channel_id=1, source_target_pairs={{0,24},{8,16},{16,8},{24,0},{1,25},{9,17},{17,9},{25,1},{2,26},{10... | collective-permute-start | bytes 12296 | tf_op jit(solution)/shard_map/ppermute | solution.py:228
  47.0 1.8 %collective-permute-done.4.refs_2_ = f32[8,128]{1,0:T(8,128)S(1)} collective-permute-done((f32[8,128]{1,0:T(8,128)S(1)}, f32[8,128]{1,0:T(8,128)S(1)}, u32[]{:S(2)}, u32[]{:S(2)}) %collective-permute-start.4) | collective-permute-done | bytes 4128 | tf_op jit(solution)/shard_map/ppermute | solution.py:228
  48.9 0.8 %commands.3 = bf16[32,1280]{1,0:T(8,128)(2,1)S(1)} custom-call(s32[1]{0:T(128)} %bitcast.own_case_ref, f32[8,128]{1,0:T(8,128)S(1)} %get-tuple-element.7.refs_0_, f32[8,128]{1,0:T(8,128)S(1)} %collective-permute-done.3.refs_1_, f32[8,128]{1,0:T(8,128)S(1)} %collective-permute-done.4.refs_2_, f32[8,128]{1,0:T(8,128)S(1)} %collective-permute-done.5.refs_3_, ...), custom_call_target="tpu_custom_call" | custom-call | tf_op jit(solution)/shard_map/commands/pallas_call | solution.py:229
  49.7 0.7 %reduce.1 = bf16[32,1280]{1,0:T(8,128)(2,1)S(1)} reduce(bf16[32,1,1280]{2,0,1:T(8,128)(2,1)S(1)} %bitcast.20, bf16[]{:T(256)} %broadcast.5), dimensions={1}, to_apply=%copy.18.reduce_sub_computation | reduce | bytes 163842 | tf_op jit(solution)/shard_map/all_to_all | solution.py:236
  50.4 9.6 %all_to_all.27 = bf16[32,2,640]{2,1,0:T(2,128)(2,1)S(1)} all-to-all(bf16[32,2,640]{2,1,0:T(2,128)(2,1)S(1)} %reshape.30), channel_id=1, replica_groups=mesh['case'=4,'mod'=8] {'case','mod'}, dimensions={0} | all-to-all | bytes 163840 | tf_op jit(solution)/shard_map/all_to_all | solution.py:236
  60.0 0.7 %copy-done.9 = f32[4,1280]{1,0:T(4,128)S(1)} copy-done((f32[4,1280]{1,0:T(4,128)S(1)}, f32[4,1280]{1,0:T(4,128)}, u32[]{:S(2)}) %copy-start.9) | copy-done | bytes 20504
  60.8 0.7 %total.1 = f32[1,5120]{1,0:T(1,128)} custom-call(bf16[32,1280]{1,0:T(8,128)(2,1)S(1)} %bitcast.22, f32[4,1280]{1,0:T(4,128)S(1)} %copy-done.9), custom_call_target="tpu_custom_call" | custom-call | tf_op jit(solution)/shard_map/total/pallas_call | solution.py:260
  (28 shorter events, 2.8 us)
Async XLA Ops:
  0.6 22.7 %copy-start = (bf16[1280,1024]{1,0:T(8,128)(2,1)S(1)}, bf16[1280,1024]{1,0:T(8,128)(2,1)}, u32[]{:S(2)}) copy-start(bf16[1280,1024]{1,0:T(8,128)(2,1)} %refs_4_.3) | copy-start | bytes 7864324
  2.0 13.6 %all-to-all-start = ((s32[8,1,128]{2,1,0:T(1,128)}), s32[8,1,128]{2,1,0:T(1,128)S(1)}, u32[]{:S(2)}, u32[]{:S(2)}) async-start(s32[8,1,128]{2,1,0:T(1,128)} %broadcast_in_dim.15), calls=%async_computation | async-start | bytes 8192 | tf_op jit(solution)/shard_map/modulation_points/all_to_all | solution.py:215
  10.9 1.0 %copy-start.3 = (f32[1,256,256]{2,1,0:T(8,128)S(1)}, f32[1,256,256]{2,1,0:T(8,128)}, u32[]{:S(2)}) copy-start(f32[1,256,256]{2,1,0:T(8,128)} %param.10) | copy-start | bytes 786436
  11.8 0.9 %copy-start.5 = (f32[256,256]{1,0:T(8,128)S(1)}, f32[256,256]{1,0:T(8,128)}, u32[]{:S(2)}) copy-start(f32[256,256]{1,0:T(8,128)} %amp_ref.3) | copy-start | bytes 786436
  15.7 1.2 %copy-start.1 = (bf16[512,1024]{1,0:T(8,128)(2,1)S(1)}, bf16[512,1024]{1,0:T(8,128)(2,1)}, u32[]{:S(2)}) copy-start(bf16[512,1024]{1,0:T(8,128)(2,1)} %constant.31.full_ref) | copy-start | bytes 3145732
  16.9 22.4 %copy-start.4 = (f32[1,256,256]{2,1,0:T(8,128)S(1)}, f32[1,256,256]{2,1,0:T(8,128)}, u32[]{:S(2)}) copy-start(f32[1,256,256]{2,1,0:T(8,128)} %param.10) | copy-start | bytes 786436
  18.8 20.5 %copy-start.6 = (f32[256,256]{1,0:T(8,128)S(1)}, f32[256,256]{1,0:T(8,128)}, u32[]{:S(2)}) copy-start(f32[256,256]{1,0:T(8,128)} %amp_ref.3) | copy-start | bytes 786436
  18.8 1.9 %collective-permute-start = (f32[8,128]{1,0:T(8,128)S(1)}, f32[8,128]{1,0:T(8,128)S(1)}, u32[]{:S(2)}, u32[]{:S(2)}) collective-permute-start(f32[8,128]{1,0:T(8,128)S(1)} %get-tuple-element.6.refs_0_), channel_id=1, source_target_pairs={{0,8},{8,0},{16,24},{24,16},{1,9},{9,1},{17,25},{25,17},{2,10},{10... | collective-permute-start | bytes 12296 | tf_op jit(solution)/shard_map/ppermute | solution.py:228
  18.8 3.6 %collective-permute-start.1 = (f32[8,128]{1,0:T(8,128)S(1)}, f32[8,128]{1,0:T(8,128)S(1)}, u32[]{:S(2)}, u32[]{:S(2)}) collective-permute-start(f32[8,128]{1,0:T(8,128)S(1)} %get-tuple-element.6.refs_0_), channel_id=1, source_target_pairs={{0,16},{8,24},{16,0},{24,8},{1,17},{9,25},{17,1},{25,9},{2,18},{10... | collective-permute-start | bytes 12296 | tf_op jit(solution)/shard_map/ppermute | solution.py:228
  20.3 3.0 %collective-permute-start.2 = (f32[8,128]{1,0:T(8,128)S(1)}, f32[8,128]{1,0:T(8,128)S(1)}, u32[]{:S(2)}, u32[]{:S(2)}) collective-permute-start(f32[8,128]{1,0:T(8,128)S(1)} %get-tuple-element.6.refs_0_), channel_id=1, source_target_pairs={{0,24},{8,16},{16,8},{24,0},{1,25},{9,17},{17,9},{25,1},{2,26},{10... | collective-permute-start | bytes 12296 | tf_op jit(solution)/shard_map/ppermute | solution.py:228
  26.0 10.7 %all-to-all-start.1 = ((bf16[32,2,640]{2,1,0:T(2,128)(2,1)}), bf16[32,2,640]{2,1,0:T(2,128)(2,1)}, u32[]{:S(2)}, u32[]{:S(2)}) async-start(bf16[32,2,640]{2,1,0:T(2,128)(2,1)} %reshape.28), calls=%async_computation.1 | async-start | bytes 163840 | tf_op jit(solution)/shard_map/all_to_all | solution.py:236
  39.3 1.2 %copy-start.2 = (bf16[512,1024]{1,0:T(8,128)(2,1)S(1)}, bf16[512,1024]{1,0:T(8,128)(2,1)}, u32[]{:S(2)}) copy-start(bf16[512,1024]{1,0:T(8,128)(2,1)} %constant.31.full_ref) | copy-start | bytes 3145732
  40.5 0.8 %copy-start.7 = (s32[64,128]{1,0:T(8,128)S(1)}, s32[64,128]{1,0:T(8,128)}, u32[]{:S(2)}) copy-start(s32[64,128]{1,0:T(8,128)} %pad.8.map_ref) | copy-start | bytes 98308
  45.1 4.5 %copy-start.8 = (f32[4,1280]{1,0:T(4,128)}, f32[4,1280]{1,0:T(4,128)S(1)}, u32[]{:S(2)}) copy-start(f32[4,1280]{1,0:T(4,128)S(1)} %get-tuple-element.8.total_ref) | copy-start | bytes 61444
  45.1 1.9 %collective-permute-start.3 = (f32[8,128]{1,0:T(8,128)S(1)}, f32[8,128]{1,0:T(8,128)S(1)}, u32[]{:S(2)}, u32[]{:S(2)}) collective-permute-start(f32[8,128]{1,0:T(8,128)S(1)} %get-tuple-element.7.refs_0_), channel_id=1, source_target_pairs={{0,8},{8,0},{16,24},{24,16},{1,9},{9,1},{17,25},{25,17},{2,10},{10... | collective-permute-start | bytes 12296 | tf_op jit(solution)/shard_map/ppermute | solution.py:228
  45.2 3.6 %collective-permute-start.4 = (f32[8,128]{1,0:T(8,128)S(1)}, f32[8,128]{1,0:T(8,128)S(1)}, u32[]{:S(2)}, u32[]{:S(2)}) collective-permute-start(f32[8,128]{1,0:T(8,128)S(1)} %get-tuple-element.7.refs_0_), channel_id=1, source_target_pairs={{0,16},{8,24},{16,0},{24,8},{1,17},{9,25},{17,1},{25,9},{2,18},{10... | collective-permute-start | bytes 12296 | tf_op jit(solution)/shard_map/ppermute | solution.py:228
  45.9 3.0 %collective-permute-start.5 = (f32[8,128]{1,0:T(8,128)S(1)}, f32[8,128]{1,0:T(8,128)S(1)}, u32[]{:S(2)}, u32[]{:S(2)}) collective-permute-start(f32[8,128]{1,0:T(8,128)S(1)} %get-tuple-element.7.refs_0_), channel_id=1, source_target_pairs={{0,24},{8,16},{16,8},{24,0},{1,25},{9,17},{17,9},{25,1},{2,26},{10... | collective-permute-start | bytes 12296 | tf_op jit(solution)/shard_map/ppermute | solution.py:228
  60.0 0.7 %copy-start.9 = (f32[4,1280]{1,0:T(4,128)S(1)}, f32[4,1280]{1,0:T(4,128)}, u32[]{:S(2)}) copy-start(f32[4,1280]{1,0:T(4,128)} %copy-done.8) | copy-start | bytes 61444

commit v2 on v1

v2 whole, which is shorter than its diff:
```python
import math

import jax
import jax.numpy as jnp
import numpy as np
from jax import lax
from jax.experimental import pallas as pl
from jax.experimental.pallas import tpu as pltpu
from jax.sharding import PartitionSpec as P

STEPS = 2


loop_gain = 0.5
radius_pixels = 6.0
point_count = 256
LANES = 128
VMEM_LIMIT = 16 * 1024 * 1024


def rounded_table(angle, length, sign):
    scale = 1.0 / math.sqrt(length)
    real = (np.cos(angle) * scale).astype(np.float32).astype(jnp.bfloat16).astype(np.float64)
    imag = (sign * np.sin(angle) * scale).astype(np.float32).astype(jnp.bfloat16).astype(np.float64)
    return real + 1j * imag


def pyramid_table(pupil_size, length):
    centred = np.arange(length) - length // 2
    forward = np.mod(centred[:, None] * np.arange(pupil_size)[None, :], length) * (2.0 * math.pi / length)
    inverse = np.mod(np.arange(length)[:, None] * centred[None, :], length) * (2.0 * math.pi / length)
    mask = np.array([1, 1j, -1, -1j])[np.abs(centred) % 4]
    return rounded_table(inverse, length, 1.0) @ (mask[:, None] * rounded_table(forward, length, -1.0))


def sin_cos(angle):
    turns = jnp.floor(angle * (2.0 / math.pi) + 0.5)
    rest = angle - turns * 1.5703125
    rest = rest - turns * 4.837512969970703125e-4
    rest = rest - turns * 7.54978995489188216e-8
    square = rest * rest
    sine = rest + rest * square * (-1.6666654611e-1 + square * (8.3321608736e-3 - square * 1.9515295891e-4))
    cosine = (
        1.0
        - 0.5 * square
        + square * square * (4.166664568298827e-2 + square * (-1.388731625493765e-3 + square * 2.443315711809948e-5))
    )
    quarter = turns.astype(jnp.int32)
    swap = (quarter & 1) == 1
    sin_out = jnp.where(swap, cosine, sine)
    cos_out = jnp.where(swap, sine, cosine)
    sin_out = jnp.where((quarter & 2) == 2, -sin_out, sin_out)
    cos_out = jnp.where(((quarter + 1) & 2) == 2, -cos_out, cos_out)
    return sin_out, cos_out


def field_matrix(phase, amplitude):
    sine, cosine = sin_cos(phase)
    real, imag = amplitude * cosine, amplitude * sine
    top = jnp.concatenate([real, imag], 1)
    bottom = jnp.concatenate([-imag, real], 1)
    return jnp.concatenate([top, bottom], 0).astype(jnp.bfloat16)


def halves(values):
    high = values.astype(jnp.bfloat16)
    low = (values - high.astype(jnp.float32)).astype(jnp.bfloat16)
    return high, low


def look_up(count, row, index):
    high = index >> 7
    low = index & (LANES - 1)
    sums = [jnp.zeros(index.shape, jnp.float32) for _ in range(4)]
    for i in range(count):
        spread = jnp.broadcast_to(row(i), index.shape)
        picked = jnp.take_along_axis(spread, low, axis=1, mode="promise_in_bounds")
        sums[i % 4] = jnp.where(high == i, picked, sums[i % 4])
    return (sums[0] + sums[1]) + (sums[2] + sums[3])


def runs(ref):
    per_row = ref.shape[1] // LANES

    def row(i):
        column = (i % per_row) * LANES
        return ref[i // per_row : i // per_row + 1, column : column + LANES]

    return ref.shape[0] * per_row, row


def prepare_kernel(
    phase_ref, amp_ref, table_ref, map_ref, gxt_ref, gyt_ref,
    field_ref, full_ref, cells_ref, gx_out_ref, gy_out_ref, floats,
):
    field_ref[...] = field_matrix(phase_ref[...], amp_ref[...])
    full_ref[...] = table_ref[...]
    floats[...] = map_ref[...].astype(jnp.float32)
    grid_rows, grid_columns = gxt_ref.shape[0], gyt_ref.shape[0]
    cell = lax.broadcasted_iota(jnp.int32, cells_ref.shape, 0) * grid_columns
    column = lax.broadcasted_iota(jnp.int32, cells_ref.shape, 1)
    cell = jnp.where(column < grid_columns, cell + column, 0)
    cells_ref[...] = look_up(*runs(floats), cell).astype(jnp.int32)
    high, low = halves(gxt_ref[...].T)
    gx_out_ref[...] = jnp.concatenate([high, low, high], 1)
    gyt = jnp.concatenate(
        [gyt_ref[...], jnp.zeros((LANES - grid_columns, gyt_ref.shape[1]), jnp.float32)], 0
    )
    high, low = halves(gyt)
    gy_out_ref[...] = jnp.concatenate([high, high, low], 0)


def tilt_factors(angles_ref, pupil, length):
    sin_a, cos_a = sin_cos(angles_ref[...])
    spread = pupil // LANES
    sin_a = jnp.concatenate([sin_a] * spread, 1)
    cos_a = jnp.concatenate([cos_a] * spread, 1)
    place = (lax.broadcasted_iota(jnp.int32, sin_a.shape, 1) - pupil // 2).astype(jnp.float32)
    place = place * (2.0 * math.pi * radius_pixels / length)
    return sin_cos(place * cos_a), sin_cos(place * sin_a)


def turned(real, imag, sine, cosine):
    sine, cosine = sine[:, None, :], cosine[:, None, :]
    return jnp.concatenate([real * cosine - imag * sine, real * sine + imag * cosine], 2)


def optics(left, field, full_table, sine, cosine):
    count, pupil = sine.shape
    row_count = left.shape[0] // count
    length = full_table.shape[1] // 2
    half = jnp.dot(left, field, preferred_element_type=jnp.float32)
    half = half.reshape(count, row_count, 2 * pupil)
    half = turned(half[:, :, :pupil], half[:, :, pupil:], sine, cosine)
    half = half.reshape(count * row_count, 2 * pupil).astype(jnp.bfloat16)
    detector = jnp.dot(half, full_table, preferred_element_type=jnp.float32)
    real, imag = detector[:, :length], detector[:, length:]
    intensity = (real * real + imag * imag).reshape(count, row_count, length)
    return jnp.sum(intensity, 0) * (1.0 / count)


def read_signals(frame_ref, pixels):
    return look_up(*runs(frame_ref), pixels).astype(jnp.bfloat16).astype(jnp.float32)


def first_kernel(
    angles_ref, field_ref, rows_ref, full_ref, pixels_ref,
    signal_ref, left_ref, sine_ref, cosine_ref, frame_ref,
):
    pupil = rows_ref.shape[1] // 2
    (s1, c1), (s2, c2) = tilt_factors(angles_ref, pupil, full_ref.shape[1] // 2)
    rows = rows_ref[...]
    left = turned(rows[None, :, :pupil], rows[None, :, pupil:], s1, c1)
    left = left.reshape(left_ref.shape).astype(jnp.bfloat16)
    left_ref[...] = left
    sine_ref[...] = s2
    cosine_ref[...] = c2
    frame_ref[...] = optics(left, field_ref[...], full_ref[...], s2, c2)
    signal_ref[...] = read_signals(frame_ref, pixels_ref[...])


def add_commands(parts_ref, total_ref, out_ref):
    cases = out_ref.shape[0]
    each = parts_ref.shape[0] // cases
    for case in range(cases):
        sums = jnp.sum(parts_ref[case * each : (case + 1) * each].astype(jnp.float32), 0)
        out_ref[case] = loop_gain * sums if total_ref is None else total_ref[case] + loop_gain * sums


def later_kernel(
    parts_ref, cells_ref, gx_ref, gy_ref, phase_ref, amp_ref, left_ref, sine_ref, cosine_ref, full_ref, pixels_ref,
    *refs,
):
    frame_out_ref, signal_ref, new_total_ref, frame_ref, frame_done = refs[-5:]
    add_commands(parts_ref, refs[0] if len(refs) > 5 else None, new_total_ref)
    cases, pieces, width = new_total_ref.shape
    per_piece = width // LANES

    def row(i):
        column = (i % per_piece) * LANES
        piece = i // per_piece
        return new_total_ref[piece // pieces, piece % pieces : piece % pieces + 1, column : column + LANES]

    grid = look_up(cases * pieces * per_piece, row, cells_ref[...])
    high, low = halves(grid)
    rows_mapped = jnp.dot(
        gx_ref[...], jnp.concatenate([high, high, low], 0), preferred_element_type=jnp.float32
    )
    high, low = halves(rows_mapped)
    surface = jnp.dot(
        jnp.concatenate([high, low, high], 1), gy_ref[...], preferred_element_type=jnp.float32
    )
    field = field_matrix(phase_ref[...] - surface, amp_ref[...])
    frame_ref[...] = optics(left_ref[...], field, full_ref[...], sine_ref[...], cosine_ref[...])
    copy = pltpu.make_async_copy(frame_ref, frame_out_ref, frame_done)
    copy.start()
    signal_ref[...] = read_signals(frame_ref, pixels_ref[...])
    copy.wait()


def command_kernel(own_case_ref, *refs):
    signal_refs, recon_ref, out_ref = refs[:-2], refs[-2], refs[-1]
    cases = len(signal_refs)
    own_case = own_case_ref[0]
    received = [ref[...] for ref in signal_refs]
    ordered = []
    for case in range(cases):
        values = received[0]
        for j in range(1, cases):
            values = jnp.where((own_case ^ j) == case, received[j], values)
        ordered.append(values)
    groups = received[0].shape[0]
    signals = jnp.concatenate(
        [jnp.concatenate([values[g : g + 1] for values in ordered], 0) for g in range(groups)], 1
    ).astype(jnp.bfloat16)
    partial = lax.dot_general(
        signals, recon_ref[...], (((1,), (1,)), ((), ())), preferred_element_type=jnp.float32
    )
    messages, pieces, width = out_ref.shape
    copies = messages // cases
    for case in range(cases):
        message = jnp.concatenate(
            [partial[case : case + 1, i * width : (i + 1) * width] for i in range(pieces)], 0
        ).astype(jnp.bfloat16)
        for i in range(copies):
            out_ref[case * copies + i] = message


def last_kernel(parts_ref, total_ref, out_ref, sums_ref):
    add_commands(parts_ref, total_ref, sums_ref)
    cases, pieces, width = sums_ref.shape
    for case in range(cases):
        for i in range(pieces):
            start = (case * pieces + i) * width
            out_ref[:, start : start + width] = sums_ref[case, i : i + 1, :]


def body(turbulence, pupil_amp, mod_points, valid_pix, recon, gx, gy, act_map):
    pupil = pupil_amp.shape[0]
    length = 2 * pupil
    cases = lax.axis_size("case")
    devices_mod = lax.axis_size("mod")
    per_device = mod_points.shape[0]
    count = devices_mod * per_device
    row_count = length // devices_mod
    block = recon.shape[0]
    pieces = 2
    signal_rows = valid_pix.shape[0] // LANES
    own_mod = lax.axis_index("mod")
    own_case = lax.axis_index("case")
    screen = turbulence[0]

    def call(kernel, name, out_shape, scratch=(), **specs):
        return pl.pallas_call(
            kernel,
            out_shape=out_shape,
            scratch_shapes=scratch,
            compiler_params=pltpu.CompilerParams(vmem_limit_bytes=VMEM_LIMIT),
            name=name,
            **specs,
        )

    table = pyramid_table(pupil, length)
    rows_all = jnp.asarray(np.concatenate([table.real, table.imag], 1).astype(np.float32))
    full_table = jnp.asarray(
        np.concatenate(
            [
                np.concatenate([table.real.T, table.imag.T], 1),
                np.concatenate([-table.imag.T, table.real.T], 1),
            ],
            0,
        ).astype(jnp.bfloat16)
    )
    rows_table = lax.dynamic_slice_in_dim(rows_all, own_mod * row_count, row_count, 0)

    with jax.named_scope("modulation_angles"):
        angles = mod_points.astype(jnp.float32) * (2.0 * math.pi / point_count)
        angles = jnp.broadcast_to(angles[None, :, None], (devices_mod, per_device, LANES))
        angles = lax.all_to_all(angles, "mod", 0, 0, tiled=True).reshape(count, LANES)
    pixels = (valid_pix - own_mod * (row_count * length)).reshape(signal_rows, LANES)
    grid_rows = gx.shape[1]

    f32, bf16 = jnp.float32, jnp.bfloat16
    shape = jax.ShapeDtypeStruct
    field, full_table, cells, gx_parts, gy_parts = call(
        prepare_kernel,
        "prepare",
        (
            shape((2 * pupil, 2 * pupil), bf16),
            shape(full_table.shape, bf16),
            shape((grid_rows, LANES), jnp.int32),
            shape((pupil, 3 * grid_rows), bf16),
            shape((3 * LANES, pupil), bf16),
        ),
        [pltpu.VMEM((act_map.shape[0] // LANES, LANES), f32)],
    )(screen, pupil_amp, full_table, act_map.reshape(-1, LANES), gx.T, gy.T)

    def commands(signal):
        signals = [signal]
        for j in range(1, cases):
            signals.append(lax.ppermute(signal, "case", [(i, i ^ j) for i in range(cases)]))
        partial = call(
            command_kernel,
            "commands",
            shape((cases * devices_mod, pieces, block // pieces), bf16),
            in_specs=[pl.BlockSpec(memory_space=pltpu.SMEM)] + [pl.BlockSpec(memory_space=pltpu.VMEM)] * (cases + 1),
        )(own_case.reshape(1), *signals, recon)
        return lax.all_to_all(partial, ("case", "mod"), 0, 0, tiled=True)

    signal, left, sine, cosine = call(
        first_kernel,
        "first_frame",
        (
            shape((signal_rows, LANES), f32),
            shape((count * row_count, 2 * pupil), bf16),
            shape((count, pupil), f32),
            shape((count, pupil), f32),
        ),
        [pltpu.VMEM((row_count, length), f32)],
    )(angles, field, rows_table, full_table, pixels)
    total_shape = shape((cases, pieces, block // pieces), f32)
    totals = ()
    for iteration in range(1, STEPS):
        parts = commands(signal)
        frame, signal, *totals = call(
            later_kernel,
            "next_frame",
            (
                shape((row_count, length), f32),
                shape((signal_rows, LANES), f32),
                total_shape,
            ),
            [pltpu.VMEM((row_count, length), f32), pltpu.SemaphoreType.DMA(())],
            out_specs=(
                pl.BlockSpec(memory_space=pl.ANY),
                pl.BlockSpec(memory_space=pltpu.VMEM),
                pl.BlockSpec(memory_space=pltpu.VMEM),
            ),
        )(parts, cells, gx_parts, gy_parts, screen, pupil_amp, left, sine, cosine, full_table, pixels, *totals)
    parts = commands(signal)
    command_total = call(
        last_kernel,
        "total",
        shape((1, cases * block), f32),
        [pltpu.VMEM(total_shape.shape, f32)],
    )(parts, *totals)
    return (command_total, frame[None])


def solution(mesh):
    return jax.shard_map(
        body,
        mesh=mesh,
        in_specs=(P("case", None, None), P(), P("mod"), P("mod"), P("case", "mod"), P(), P(), P()),
        out_specs=(P("case", None), P("case", "mod", None)),
        check_vma=False,
    )
```

time: 62.2 us -> 62 us (level)
  blocking collectives: 9.59 us -> 22.4 us
  waiting for transfers between devices: 11.2 us -> 4.42 us
  starting transfers between devices: 14.3 us -> 11.1 us
  local copies, waits for them, and re-layouts: 14.5 us -> 12.6 us
  other arithmetic: 1.97 us -> 0.69 us
    all_to_all x1 -> x2, blocking collectives: 9.59 us -> 22.4 us  [commands(): return lax.all_to_all(partial, ('case', 'mod'), 0, 0, tiled=True)]
    all_to_all x2 -> x1, waiting for transfers between devices: 6.66 us -> 0.01 us  [body(): lax.all_to_all(angles, 'mod', 0, 0, tiled=True).reshape(count, LANES)]
    all_to_all x2 -> x1, starting transfers between devices: 10.5 us -> 7.25 us  [body(): lax.all_to_all(angles, 'mod', 0, 0, tiled=True).reshape(count, LANES)]
    pad x2 -> x0, local copies, waits for them, and re-layouts: 1.51 us -> none  [the longest x1 0.9 us: body(): gy_t = jnp.pad(gy.T, ((0, LANES - grid_columns), (0, 0)))]
    all_to_all x2 -> x0, other arithmetic: 1.28 us -> none  [commands(): return lax.all_to_all(partial, ('case', 'mod'), 0, 0, tiled=True)]
    unnamed x27 -> x36, local copies, waits for them, and re-layouts: 10.1 us -> 11.1 us
    reshape x1 -> x0, local copies, waits for them, and re-layouts: 0.81 us -> none  [body(): act_map.reshape(grid_rows, grid_columns)]
  transfers between devices with their start and end apart: 8 -> 7, of which waited for: 5 -> 4; matrix products, arithmetic and copies ran while one was open for 8% -> 3% of each run, Pallas kernels for 1% -> 3%
where the time goes in v2:
time: 62 us; the launch traced here: 61.4 us
  blocking collectives  22.4 us (36%)
  local copies, waits for them, and re-layouts  12.6 us (20%)
  starting transfers between devices  11.1 us (18%)
  Pallas kernels  8.72 us (14%)
  waiting for transfers between devices  4.42 us (7%)
  between operations  1.54 us (2%)
  other arithmetic  0.69 us (1%)
    all_to_all x2, blocking collectives, commands(): return lax.all_to_all(partial, ('case', 'mod'), 0, 0, tiled=True)  22.4 us
    unnamed x36, local copies, waits for them, and re-layouts  11.1 us
    all_to_all x1, starting transfers between devices, body(): lax.all_to_all(angles, 'mod', 0, 0, tiled=True).reshape(count, LANES)  7.25 us
    ppermute x6, waiting for transfers between devices, commands(): lax.ppermute(signal, 'case', [(i, i ^ j) for i in range(cases)])  4.42 us
    ppermute x6, starting transfers between devices, commands(): lax.ppermute(signal, 'case', [(i, i ^ j) for i in range(cases)])  3.82 us
    pallas_call x1, Pallas kernels, body(): call(later_kernel, 'next_frame', (shape((row_count, length), f32), shape(...  3.36 us
    pallas_call x1, Pallas kernels, body(): call(prepare_kernel, 'prepare', (shape((2 * pupil, 2 * pupil), bf16), sha...  1.67 us
    pallas_call x2, Pallas kernels, commands(): call(command_kernel, 'commands', shape((cases * devices_mod, pieces, bloc...  1.61 us
  transfers between devices with their start and end apart: 7, of which 4 were waited for; matrix products, arithmetic and copies ran while one was open for 3% of the time, Pallas kernels for 3%

profile of v2, /device:TPU:0, one launch (start us, length us, event | category | flops | bytes accessed | tf_op | source)
XLA Modules:
  0.0 61.4 jit_solution(1556527950247143345)
XLA Ops:
  1.4 0.6 broadcast_in_dim.12
  2.0 7.3 %all-to-all-start = ((f32[8,1,128]{2,1,0:T(1,128)}), f32[8,1,128]{2,1,0:T(1,128)S(1)}, u32[]{:S(2)}, u32[]{:S(2)}) async-start(f32[8,1,128]{2,1,0:T(1,128)} %broadcast_in_dim.12), calls=%async_computation | async-start | bytes 8192 | tf_op jit(solution)/shard_map/modulation_angles/all_to_all | solution.py:279
  9.3 0.7 %subtract_bitcast_fusion.pixels_ref = s32[8,128]{1,0:T(8,128)S(1)} fusion(s32[1024]{0:T(1024)} %param.13, s32[]{:T(128)S(6)} %mul.11), kind=kLoop, calls=%fused_computation | loop fusion | flops 1024 | bytes 8196 | tf_op jit(solution)/shard_map/reshape | solution.py:280
  10.0 0.9 %constant_dynamic-slice_fusion.rows_ref = f32[64,512]{1,0:T(8,128)S(1)} fusion(f32[512,512]{1,0:T(8,128)} %constant.22.clone, s32[]{:T(128)S(6)} %select_n.3), kind=kLoop, calls=%fused_computation.1 | loop fusion | bytes 262148 | tf_op jit(solution)/shard_map/dynamic_slice | solution.py:274
  10.9 1.2 %copy-done.4 = bf16[512,1024]{1,0:T(8,128)(2,1)S(1)} copy-done((bf16[512,1024]{1,0:T(8,128)(2,1)S(1)}, bf16[512,1024]{1,0:T(8,128)(2,1)}, u32[]{:S(2)}) %copy-start.4) | copy-done | bytes 1048600
  12.1 0.9 %copy-done.5 = f32[1,256,256]{2,1,0:T(8,128)S(1)} copy-done((f32[1,256,256]{2,1,0:T(8,128)S(1)}, f32[1,256,256]{2,1,0:T(8,128)}, u32[]{:S(2)}) %copy-start.5) | copy-done | bytes 262168
  13.1 0.9 %copy-done.7 = f32[256,256]{1,0:T(8,128)S(1)} copy-done((f32[256,256]{1,0:T(8,128)S(1)}, f32[256,256]{1,0:T(8,128)}, u32[]{:S(2)}) %copy-start.7) | copy-done | bytes 262168
  14.0 0.9 %copy-done.15 = f32[256,80]{0,1:T(8,128)S(1)} copy-done((f32[256,80]{0,1:T(8,128)S(1)}, f32[256,80]{0,1:T(8,128)}, u32[]{:S(2)}) %copy-start.15) | copy-done | bytes 81944
  14.9 0.8 %copy-done.16 = f32[256,64]{0,1:T(8,128)S(1)} copy-done((f32[256,64]{0,1:T(8,128)S(1)}, f32[256,64]{0,1:T(8,128)}, u32[]{:S(2)}) %copy-start.16) | copy-done | bytes 65560
  15.8 0.7 %copy-done.17 = s32[5120]{0:T(1024)S(1)} copy-done((s32[5120]{0:T(1024)S(1)}, s32[5120]{0:T(1024)}, u32[]{:S(2)}) %copy-start.17) | copy-done | bytes 20504
  16.5 1.7 %prepare.1 = (bf16[512,512]{1,0:T(8,128)(2,1)S(1)}, bf16[512,1024]{1,0:T(8,128)(2,1)S(1)}, s32[64,128]{1,0:T(8,128)S(1)}, bf16[256,192]{1,0:T(8,128)(2,1)S(1)}, bf16[384,256]{1,0:T(8,128)(2,1)S(1)}) custom-call(f32[256,256]{1,0:T(8,128)S(1)} %bitcast.10, f32[256,256]{1,0:T(8,128)S(1)} %copy-done.7, bf16[512,1024]{1,0:T(8,128)(2,1)S(1)} %copy-done.4, ...), custom_call_target="tpu_custom_call" | custom-call | tf_op jit(solution)/shard_map/prepare/pallas_call | solution.py:285
  18.2 1.0 %copy-done.1 = bf16[512,1024]{1,0:T(8,128)(2,1)} copy-done((bf16[512,1024]{1,0:T(8,128)(2,1)}, bf16[512,1024]{1,0:T(8,128)(2,1)S(1)}, u32[]{:S(2)}) %copy-start.1) | copy-done | bytes 1048600
  19.2 0.8 %copy-done.11 = bf16[512,512]{1,0:T(8,128)(2,1)} copy-done((bf16[512,512]{1,0:T(8,128)(2,1)}, bf16[512,512]{1,0:T(8,128)(2,1)S(1)}, u32[]{:S(2)}) %copy-start.11) | copy-done | bytes 524312
  20.0 0.7 %copy-done.13 = bf16[256,192]{1,0:T(8,128)(2,1)} copy-done((bf16[256,192]{1,0:T(8,128)(2,1)}, bf16[256,192]{1,0:T(8,128)(2,1)S(1)}, u32[]{:S(2)}) %copy-start.13) | copy-done | bytes 98328
  20.6 1.2 %copy-done.2 = bf16[512,1024]{1,0:T(8,128)(2,1)S(1)} copy-done((bf16[512,1024]{1,0:T(8,128)(2,1)S(1)}, bf16[512,1024]{1,0:T(8,128)(2,1)}, u32[]{:S(2)}) %copy-start.2) | copy-done | bytes 1048600
  21.8 1.0 %copy-done.12 = bf16[512,512]{1,0:T(8,128)(2,1)S(1)} copy-done((bf16[512,512]{1,0:T(8,128)(2,1)S(1)}, bf16[512,512]{1,0:T(8,128)(2,1)}, u32[]{:S(2)}) %copy-start.12) | copy-done | bytes 524312
  22.9 1.4 %first_frame.1 = (f32[8,128]{1,0:T(8,128)S(1)}, bf16[512,512]{1,0:T(8,128)(2,1)S(1)}, f32[8,256]{1,0:T(8,128)S(1)}, f32[8,256]{1,0:T(8,128)S(1)}) custom-call(f32[8,128]{1,0:T(8,128)S(1)} %bitcast.15, bf16[512,512]{1,0:T(8,128)(2,1)S(1)} %copy-done.12, f32[64,512]{1,0:T(8,128)S(1)} %constant_dynamic-slice_fusion.rows_ref, bf16[512,1024]{1,0:T(8,128)(2,1)S(1)} %copy-done.2, ...), custom_call_target="tpu_custom_call" | custom-call | tf_op jit(solution)/shard_map/first_frame/pallas_call | solution.py:310
  24.3 0.8 %copy-done.9 = bf16[512,512]{1,0:T(8,128)(2,1)} copy-done((bf16[512,512]{1,0:T(8,128)(2,1)}, bf16[512,512]{1,0:T(8,128)(2,1)S(1)}, u32[]{:S(2)}) %copy-start.9) | copy-done | bytes 524312
  25.1 0.7 %collective-permute-start.2 = (f32[8,128]{1,0:T(8,128)S(1)}, f32[8,128]{1,0:T(8,128)S(1)}, u32[]{:S(2)}, u32[]{:S(2)}) collective-permute-start(f32[8,128]{1,0:T(8,128)S(1)} %get-tuple-element.16.refs_0_), channel_id=1, source_target_pairs={{0,24},{8,16},{16,8},{24,0},{1,25},{9,17},{17,9},{25,1},{2,26},{10... | collective-permute-start | bytes 12296 | tf_op jit(solution)/shard_map/ppermute | solution.py:301
  25.7 0.9 %collective-permute-start.1 = (f32[8,128]{1,0:T(8,128)S(1)}, f32[8,128]{1,0:T(8,128)S(1)}, u32[]{:S(2)}, u32[]{:S(2)}) collective-permute-start(f32[8,128]{1,0:T(8,128)S(1)} %get-tuple-element.16.refs_0_), channel_id=1, source_target_pairs={{0,16},{8,24},{16,0},{24,8},{1,17},{9,25},{17,1},{25,9},{2,18},{10... | collective-permute-start | bytes 12296 | tf_op jit(solution)/shard_map/ppermute | solution.py:301
  26.9 1.2 %collective-permute-done.2.refs_3_ = f32[8,128]{1,0:T(8,128)S(1)} collective-permute-done((f32[8,128]{1,0:T(8,128)S(1)}, f32[8,128]{1,0:T(8,128)S(1)}, u32[]{:S(2)}, u32[]{:S(2)}) %collective-permute-start.2) | collective-permute-done | bytes 4128 | tf_op jit(solution)/shard_map/ppermute | solution.py:301
  28.1 1.3 %collective-permute-done.1.refs_2_ = f32[8,128]{1,0:T(8,128)S(1)} collective-permute-done((f32[8,128]{1,0:T(8,128)S(1)}, f32[8,128]{1,0:T(8,128)S(1)}, u32[]{:S(2)}, u32[]{:S(2)}) %collective-permute-start.1) | collective-permute-done | bytes 4128 | tf_op jit(solution)/shard_map/ppermute | solution.py:301
  29.4 0.8 %commands.2 = bf16[32,2,640]{2,1,0:T(2,128)(2,1)S(1)} custom-call(s32[1]{0:T(128)} %bitcast.own_case_ref, f32[8,128]{1,0:T(8,128)S(1)} %get-tuple-element.16.refs_0_, f32[8,128]{1,0:T(8,128)S(1)} %collective-permute-done.refs_1_, f32[8,128]{1,0:T(8,128)S(1)} %collective-permute-done.1.refs_2_, f32[8,128]{1,0:T(8,128)S(1)} %collective-permute-done.2.refs_3_, ...), custom_call_target="tpu_custom_call" | custom-call | tf_op jit(solution)/shard_map/commands/pallas_call | solution.py:302
  30.2 12.6 %all_to_all.15.parts_ref = bf16[32,2,640]{2,1,0:T(2,128)(2,1)S(1)} all-to-all(bf16[32,2,640]{2,1,0:T(2,128)(2,1)S(1)} %commands.2), channel_id=1, replica_groups=mesh['case'=4,'mod'=8] {'case','mod'}, dimensions={0} | all-to-all | bytes 163840 | tf_op jit(solution)/shard_map/all_to_all | solution.py:308
  42.8 3.4 %next_frame.1 = (f32[64,512]{1,0:T(8,128)}, f32[8,128]{1,0:T(8,128)S(1)}, f32[4,2,640]{2,1,0:T(2,128)S(1)}) custom-call(bf16[32,2,640]{2,1,0:T(2,128)(2,1)S(1)} %all_to_all.15.parts_ref, s32[64,128]{1,0:T(8,128)S(1)} %get-tuple-element.17.cells_ref, bf16[256,192]{1,0:T(8,128)(2,1)S(1)} %copy-done.14, bf16[384,256]{1,0:T(8,128)(2,1)S(1)} %get-tuple-element.19.gy_ref, ...), custom_call_target="tpu_custom_call" | custom-call | tf_op jit(solution)/shard_map/next_frame/pallas_call | solution.py:325
  46.2 0.3 collective-permute-start.5
  46.5 1.5 %collective-permute-start.4 = (f32[8,128]{1,0:T(8,128)S(1)}, f32[8,128]{1,0:T(8,128)S(1)}, u32[]{:S(2)}, u32[]{:S(2)}) collective-permute-start(f32[8,128]{1,0:T(8,128)S(1)} %get-tuple-element.23.refs_0_), channel_id=1, source_target_pairs={{0,16},{8,24},{16,0},{24,8},{1,17},{9,25},{17,1},{25,9},{2,18},{10... | collective-permute-start | bytes 12296 | tf_op jit(solution)/shard_map/ppermute | solution.py:301
  48.2 1.1 %collective-permute-done.5.refs_3_ = f32[8,128]{1,0:T(8,128)S(1)} collective-permute-done((f32[8,128]{1,0:T(8,128)S(1)}, f32[8,128]{1,0:T(8,128)S(1)}, u32[]{:S(2)}, u32[]{:S(2)}) %collective-permute-start.5) | collective-permute-done | bytes 4128 | tf_op jit(solution)/shard_map/ppermute | solution.py:301
  49.3 0.8 %collective-permute-done.4.refs_2_ = f32[8,128]{1,0:T(8,128)S(1)} collective-permute-done((f32[8,128]{1,0:T(8,128)S(1)}, f32[8,128]{1,0:T(8,128)S(1)}, u32[]{:S(2)}, u32[]{:S(2)}) %collective-permute-start.4) | collective-permute-done | bytes 4128 | tf_op jit(solution)/shard_map/ppermute | solution.py:301
  50.1 0.8 %commands.3 = bf16[32,2,640]{2,1,0:T(2,128)(2,1)S(1)} custom-call(s32[1]{0:T(128)} %bitcast.own_case_ref, f32[8,128]{1,0:T(8,128)S(1)} %get-tuple-element.23.refs_0_, f32[8,128]{1,0:T(8,128)S(1)} %collective-permute-done.3.refs_1_, f32[8,128]{1,0:T(8,128)S(1)} %collective-permute-done.4.refs_2_, f32[8,128]{1,0:T(8,128)S(1)} %collective-permute-done.5.refs_3_, ...), custom_call_target="tpu_custom_call" | custom-call | tf_op jit(solution)/shard_map/commands/pallas_call | solution.py:302
  51.0 9.8 %all_to_all.16.parts_ref = bf16[32,2,640]{2,1,0:T(2,128)(2,1)S(1)} all-to-all(bf16[32,2,640]{2,1,0:T(2,128)(2,1)S(1)} %commands.3), channel_id=1, replica_groups=mesh['case'=4,'mod'=8] {'case','mod'}, dimensions={0} | all-to-all | bytes 163840 | tf_op jit(solution)/shard_map/all_to_all | solution.py:308
  60.7 0.7 %total.1 = f32[1,5120]{1,0:T(1,128)} custom-call(bf16[32,2,640]{2,1,0:T(2,128)(2,1)S(1)} %all_to_all.16.parts_ref, f32[4,2,640]{2,1,0:T(2,128)S(1)} %get-tuple-element.24.total_ref), custom_call_target="tpu_custom_call" | custom-call | tf_op jit(solution)/shard_map/total/pallas_call | solution.py:341
  (29 shorter events, 0.5 us)
Async XLA Ops:
  0.6 28.8 %copy-start = (bf16[1280,1024]{1,0:T(8,128)(2,1)S(1)}, bf16[1280,1024]{1,0:T(8,128)(2,1)}, u32[]{:S(2)}) copy-start(bf16[1280,1024]{1,0:T(8,128)(2,1)} %refs_4_.3) | copy-start | bytes 7864324
  2.0 18.6 %all-to-all-start = ((f32[8,1,128]{2,1,0:T(1,128)}), f32[8,1,128]{2,1,0:T(1,128)S(1)}, u32[]{:S(2)}, u32[]{:S(2)}) async-start(f32[8,1,128]{2,1,0:T(1,128)} %broadcast_in_dim.12), calls=%async_computation | async-start | bytes 8192 | tf_op jit(solution)/shard_map/modulation_angles/all_to_all | solution.py:279
  10.9 1.2 %copy-start.4 = (bf16[512,1024]{1,0:T(8,128)(2,1)S(1)}, bf16[512,1024]{1,0:T(8,128)(2,1)}, u32[]{:S(2)}) copy-start(bf16[512,1024]{1,0:T(8,128)(2,1)} %constant.23.clone.table_ref) | copy-start | bytes 3145732
  12.1 0.9 %copy-start.5 = (f32[1,256,256]{2,1,0:T(8,128)S(1)}, f32[1,256,256]{2,1,0:T(8,128)}, u32[]{:S(2)}) copy-start(f32[1,256,256]{2,1,0:T(8,128)} %param.10) | copy-start | bytes 786436
  13.1 0.9 %copy-start.7 = (f32[256,256]{1,0:T(8,128)S(1)}, f32[256,256]{1,0:T(8,128)}, u32[]{:S(2)}) copy-start(f32[256,256]{1,0:T(8,128)} %amp_ref.3) | copy-start | bytes 786436
  14.0 0.9 %copy-start.15 = (f32[256,80]{0,1:T(8,128)S(1)}, f32[256,80]{0,1:T(8,128)}, u32[]{:S(2)}) copy-start(f32[256,80]{0,1:T(8,128)} %param.16) | copy-start | bytes 245764
  14.9 0.8 %copy-start.16 = (f32[256,64]{0,1:T(8,128)S(1)}, f32[256,64]{0,1:T(8,128)}, u32[]{:S(2)}) copy-start(f32[256,64]{0,1:T(8,128)} %param.15) | copy-start | bytes 196612
  15.7 0.7 %copy-start.17 = (s32[5120]{0:T(1024)S(1)}, s32[5120]{0:T(1024)}, u32[]{:S(2)}) copy-start(s32[5120]{0:T(1024)} %param.17) | copy-start | bytes 61444
  18.2 1.0 %copy-start.1 = (bf16[512,1024]{1,0:T(8,128)(2,1)}, bf16[512,1024]{1,0:T(8,128)(2,1)S(1)}, u32[]{:S(2)}) copy-start(bf16[512,1024]{1,0:T(8,128)(2,1)S(1)} %get-tuple-element.15.full_ref) | copy-start | bytes 3145732
  19.2 0.8 %copy-start.11 = (bf16[512,512]{1,0:T(8,128)(2,1)}, bf16[512,512]{1,0:T(8,128)(2,1)S(1)}, u32[]{:S(2)}) copy-start(bf16[512,512]{1,0:T(8,128)(2,1)S(1)} %get-tuple-element.14.field_ref) | copy-start | bytes 1572868
  20.0 0.7 %copy-start.13 = (bf16[256,192]{1,0:T(8,128)(2,1)}, bf16[256,192]{1,0:T(8,128)(2,1)S(1)}, u32[]{:S(2)}) copy-start(bf16[256,192]{1,0:T(8,128)(2,1)S(1)} %get-tuple-element.18.gx_ref) | copy-start | bytes 294916
  20.6 1.2 %copy-start.2 = (bf16[512,1024]{1,0:T(8,128)(2,1)S(1)}, bf16[512,1024]{1,0:T(8,128)(2,1)}, u32[]{:S(2)}) copy-start(bf16[512,1024]{1,0:T(8,128)(2,1)} %copy-done.1) | copy-start | bytes 3145732
  21.8 1.0 %copy-start.12 = (bf16[512,512]{1,0:T(8,128)(2,1)S(1)}, bf16[512,512]{1,0:T(8,128)(2,1)}, u32[]{:S(2)}) copy-start(bf16[512,512]{1,0:T(8,128)(2,1)} %copy-done.11) | copy-start | bytes 1572868
  22.9 19.9 %copy-start.6 = (f32[1,256,256]{2,1,0:T(8,128)S(1)}, f32[1,256,256]{2,1,0:T(8,128)}, u32[]{:S(2)}) copy-start(f32[1,256,256]{2,1,0:T(8,128)} %param.10) | copy-start | bytes 786436
  22.9 19.9 %copy-start.8 = (f32[256,256]{1,0:T(8,128)S(1)}, f32[256,256]{1,0:T(8,128)}, u32[]{:S(2)}) copy-start(f32[256,256]{1,0:T(8,128)} %amp_ref.3) | copy-start | bytes 786436
  24.3 0.8 %copy-start.9 = (bf16[512,512]{1,0:T(8,128)(2,1)}, bf16[512,512]{1,0:T(8,128)(2,1)S(1)}, u32[]{:S(2)}) copy-start(bf16[512,512]{1,0:T(8,128)(2,1)S(1)} %get-tuple-element.20.left_ref) | copy-start | bytes 1572868
  25.1 17.8 %copy-start.14 = (bf16[256,192]{1,0:T(8,128)(2,1)S(1)}, bf16[256,192]{1,0:T(8,128)(2,1)}, u32[]{:S(2)}) copy-start(bf16[256,192]{1,0:T(8,128)(2,1)} %copy-done.13) | copy-start | bytes 294916
  25.1 3.0 %collective-permute-start.2 = (f32[8,128]{1,0:T(8,128)S(1)}, f32[8,128]{1,0:T(8,128)S(1)}, u32[]{:S(2)}, u32[]{:S(2)}) collective-permute-start(f32[8,128]{1,0:T(8,128)S(1)} %get-tuple-element.16.refs_0_), channel_id=1, source_target_pairs={{0,24},{8,16},{16,8},{24,0},{1,25},{9,17},{17,9},{25,1},{2,26},{10... | collective-permute-start | bytes 12296 | tf_op jit(solution)/shard_map/ppermute | solution.py:301
  25.7 3.6 %collective-permute-start.1 = (f32[8,128]{1,0:T(8,128)S(1)}, f32[8,128]{1,0:T(8,128)S(1)}, u32[]{:S(2)}, u32[]{:S(2)}) collective-permute-start(f32[8,128]{1,0:T(8,128)S(1)} %get-tuple-element.16.refs_0_), channel_id=1, source_target_pairs={{0,16},{8,24},{16,0},{24,8},{1,17},{9,25},{17,1},{25,9},{2,18},{10... | collective-permute-start | bytes 12296 | tf_op jit(solution)/shard_map/ppermute | solution.py:301
  26.6 2.8 %collective-permute-start = (f32[8,128]{1,0:T(8,128)S(1)}, f32[8,128]{1,0:T(8,128)S(1)}, u32[]{:S(2)}, u32[]{:S(2)}) collective-permute-start(f32[8,128]{1,0:T(8,128)S(1)} %get-tuple-element.16.refs_0_), channel_id=1, source_target_pairs={{0,8},{8,0},{16,24},{24,16},{1,9},{9,1},{17,25},{25,17},{2,10},{10... | collective-permute-start | bytes 12296 | tf_op jit(solution)/shard_map/ppermute | solution.py:301
  26.9 15.9 %copy-start.3 = (bf16[512,1024]{1,0:T(8,128)(2,1)S(1)}, bf16[512,1024]{1,0:T(8,128)(2,1)}, u32[]{:S(2)}) copy-start(bf16[512,1024]{1,0:T(8,128)(2,1)} %copy-done.1) | copy-start | bytes 3145732
  26.9 15.9 %copy-start.10 = (bf16[512,512]{1,0:T(8,128)(2,1)S(1)}, bf16[512,512]{1,0:T(8,128)(2,1)}, u32[]{:S(2)}) copy-start(bf16[512,512]{1,0:T(8,128)(2,1)} %copy-done.9) | copy-start | bytes 1572868
  46.2 3.1 %collective-permute-start.5 = (f32[8,128]{1,0:T(8,128)S(1)}, f32[8,128]{1,0:T(8,128)S(1)}, u32[]{:S(2)}, u32[]{:S(2)}) collective-permute-start(f32[8,128]{1,0:T(8,128)S(1)} %get-tuple-element.23.refs_0_), channel_id=1, source_target_pairs={{0,24},{8,16},{16,8},{24,0},{1,25},{9,17},{17,9},{25,1},{2,26},{10... | collective-permute-start | bytes 12296 | tf_op jit(solution)/shard_map/ppermute | solution.py:301
  46.5 3.6 %collective-permute-start.4 = (f32[8,128]{1,0:T(8,128)S(1)}, f32[8,128]{1,0:T(8,128)S(1)}, u32[]{:S(2)}, u32[]{:S(2)}) collective-permute-start(f32[8,128]{1,0:T(8,128)S(1)} %get-tuple-element.23.refs_0_), channel_id=1, source_target_pairs={{0,16},{8,24},{16,0},{24,8},{1,17},{9,25},{17,1},{25,9},{2,18},{10... | collective-permute-start | bytes 12296 | tf_op jit(solution)/shard_map/ppermute | solution.py:301
  48.0 2.1 %collective-permute-start.3 = (f32[8,128]{1,0:T(8,128)S(1)}, f32[8,128]{1,0:T(8,128)S(1)}, u32[]{:S(2)}, u32[]{:S(2)}) collective-permute-start(f32[8,128]{1,0:T(8,128)S(1)} %get-tuple-element.23.refs_0_), channel_id=1, source_target_pairs={{0,8},{8,0},{16,24},{24,16},{1,9},{9,1},{17,25},{25,17},{2,10},{10... | collective-permute-start | bytes 12296 | tf_op jit(solution)/shard_map/ppermute | solution.py:301

commit v3 on v2

v3 whole, which is shorter than its diff:
```python
import math

import jax
import jax.numpy as jnp
import numpy as np
from jax import lax
from jax.experimental import pallas as pl
from jax.experimental.pallas import tpu as pltpu
from jax.sharding import PartitionSpec as P

STEPS = 2


loop_gain = 0.5
radius_pixels = 6.0
point_count = 256
LANES = 128
VMEM_LIMIT = 16 * 1024 * 1024


def rounded_table(angle, length, sign):
    scale = 1.0 / math.sqrt(length)
    real = (np.cos(angle) * scale).astype(np.float32).astype(jnp.bfloat16).astype(np.float64)
    imag = (sign * np.sin(angle) * scale).astype(np.float32).astype(jnp.bfloat16).astype(np.float64)
    return real + 1j * imag


def pyramid_table(pupil_size, length):
    centred = np.arange(length) - length // 2
    forward = np.mod(centred[:, None] * np.arange(pupil_size)[None, :], length) * (2.0 * math.pi / length)
    inverse = np.mod(np.arange(length)[:, None] * centred[None, :], length) * (2.0 * math.pi / length)
    mask = np.array([1, 1j, -1, -1j])[np.abs(centred) % 4]
    return rounded_table(inverse, length, 1.0) @ (mask[:, None] * rounded_table(forward, length, -1.0))


def sin_cos(angle):
    turns = jnp.floor(angle * (2.0 / math.pi) + 0.5)
    rest = angle - turns * 1.5703125
    rest = rest - turns * 4.837512969970703125e-4
    rest = rest - turns * 7.54978995489188216e-8
    square = rest * rest
    sine = rest + rest * square * (-1.6666654611e-1 + square * (8.3321608736e-3 - square * 1.9515295891e-4))
    cosine = (
        1.0
        - 0.5 * square
        + square * square * (4.166664568298827e-2 + square * (-1.388731625493765e-3 + square * 2.443315711809948e-5))
    )
    quarter = turns.astype(jnp.int32)
    swap = (quarter & 1) == 1
    sin_out = jnp.where(swap, cosine, sine)
    cos_out = jnp.where(swap, sine, cosine)
    sin_out = jnp.where((quarter & 2) == 2, -sin_out, sin_out)
    cos_out = jnp.where(((quarter + 1) & 2) == 2, -cos_out, cos_out)
    return sin_out, cos_out


def field_matrix(real, imag):
    return jnp.concatenate([jnp.concatenate([real, imag], 1), jnp.concatenate([-imag, real], 1)], 0)


def halves(values):
    high = values.astype(jnp.bfloat16)
    low = (values - high.astype(jnp.float32)).astype(jnp.bfloat16)
    return high, low


def look_up(count, row, index):
    high = index >> 7
    low = index & (LANES - 1)
    sums = [jnp.zeros(index.shape, jnp.float32) for _ in range(4)]
    for i in range(count):
        spread = jnp.broadcast_to(row(i), index.shape)
        picked = jnp.take_along_axis(spread, low, axis=1, mode="promise_in_bounds")
        sums[i % 4] = jnp.where(high == i, picked, sums[i % 4])
    return (sums[0] + sums[1]) + (sums[2] + sums[3])


def runs(ref):
    per_row = ref.shape[1] // LANES

    def row(i):
        column = (i % per_row) * LANES
        return ref[i // per_row : i // per_row + 1, column : column + LANES]

    return ref.shape[0] * per_row, row


def copies(pairs, semaphores):
    started = [pltpu.make_async_copy(*pair, semaphores.at[i]) for i, pair in enumerate(pairs)]
    for copy in started:
        copy.start()
    return started


def spread_kernel(point_ref, angles_ref):
    angle = point_ref[0].astype(jnp.float32) * (2.0 * math.pi / point_count)
    angles_ref[...] = jnp.full(angles_ref.shape, angle, jnp.float32)


def prepare_kernel(
    phase_hbm, amp_hbm, map_hbm, gxt_hbm, gyt_hbm, field_ref, cells_hbm, gx_hbm, gy_hbm,
    phase_ref, amp_ref, map_ref, gxt_ref, gyt_ref, floats, cells_ref, gx_ref, gy_ref, semaphores,
):
    phase, amp, actuators, gxt, gyt = copies(
        [(phase_hbm, phase_ref), (amp_hbm, amp_ref), (map_hbm, map_ref), (gxt_hbm, gxt_ref), (gyt_hbm, gyt_ref)],
        semaphores,
    )
    actuators.wait()
    floats[...] = map_ref[...].astype(jnp.float32)
    grid_rows, grid_columns = gxt_ref.shape[0], gyt_ref.shape[0]
    cell = lax.broadcasted_iota(jnp.int32, cells_ref.shape, 0) * grid_columns
    column = lax.broadcasted_iota(jnp.int32, cells_ref.shape, 1)
    cell = jnp.where(column < grid_columns, cell + column, 0)
    cells_ref[...] = look_up(*runs(floats), cell).astype(jnp.int32)
    gxt.wait()
    high, low = halves(gxt_ref[...].T)
    gx_ref[...] = jnp.concatenate([high, low, high], 1)
    gyt.wait()
    padded = jnp.concatenate(
        [gyt_ref[...], jnp.zeros((LANES - grid_columns, gyt_ref.shape[1]), jnp.float32)], 0
    )
    high, low = halves(padded)
    gy_ref[...] = jnp.concatenate([high, high, low], 0)
    phase.wait()
    amp.wait()
    out = copies([(cells_ref, cells_hbm), (gx_ref, gx_hbm), (gy_ref, gy_hbm)], semaphores)
    sine, cosine = sin_cos(phase_ref[...])
    amplitude = amp_ref[...]
    field_ref[...] = jnp.concatenate([amplitude * cosine, amplitude * sine], 1).astype(jnp.bfloat16)
    for copy in out:
        copy.wait()


def tilt_factors(angles_ref, pupil, length):
    sin_a, cos_a = sin_cos(angles_ref[...])
    spread = pupil // LANES
    sin_a = jnp.concatenate([sin_a] * spread, 1)
    cos_a = jnp.concatenate([cos_a] * spread, 1)
    place = (lax.broadcasted_iota(jnp.int32, sin_a.shape, 1) - pupil // 2).astype(jnp.float32)
    place = place * (2.0 * math.pi * radius_pixels / length)
    return sin_cos(place * cos_a), sin_cos(place * sin_a)


def turned(real, imag, sine, cosine):
    sine, cosine = sine[:, None, :], cosine[:, None, :]
    return jnp.concatenate([real * cosine - imag * sine, real * sine + imag * cosine], 2)


def first_half(left, field, sine, cosine):
    count, pupil = sine.shape
    half = jnp.dot(left, field, preferred_element_type=jnp.float32)
    half = half.reshape(count, left.shape[0] // count, 2 * pupil)
    half = turned(half[:, :, :pupil], half[:, :, pupil:], sine, cosine)
    return half.reshape(left.shape).astype(jnp.bfloat16)


def second_half(half, full_table, count):
    length = full_table.shape[1] // 2
    detector = jnp.dot(half, full_table, preferred_element_type=jnp.float32)
    real, imag = detector[:, :length], detector[:, length:]
    intensity = (real * real + imag * imag).reshape(count, half.shape[0] // count, length)
    return jnp.sum(intensity, 0) * (1.0 / count)


def read_signals(frame_ref, pixels):
    return look_up(*runs(frame_ref), pixels).astype(jnp.bfloat16).astype(jnp.float32)


def own_pixels(pixels_ref, row_count, length):
    return pixels_ref[...] - lax.axis_index("mod") * (row_count * length)


def first_kernel(
    angles_ref, field_ref, rows_hbm, full_hbm, pixels_hbm, signal_ref, left_hbm, tilt_ref,
    rows_ref, full_ref, pixels_ref, left_ref, frame_ref, semaphores,
):
    row_count, length = frame_ref.shape
    count, pupil = angles_ref.shape[0], length // 2
    own_rows = pl.ds(pl.multiple_of(lax.axis_index("mod") * row_count, row_count), row_count)
    rows, full, pixels = copies(
        [(rows_hbm.at[own_rows], rows_ref), (full_hbm, full_ref), (pixels_hbm, pixels_ref)], semaphores
    )
    (s1, c1), (s2, c2) = tilt_factors(angles_ref, pupil, length)
    tilt_ref[:count] = s2
    tilt_ref[count:] = c2
    rows.wait()
    own = rows_ref[...]
    left = turned(own[None, :, :pupil], own[None, :, pupil:], s1, c1)
    left = left.reshape(left_ref.shape).astype(jnp.bfloat16)
    left_ref[...] = left
    left_out = pltpu.make_async_copy(left_ref, left_hbm, semaphores.at[0])
    left_out.start()
    field = field_matrix(field_ref[:, :pupil], field_ref[:, pupil:])
    half = first_half(left, field, s2, c2)
    full.wait()
    frame_ref[...] = second_half(half, full_ref[...], count)
    pixels.wait()
    signal_ref[...] = read_signals(frame_ref, own_pixels(pixels_ref, row_count, length))
    left_out.wait()


def add_commands(parts_ref, total_ref, out_ref):
    cases = out_ref.shape[0]
    each = parts_ref.shape[0] // cases
    for case in range(cases):
        sums = jnp.sum(parts_ref[case * each : (case + 1) * each].astype(jnp.float32), 0)
        out_ref[case] = loop_gain * sums if total_ref is None else total_ref[case] + loop_gain * sums


def later_kernel(
    parts_ref, tilt_ref, cells_hbm, gx_hbm, gy_hbm, phase_hbm, amp_hbm, left_hbm, full_hbm, pixels_hbm, *refs
):
    old_total, refs = (None, refs) if len(refs) == 13 else (refs[0], refs[1:])
    frame_hbm, signal_ref, new_total_ref, frame_ref = refs[:4]
    cells_ref, gx_ref, gy_ref, phase_ref, amp_ref, left_ref, full_ref, pixels_ref = refs[4:12]
    semaphores = refs[12]
    cells, gx, gy, phase, amp, left, full, pixels = copies(
        [
            (cells_hbm, cells_ref), (gx_hbm, gx_ref), (gy_hbm, gy_ref), (phase_hbm, phase_ref), (amp_hbm, amp_ref),
            (left_hbm, left_ref), (full_hbm, full_ref), (pixels_hbm, pixels_ref),
        ],
        semaphores,
    )
    row_count, length = frame_ref.shape
    count = tilt_ref.shape[0] // 2
    add_commands(parts_ref, old_total, new_total_ref)
    cases, pieces, width = new_total_ref.shape
    per_piece = width // LANES

    def row(i):
        column = (i % per_piece) * LANES
        piece = i // per_piece
        return new_total_ref[piece // pieces, piece % pieces : piece % pieces + 1, column : column + LANES]

    cells.wait()
    grid = look_up(cases * pieces * per_piece, row, cells_ref[...])
    high, low = halves(grid)
    gx.wait()
    rows_mapped = jnp.dot(
        gx_ref[...], jnp.concatenate([high, high, low], 0), preferred_element_type=jnp.float32
    )
    high, low = halves(rows_mapped)
    gy.wait()
    surface = jnp.dot(
        jnp.concatenate([high, low, high], 1), gy_ref[...], preferred_element_type=jnp.float32
    )
    phase.wait()
    sine, cosine = sin_cos(phase_ref[...] - surface)
    amp.wait()
    amplitude = amp_ref[...]
    field = field_matrix((amplitude * cosine).astype(jnp.bfloat16), (amplitude * sine).astype(jnp.bfloat16))
    left.wait()
    half = first_half(left_ref[...], field, tilt_ref[:count], tilt_ref[count:])
    full.wait()
    frame_ref[...] = second_half(half, full_ref[...], count)
    frame_out = pltpu.make_async_copy(frame_ref, frame_hbm, semaphores.at[0])
    frame_out.start()
    pixels.wait()
    signal_ref[...] = read_signals(frame_ref, own_pixels(pixels_ref, row_count, length))
    frame_out.wait()


def command_kernel(*refs):
    signal_refs, recon_ref, out_ref = refs[:-2], refs[-2], refs[-1]
    cases = len(signal_refs)
    own_case = lax.axis_index("case")
    received = [ref[...] for ref in signal_refs]
    ordered = []
    for case in range(cases):
        values = received[0]
        for j in range(1, cases):
            values = jnp.where((own_case ^ j) == case, received[j], values)
        ordered.append(values)
    groups = received[0].shape[0]
    signals = jnp.concatenate(
        [jnp.concatenate([values[g : g + 1] for values in ordered], 0) for g in range(groups)], 1
    ).astype(jnp.bfloat16)
    partial = lax.dot_general(
        signals, recon_ref[...], (((1,), (1,)), ((), ())), preferred_element_type=jnp.float32
    )
    messages, pieces, width = out_ref.shape
    copies = messages // cases
    for case in range(cases):
        message = jnp.concatenate(
            [partial[case : case + 1, i * width : (i + 1) * width] for i in range(pieces)], 0
        ).astype(jnp.bfloat16)
        for i in range(copies):
            out_ref[case * copies + i] = message


def last_kernel(parts_ref, total_ref, out_ref, sums_ref):
    add_commands(parts_ref, total_ref, sums_ref)
    cases, pieces, width = sums_ref.shape
    for case in range(cases):
        for i in range(pieces):
            start = (case * pieces + i) * width
            out_ref[:, start : start + width] = sums_ref[case, i : i + 1, :]


def body(turbulence, pupil_amp, mod_points, valid_pix, recon, gx, gy, act_map):
    pupil = pupil_amp.shape[0]
    length = 2 * pupil
    cases = lax.axis_size("case")
    devices_mod = lax.axis_size("mod")
    count = devices_mod * mod_points.shape[0]
    row_count = length // devices_mod
    block = recon.shape[0]
    pieces = 2
    signal_rows = valid_pix.shape[0] // LANES
    grid_rows = gx.shape[1]
    screen = turbulence[0]
    pixels = valid_pix.reshape(signal_rows, LANES)
    f32, bf16 = jnp.float32, jnp.bfloat16
    shape = jax.ShapeDtypeStruct
    hbm = pl.BlockSpec(memory_space=pltpu.HBM)
    vmem = pl.BlockSpec(memory_space=pltpu.VMEM)
    smem = pl.BlockSpec(memory_space=pltpu.SMEM)

    def call(kernel, name, outs, out_specs, in_specs, scratch, *operands):
        operands = [
            pltpu.with_memory_space_constraint(operand, pltpu.HBM) if spec is hbm else operand
            for operand, spec in zip(operands, in_specs)
        ]
        if isinstance(outs, tuple):
            outs = tuple(
                pltpu.HBM(out.shape, out.dtype) if spec is hbm else out for out, spec in zip(outs, out_specs)
            )
        return pl.pallas_call(
            kernel,
            out_shape=outs,
            in_specs=in_specs,
            out_specs=out_specs,
            scratch_shapes=scratch,
            compiler_params=pltpu.CompilerParams(vmem_limit_bytes=VMEM_LIMIT),
            name=name,
        )(*operands)

    def like(*arrays):
        return [pltpu.VMEM(array.shape, array.dtype) for array in arrays]

    def done(count):
        return pltpu.SemaphoreType.DMA((count,))

    table = pyramid_table(pupil, length)
    rows_table = jnp.asarray(np.concatenate([table.real, table.imag], 1).astype(np.float32))
    full_table = jnp.asarray(
        np.concatenate(
            [
                np.concatenate([table.real.T, table.imag.T], 1),
                np.concatenate([-table.imag.T, table.real.T], 1),
            ],
            0,
        ).astype(jnp.bfloat16)
    )

    with jax.named_scope("modulation_angles"):
        angles = call(
            spread_kernel, "spread", shape((devices_mod, 1, LANES), f32), vmem, [smem], [], mod_points
        )
        angles = lax.all_to_all(angles, "mod", 0, 0, tiled=True).reshape(count, LANES)

    field, cells, gx_parts, gy_parts = call(
        prepare_kernel,
        "prepare",
        (
            shape((pupil, 2 * pupil), bf16),
            shape((grid_rows, LANES), jnp.int32),
            shape((pupil, 3 * grid_rows), bf16),
            shape((3 * LANES, pupil), bf16),
        ),
        (vmem, hbm, hbm, hbm),
        [hbm] * 5,
        like(screen, pupil_amp)
        + [
            pltpu.VMEM((act_map.shape[0] // LANES, LANES), jnp.int32),
            pltpu.VMEM(gx.shape[::-1], f32),
            pltpu.VMEM(gy.shape[::-1], f32),
            pltpu.VMEM((act_map.shape[0] // LANES, LANES), f32),
            pltpu.VMEM((grid_rows, LANES), jnp.int32),
            pltpu.VMEM((pupil, 3 * grid_rows), bf16),
            pltpu.VMEM((3 * LANES, pupil), bf16),
            done(5),
        ],
        screen, pupil_amp, act_map.reshape(-1, LANES), gx.T, gy.T,
    )

    def commands(signal):
        signals = [signal]
        for j in range(1, cases):
            signals.append(lax.ppermute(signal, "case", [(i, i ^ j) for i in range(cases)]))
        partial = call(
            command_kernel, "commands", shape((cases * devices_mod, pieces, block // pieces), bf16), vmem,
            [vmem] * (cases + 1), [], *signals, recon,
        )
        return lax.all_to_all(partial, ("case", "mod"), 0, 0, tiled=True)

    frame_shape = shape((row_count, length), f32)
    signal_shape = shape((signal_rows, LANES), f32)
    left_shape = shape((count * row_count, 2 * pupil), bf16)
    total_shape = shape((cases, pieces, block // pieces), f32)
    signal, left, tilt = call(
        first_kernel,
        "first_frame",
        (signal_shape, left_shape, shape((2 * count, pupil), f32)),
        (vmem, hbm, vmem),
        [vmem, vmem, hbm, hbm, hbm],
        [pltpu.VMEM((row_count, 2 * pupil), f32)] + like(full_table, pixels, left_shape, frame_shape) + [done(3)],
        angles, field, rows_table, full_table, pixels,
    )
    totals = ()
    for iteration in range(1, STEPS):
        parts = commands(signal)
        held = (cells, gx_parts, gy_parts, screen, pupil_amp, left, full_table, pixels)
        frame, signal, *totals = call(
            later_kernel,
            "next_frame",
            (frame_shape, signal_shape, total_shape),
            (hbm, vmem, vmem),
            [vmem, vmem] + [hbm] * len(held) + [vmem] * len(totals),
            like(frame_shape, *held) + [done(len(held))],
            parts, tilt, *held, *totals,
        )
    parts = commands(signal)
    command_total = call(
        last_kernel, "total", shape((1, cases * block), f32), vmem, [vmem, vmem], like(total_shape), parts, *totals
    )
    return (command_total, frame[None])


def solution(mesh):
    return jax.shard_map(
        body,
        mesh=mesh,
        in_specs=(P("case", None, None), P(), P("mod"), P("mod"), P("case", "mod"), P(), P(), P()),
        out_specs=(P("case", None), P("case", "mod", None)),
        check_vma=False,
    )
```

time: 62 us -> 52.8 us (0.85)
  local copies, waits for them, and re-layouts: 12.6 us -> 0.01 us
  Pallas kernels: 8.72 us -> 13 us
  waiting for transfers between devices: 4.42 us -> 7.27 us
  blocking collectives: 22.4 us -> 19.6 us
  other arithmetic: 0.69 us -> 0 us
    unnamed x36 -> x2, local copies, waits for them, and re-layouts: 11.1 us -> 0.01 us
    pallas_call x6 -> x7, Pallas kernels: 8.72 us -> 13 us  [call(): pl.pallas_call(kernel, out_shape=outs, in_specs=in_specs, out_specs=out_s...]
    all_to_all x1, waiting for transfers between devices: 0.01 us -> 3.48 us  [body(): lax.all_to_all(angles, 'mod', 0, 0, tiled=True).reshape(count, LANES)]
    all_to_all x2, blocking collectives: 22.4 us -> 19.6 us  [commands(): return lax.all_to_all(partial, ('case', 'mod'), 0, 0, tiled=True)]
    dynamic_slice x1 -> x0, local copies, waits for them, and re-layouts: 0.91 us -> none  [body(): lax.dynamic_slice_in_dim(rows_all, own_mod * row_count, row_count, 0)]
    reshape x1 -> x0, other arithmetic: 0.69 us -> none  [body(): (valid_pix - own_mod * (row_count * length)).reshape(signal_rows, LANES)]
    ppermute x6, waiting for transfers between devices: 4.42 us -> 3.79 us  [commands(): lax.ppermute(signal, 'case', [(i, i ^ j) for i in range(cases)])]
  transfers between devices with their start and end apart: 7 -> 7, of which waited for: 4 -> 5; matrix products, arithmetic and copies ran while one was open for 3% -> 0% of each run, Pallas kernels for 3% -> 6%
where the time goes in v3:
time: 52.8 us; the launch traced here: 52.5 us
  blocking collectives  19.6 us (37%)
  Pallas kernels  13 us (25%)
  starting transfers between devices  11.1 us (21%)
  waiting for transfers between devices  7.27 us (14%)
  between operations  1.49 us (3%)
    all_to_all x2, blocking collectives, commands(): return lax.all_to_all(partial, ('case', 'mod'), 0, 0, tiled=True)  19.6 us
    pallas_call x7, Pallas kernels, call(): pl.pallas_call(kernel, out_shape=outs, in_specs=in_specs, out_specs=out_s...  13 us
    all_to_all x1, starting transfers between devices, body(): lax.all_to_all(angles, 'mod', 0, 0, tiled=True).reshape(count, LANES)  7.25 us
    ppermute x6, starting transfers between devices, commands(): lax.ppermute(signal, 'case', [(i, i ^ j) for i in range(cases)])  3.88 us
    ppermute x6, waiting for transfers between devices, commands(): lax.ppermute(signal, 'case', [(i, i ^ j) for i in range(cases)])  3.79 us
    all_to_all x1, waiting for transfers between devices, body(): lax.all_to_all(angles, 'mod', 0, 0, tiled=True).reshape(count, LANES)  3.48 us
  transfers between devices with their start and end apart: 7, of which 5 were waited for; matrix products, arithmetic and copies ran while one was open for 0% of the time, Pallas kernels for 6%

profile of v3, /device:TPU:0, one launch (start us, length us, event | category | flops | bytes accessed | tf_op | source)
XLA Modules:
  0.0 52.5 jit_solution(4675809714924677550)
XLA Ops:
  0.6 0.0 copy-start
  1.4 0.6 %spread.1 = f32[8,1,128]{2,1,0:T(1,128)} custom-call(s32[1]{0:T(128)S(6)} %copy.13.point_ref), custom_call_target="tpu_custom_call" | custom-call | tf_op jit(solution)/shard_map/modulation_angles/spread/pallas_call | solution.py:328
  2.0 7.3 %all-to-all-start = ((f32[8,1,128]{2,1,0:T(1,128)}), f32[8,1,128]{2,1,0:T(1,128)S(1)}, u32[]{:S(2)}, u32[]{:S(2)}) async-start(f32[8,1,128]{2,1,0:T(1,128)} %spread.1), calls=%async_computation | async-start | bytes 8192 | tf_op jit(solution)/shard_map/modulation_angles/all_to_all | solution.py:360
  9.3 2.9 %prepare.1 = (bf16[256,512]{1,0:T(8,128)(2,1)S(1)}, s32[64,128]{1,0:T(8,128)}, bf16[256,192]{1,0:T(8,128)(2,1)}, bf16[384,256]{1,0:T(8,128)(2,1)}) custom-call(f32[256,256]{1,0:T(8,128)} %bitcast.8, f32[256,256]{1,0:T(8,128)} %amp_hbm.3, s32[40,128]{1,0:T(8,128)} %bitcast.12, f32[64,256]{1,0:T(8,128)} %bitcast.11, f32[80,256]{1,0:T(8,128)} %bitcast.10), custom_call_target="tpu_custom_call" | custom-call | tf_op jit(solution)/shard_map/prepare/pallas_call | solution.py:328
  12.2 3.5 %all-to-all-done = f32[8,1,128]{2,1,0:T(1,128)S(1)} async-done(((f32[8,1,128]{2,1,0:T(1,128)}), f32[8,1,128]{2,1,0:T(1,128)S(1)}, u32[]{:S(2)}, u32[]{:S(2)}) %all-to-all-start) | async-done | bytes 4128 | tf_op jit(solution)/shard_map/modulation_angles/all_to_all | solution.py:360
  15.7 2.5 %first_frame.1 = (f32[8,128]{1,0:T(8,128)S(1)}, bf16[512,512]{1,0:T(8,128)(2,1)}, f32[16,256]{1,0:T(8,128)S(1)}) custom-call(f32[8,128]{1,0:T(8,128)S(1)} %bitcast.7, bf16[256,512]{1,0:T(8,128)(2,1)S(1)} %get-tuple-element.12.field_ref, f32[512,512]{1,0:T(8,128)} %constant.4.clone.rows_hbm, bf16[512,1024]{1,0:T(8,128)(2,1)} %constant.5.clone.full_hbm, ...), custom_call_target="tpu_custom_call" | custom-call | tf_op jit(solution)/shard_map/first_frame/pallas_call | solution.py:328
  18.2 0.1 collective-permute-start.2
  18.2 1.6 %collective-permute-start.1 = (f32[8,128]{1,0:T(8,128)S(1)}, f32[8,128]{1,0:T(8,128)S(1)}, u32[]{:S(2)}, u32[]{:S(2)}) collective-permute-start(f32[8,128]{1,0:T(8,128)S(1)} %get-tuple-element.13.refs_0_), channel_id=1, source_target_pairs={{0,16},{8,24},{16,0},{24,8},{1,17},{9,25},{17,1},{25,9},{2,18},{10... | collective-permute-start | bytes 12296 | tf_op jit(solution)/shard_map/ppermute | solution.py:390
  19.8 0.3 collective-permute-start
  20.1 1.2 %collective-permute-done.2.refs_3_ = f32[8,128]{1,0:T(8,128)S(1)} collective-permute-done((f32[8,128]{1,0:T(8,128)S(1)}, f32[8,128]{1,0:T(8,128)S(1)}, u32[]{:S(2)}, u32[]{:S(2)}) %collective-permute-start.2) | collective-permute-done | bytes 4128 | tf_op jit(solution)/shard_map/ppermute | solution.py:390
  21.3 0.7 %collective-permute-done.1.refs_2_ = f32[8,128]{1,0:T(8,128)S(1)} collective-permute-done((f32[8,128]{1,0:T(8,128)S(1)}, f32[8,128]{1,0:T(8,128)S(1)}, u32[]{:S(2)}, u32[]{:S(2)}) %collective-permute-start.1) | collective-permute-done | bytes 4128 | tf_op jit(solution)/shard_map/ppermute | solution.py:390
  21.9 0.0 collective-permute-done.refs_1_
  21.9 0.0 copy-done
  21.9 0.8 %commands.2 = bf16[32,2,640]{2,1,0:T(2,128)(2,1)S(1)} custom-call(f32[8,128]{1,0:T(8,128)S(1)} %get-tuple-element.13.refs_0_, f32[8,128]{1,0:T(8,128)S(1)} %collective-permute-done.refs_1_, f32[8,128]{1,0:T(8,128)S(1)} %collective-permute-done.1.refs_2_, f32[8,128]{1,0:T(8,128)S(1)} %collective-permute-done.2.refs_3_, bf16[1280,1024]{1,0:T(8,128)(2,1)S(1)} %copy-done), custom_call_target="tpu_custom_call" | custom-call | tf_op jit(solution)/shard_map/commands/pallas_call | solution.py:328
  22.7 9.8 %all_to_all.15.parts_ref = bf16[32,2,640]{2,1,0:T(2,128)(2,1)S(1)} all-to-all(bf16[32,2,640]{2,1,0:T(2,128)(2,1)S(1)} %commands.2), channel_id=1, replica_groups=mesh['case'=4,'mod'=8] {'case','mod'}, dimensions={0} | all-to-all | bytes 163840 | tf_op jit(solution)/shard_map/all_to_all | solution.py:395
  32.5 4.7 %next_frame.1 = (f32[64,512]{1,0:T(8,128)}, f32[8,128]{1,0:T(8,128)S(1)}, f32[4,2,640]{2,1,0:T(2,128)S(1)}) custom-call(bf16[32,2,640]{2,1,0:T(2,128)(2,1)S(1)} %all_to_all.15.parts_ref, f32[16,256]{1,0:T(8,128)S(1)} %get-tuple-element.14.tilt_ref, s32[64,128]{1,0:T(8,128)} %get-tuple-element.15.cells_hbm, bf16[256,192]{1,0:T(8,128)(2,1)} %get-tuple-element.16.gx_hbm, ...), custom_call_target="tpu_custom_call" | custom-call | tf_op jit(solution)/shard_map/next_frame/pallas_call | solution.py:328
  37.3 0.3 collective-permute-start.5
  37.6 1.5 %collective-permute-start.4 = (f32[8,128]{1,0:T(8,128)S(1)}, f32[8,128]{1,0:T(8,128)S(1)}, u32[]{:S(2)}, u32[]{:S(2)}) collective-permute-start(f32[8,128]{1,0:T(8,128)S(1)} %get-tuple-element.19.refs_0_), channel_id=1, source_target_pairs={{0,16},{8,24},{16,0},{24,8},{1,17},{9,25},{17,1},{25,9},{2,18},{10... | collective-permute-start | bytes 12296 | tf_op jit(solution)/shard_map/ppermute | solution.py:390
  39.1 0.1 collective-permute-start.3
  39.2 1.1 %collective-permute-done.5.refs_3_ = f32[8,128]{1,0:T(8,128)S(1)} collective-permute-done((f32[8,128]{1,0:T(8,128)S(1)}, f32[8,128]{1,0:T(8,128)S(1)}, u32[]{:S(2)}, u32[]{:S(2)}) %collective-permute-start.5) | collective-permute-done | bytes 4128 | tf_op jit(solution)/shard_map/ppermute | solution.py:390
  40.4 0.8 %collective-permute-done.4.refs_2_ = f32[8,128]{1,0:T(8,128)S(1)} collective-permute-done((f32[8,128]{1,0:T(8,128)S(1)}, f32[8,128]{1,0:T(8,128)S(1)}, u32[]{:S(2)}, u32[]{:S(2)}) %collective-permute-start.4) | collective-permute-done | bytes 4128 | tf_op jit(solution)/shard_map/ppermute | solution.py:390
  41.2 0.0 collective-permute-done.3.refs_1_
  41.2 0.8 %commands.3 = bf16[32,2,640]{2,1,0:T(2,128)(2,1)S(1)} custom-call(f32[8,128]{1,0:T(8,128)S(1)} %get-tuple-element.19.refs_0_, f32[8,128]{1,0:T(8,128)S(1)} %collective-permute-done.3.refs_1_, f32[8,128]{1,0:T(8,128)S(1)} %collective-permute-done.4.refs_2_, f32[8,128]{1,0:T(8,128)S(1)} %collective-permute-done.5.refs_3_, bf16[1280,1024]{1,0:T(8,128)(2,1)S(1)} %copy-done), custom_call_target="tpu_custom_call" | custom-call | tf_op jit(solution)/shard_map/commands/pallas_call | solution.py:328
  42.0 9.8 %all_to_all.16.parts_ref = bf16[32,2,640]{2,1,0:T(2,128)(2,1)S(1)} all-to-all(bf16[32,2,640]{2,1,0:T(2,128)(2,1)S(1)} %commands.3), channel_id=1, replica_groups=mesh['case'=4,'mod'=8] {'case','mod'}, dimensions={0} | all-to-all | bytes 163840 | tf_op jit(solution)/shard_map/all_to_all | solution.py:395
  51.8 0.7 %total.1 = f32[1,5120]{1,0:T(1,128)} custom-call(bf16[32,2,640]{2,1,0:T(2,128)(2,1)S(1)} %all_to_all.16.parts_ref, f32[4,2,640]{2,1,0:T(2,128)S(1)} %get-tuple-element.20.total_ref), custom_call_target="tpu_custom_call" | custom-call | tf_op jit(solution)/shard_map/total/pallas_call | solution.py:328
Async XLA Ops:
  0.6 21.3 %copy-start = (bf16[1280,1024]{1,0:T(8,128)(2,1)S(1)}, bf16[1280,1024]{1,0:T(8,128)(2,1)}, u32[]{:S(2)}) copy-start(bf16[1280,1024]{1,0:T(8,128)(2,1)} %refs_4_.3) | copy-start | bytes 7864324
  2.0 13.6 %all-to-all-start = ((f32[8,1,128]{2,1,0:T(1,128)}), f32[8,1,128]{2,1,0:T(1,128)S(1)}, u32[]{:S(2)}, u32[]{:S(2)}) async-start(f32[8,1,128]{2,1,0:T(1,128)} %spread.1), calls=%async_computation | async-start | bytes 8192 | tf_op jit(solution)/shard_map/modulation_angles/all_to_all | solution.py:360
  18.2 3.1 %collective-permute-start.2 = (f32[8,128]{1,0:T(8,128)S(1)}, f32[8,128]{1,0:T(8,128)S(1)}, u32[]{:S(2)}, u32[]{:S(2)}) collective-permute-start(f32[8,128]{1,0:T(8,128)S(1)} %get-tuple-element.13.refs_0_), channel_id=1, source_target_pairs={{0,24},{8,16},{16,8},{24,0},{1,25},{9,17},{17,9},{25,1},{2,26},{10... | collective-permute-start | bytes 12296 | tf_op jit(solution)/shard_map/ppermute | solution.py:390
  18.2 3.7 %collective-permute-start.1 = (f32[8,128]{1,0:T(8,128)S(1)}, f32[8,128]{1,0:T(8,128)S(1)}, u32[]{:S(2)}, u32[]{:S(2)}) collective-permute-start(f32[8,128]{1,0:T(8,128)S(1)} %get-tuple-element.13.refs_0_), channel_id=1, source_target_pairs={{0,16},{8,24},{16,0},{24,8},{1,17},{9,25},{17,1},{25,9},{2,18},{10... | collective-permute-start | bytes 12296 | tf_op jit(solution)/shard_map/ppermute | solution.py:390
  19.8 2.1 %collective-permute-start = (f32[8,128]{1,0:T(8,128)S(1)}, f32[8,128]{1,0:T(8,128)S(1)}, u32[]{:S(2)}, u32[]{:S(2)}) collective-permute-start(f32[8,128]{1,0:T(8,128)S(1)} %get-tuple-element.13.refs_0_), channel_id=1, source_target_pairs={{0,8},{8,0},{16,24},{24,16},{1,9},{9,1},{17,25},{25,17},{2,10},{10... | collective-permute-start | bytes 12296 | tf_op jit(solution)/shard_map/ppermute | solution.py:390
  37.3 3.1 %collective-permute-start.5 = (f32[8,128]{1,0:T(8,128)S(1)}, f32[8,128]{1,0:T(8,128)S(1)}, u32[]{:S(2)}, u32[]{:S(2)}) collective-permute-start(f32[8,128]{1,0:T(8,128)S(1)} %get-tuple-element.19.refs_0_), channel_id=1, source_target_pairs={{0,24},{8,16},{16,8},{24,0},{1,25},{9,17},{17,9},{25,1},{2,26},{10... | collective-permute-start | bytes 12296 | tf_op jit(solution)/shard_map/ppermute | solution.py:390
  37.6 3.6 %collective-permute-start.4 = (f32[8,128]{1,0:T(8,128)S(1)}, f32[8,128]{1,0:T(8,128)S(1)}, u32[]{:S(2)}, u32[]{:S(2)}) collective-permute-start(f32[8,128]{1,0:T(8,128)S(1)} %get-tuple-element.19.refs_0_), channel_id=1, source_target_pairs={{0,16},{8,24},{16,0},{24,8},{1,17},{9,25},{17,1},{25,9},{2,18},{10... | collective-permute-start | bytes 12296 | tf_op jit(solution)/shard_map/ppermute | solution.py:390
  39.1 2.1 %collective-permute-start.3 = (f32[8,128]{1,0:T(8,128)S(1)}, f32[8,128]{1,0:T(8,128)S(1)}, u32[]{:S(2)}, u32[]{:S(2)}) collective-permute-start(f32[8,128]{1,0:T(8,128)S(1)} %get-tuple-element.19.refs_0_), channel_id=1, source_target_pairs={{0,8},{8,0},{16,24},{24,16},{1,9},{9,1},{17,25},{25,17},{2,10},{10... | collective-permute-start | bytes 12296 | tf_op jit(solution)/shard_map/ppermute | solution.py:390

commit v4 on v3

--- a/solution.py
+++ b/solution.py
@@ -98,11 +98,17 @@
 
 
 def prepare_kernel(
-    phase_hbm, amp_hbm, map_hbm, gxt_hbm, gyt_hbm, field_ref, cells_hbm, gx_hbm, gy_hbm,
-    phase_ref, amp_ref, map_ref, gxt_ref, gyt_ref, floats, cells_ref, gx_ref, gy_ref, semaphores,
+    phase_hbm, amp_hbm, map_hbm, gxt_hbm, gyt_hbm, rows_hbm, full_hbm,
+    field_ref, rows_ref, full_ref, cells_ref, gx_ref, gy_ref,
+    phase_ref, amp_ref, map_ref, gxt_ref, gyt_ref, floats, semaphores,
 ):
-    phase, amp, actuators, gxt, gyt = copies(
-        [(phase_hbm, phase_ref), (amp_hbm, amp_ref), (map_hbm, map_ref), (gxt_hbm, gxt_ref), (gyt_hbm, gyt_ref)],
+    row_count = rows_ref.shape[0]
+    own_rows = pl.ds(pl.multiple_of(lax.axis_index("mod") * row_count, row_count), row_count)
+    actuators, gxt, gyt, phase, amp, rows, full = copies(
+        [
+            (map_hbm, map_ref), (gxt_hbm, gxt_ref), (gyt_hbm, gyt_ref), (phase_hbm, phase_ref), (amp_hbm, amp_ref),
+            (rows_hbm.at[own_rows], rows_ref), (full_hbm, full_ref),
+        ],
         semaphores,
     )
     actuators.wait()
@@ -114,21 +120,17 @@
     cells_ref[...] = look_up(*runs(floats), cell).astype(jnp.int32)
     gxt.wait()
     high, low = halves(gxt_ref[...].T)
-    gx_ref[...] = jnp.concatenate([high, low, high], 1)
+    gx_ref[...] = jnp.concatenate([high, low], 1)
     gyt.wait()
-    padded = jnp.concatenate(
-        [gyt_ref[...], jnp.zeros((LANES - grid_columns, gyt_ref.shape[1]), jnp.float32)], 0
-    )
-    high, low = halves(padded)
+    high, low = halves(gyt_ref[...])
     gy_ref[...] = jnp.concatenate([high, high, low], 0)
     phase.wait()
+    sine, cosine = sin_cos(phase_ref[...])
     amp.wait()
-    out = copies([(cells_ref, cells_hbm), (gx_ref, gx_hbm), (gy_ref, gy_hbm)], semaphores)
-    sine, cosine = sin_cos(phase_ref[...])
     amplitude = amp_ref[...]
     field_ref[...] = jnp.concatenate([amplitude * cosine, amplitude * sine], 1).astype(jnp.bfloat16)
-    for copy in out:
-        copy.wait()
+    rows.wait()
+    full.wait()
 
 
 def tilt_factors(angles_ref, pupil, length):
@@ -171,32 +173,28 @@
 
 
 def first_kernel(
-    angles_ref, field_ref, rows_hbm, full_hbm, pixels_hbm, signal_ref, left_hbm, tilt_ref,
-    rows_ref, full_ref, pixels_ref, left_ref, frame_ref, semaphores,
+    angles_ref, field_ref, rows_ref, full_ref, pixels_hbm, recon_hbm, signal_ref, left_hbm, tilt_ref, recon_ref,
+    pixels_ref, left_ref, frame_ref, semaphores,
 ):
     row_count, length = frame_ref.shape
     count, pupil = angles_ref.shape[0], length // 2
-    own_rows = pl.ds(pl.multiple_of(lax.axis_index("mod") * row_count, row_count), row_count)
-    rows, full, pixels = copies(
-        [(rows_hbm.at[own_rows], rows_ref), (full_hbm, full_ref), (pixels_hbm, pixels_ref)], semaphores
-    )
+    pixels, recon = copies([(pixels_hbm, pixels_ref), (recon_hbm, recon_ref)], semaphores)
     (s1, c1), (s2, c2) = tilt_factors(angles_ref, pupil, length)
     tilt_ref[:count] = s2
     tilt_ref[count:] = c2
-    rows.wait()
     own = rows_ref[...]
     left = turned(own[None, :, :pupil], own[None, :, pupil:], s1, c1)
     left = left.reshape(left_ref.shape).astype(jnp.bfloat16)
     left_ref[...] = left
-    left_out = pltpu.make_async_copy(left_ref, left_hbm, semaphores.at[0])
+    left_out = pltpu.make_async_copy(left_ref, left_hbm, semaphores.at[2])
     left_out.start()
     field = field_matrix(field_ref[:, :pupil], field_ref[:, pupil:])
     half = first_half(left, field, s2, c2)
-    full.wait()
     frame_ref[...] = second_half(half, full_ref[...], count)
     pixels.wait()
     signal_ref[...] = read_signals(frame_ref, own_pixels(pixels_ref, row_count, length))
     left_out.wait()
+    recon.wait()
 
 
 def add_commands(parts_ref, total_ref, out_ref):
@@ -208,16 +206,15 @@
 
 
 def later_kernel(
-    parts_ref, tilt_ref, cells_hbm, gx_hbm, gy_hbm, phase_hbm, amp_hbm, left_hbm, full_hbm, pixels_hbm, *refs
+    parts_ref, tilt_ref, cells_ref, gx_ref, gy_ref, phase_hbm, amp_hbm, left_hbm, full_hbm, pixels_hbm, *refs
 ):
-    old_total, refs = (None, refs) if len(refs) == 13 else (refs[0], refs[1:])
+    old_total, refs = (None, refs) if len(refs) == 10 else (refs[0], refs[1:])
     frame_hbm, signal_ref, new_total_ref, frame_ref = refs[:4]
-    cells_ref, gx_ref, gy_ref, phase_ref, amp_ref, left_ref, full_ref, pixels_ref = refs[4:12]
-    semaphores = refs[12]
-    cells, gx, gy, phase, amp, left, full, pixels = copies(
+    phase_ref, amp_ref, left_ref, full_ref, pixels_ref, semaphores = refs[4:]
+    phase, amp, left, full, pixels = copies(
         [
-            (cells_hbm, cells_ref), (gx_hbm, gx_ref), (gy_hbm, gy_ref), (phase_hbm, phase_ref), (amp_hbm, amp_ref),
-            (left_hbm, left_ref), (full_hbm, full_ref), (pixels_hbm, pixels_ref),
+            (phase_hbm, phase_ref), (amp_hbm, amp_ref), (left_hbm, left_ref), (full_hbm, full_ref),
+            (pixels_hbm, pixels_ref),
         ],
         semaphores,
     )
@@ -232,15 +229,16 @@
         piece = i // per_piece
         return new_total_ref[piece // pieces, piece % pieces : piece % pieces + 1, column : column + LANES]
 
-    cells.wait()
     grid = look_up(cases * pieces * per_piece, row, cells_ref[...])
     high, low = halves(grid)
-    gx.wait()
+    grid_rows = grid.shape[0]
+    gx_high, gx_low = gx_ref[:, :grid_rows], gx_ref[:, grid_rows:]
     rows_mapped = jnp.dot(
-        gx_ref[...], jnp.concatenate([high, high, low], 0), preferred_element_type=jnp.float32
-    )
-    high, low = halves(rows_mapped)
-    gy.wait()
+        jnp.concatenate([gx_high, gx_low, gx_high], 1),
+        jnp.concatenate([high, high, low], 0),
+        preferred_element_type=jnp.float32,
+    )
+    high, low = halves(rows_mapped[:, : gy_ref.shape[0] // 3])
     surface = jnp.dot(
         jnp.concatenate([high, low, high], 1), gy_ref[...], preferred_element_type=jnp.float32
     )
@@ -359,32 +357,31 @@
         )
         angles = lax.all_to_all(angles, "mod", 0, 0, tiled=True).reshape(count, LANES)
 
-    field, cells, gx_parts, gy_parts = call(
+    field, rows, full, cells, gx_parts, gy_parts = call(
         prepare_kernel,
         "prepare",
         (
             shape((pupil, 2 * pupil), bf16),
+            shape((row_count, 2 * pupil), f32),
+            shape(full_table.shape, bf16),
             shape((grid_rows, LANES), jnp.int32),
-            shape((pupil, 3 * grid_rows), bf16),
-            shape((3 * LANES, pupil), bf16),
+            shape((pupil, 2 * grid_rows), bf16),
+            shape((3 * gy.shape[1], pupil), bf16),
         ),
-        (vmem, hbm, hbm, hbm),
-        [hbm] * 5,
+        (vmem,) * 6,
+        [hbm] * 7,
         like(screen, pupil_amp)
         + [
             pltpu.VMEM((act_map.shape[0] // LANES, LANES), jnp.int32),
             pltpu.VMEM(gx.shape[::-1], f32),
             pltpu.VMEM(gy.shape[::-1], f32),
             pltpu.VMEM((act_map.shape[0] // LANES, LANES), f32),
-            pltpu.VMEM((grid_rows, LANES), jnp.int32),
-            pltpu.VMEM((pupil, 3 * grid_rows), bf16),
-            pltpu.VMEM((3 * LANES, pupil), bf16),
-            done(5),
+            done(7),
         ],
-        screen, pupil_amp, act_map.reshape(-1, LANES), gx.T, gy.T,
-    )
-
-    def commands(signal):
+        screen, pupil_amp, act_map.reshape(-1, LANES), gx.T, gy.T, rows_table, full_table,
+    )
+
+    def commands(signal, recon):
         signals = [signal]
         for j in range(1, cases):
             signals.append(lax.ppermute(signal, "case", [(i, i ^ j) for i in range(cases)]))
@@ -398,29 +395,29 @@
     signal_shape = shape((signal_rows, LANES), f32)
     left_shape = shape((count * row_count, 2 * pupil), bf16)
     total_shape = shape((cases, pieces, block // pieces), f32)
-    signal, left, tilt = call(
+    signal, left, tilt, recon = call(
         first_kernel,
         "first_frame",
-        (signal_shape, left_shape, shape((2 * count, pupil), f32)),
-        (vmem, hbm, vmem),
-        [vmem, vmem, hbm, hbm, hbm],
-        [pltpu.VMEM((row_count, 2 * pupil), f32)] + like(full_table, pixels, left_shape, frame_shape) + [done(3)],
-        angles, field, rows_table, full_table, pixels,
+        (signal_shape, left_shape, shape((2 * count, pupil), f32), shape(recon.shape, bf16)),
+        (vmem, hbm, vmem, vmem),
+        [vmem, vmem, vmem, vmem, hbm, hbm],
+        like(pixels, left_shape, frame_shape) + [done(3)],
+        angles, field, rows, full, pixels, recon,
     )
     totals = ()
     for iteration in range(1, STEPS):
-        parts = commands(signal)
-        held = (cells, gx_parts, gy_parts, screen, pupil_amp, left, full_table, pixels)
+        parts = commands(signal, recon)
+        held = (screen, pupil_amp, left, full_table, pixels)
         frame, signal, *totals = call(
             later_kernel,
             "next_frame",
             (frame_shape, signal_shape, total_shape),
             (hbm, vmem, vmem),
-            [vmem, vmem] + [hbm] * len(held) + [vmem] * len(totals),
+            [vmem] * 5 + [hbm] * len(held) + [vmem] * len(totals),
             like(frame_shape, *held) + [done(len(held))],
-            parts, tilt, *held, *totals,
+            parts, tilt, cells, gx_parts, gy_parts, *held, *totals,
         )
-    parts = commands(signal)
+    parts = commands(signal, recon)
     command_total = call(
         last_kernel, "total", shape((1, cases * block), f32), vmem, [vmem, vmem], like(total_shape), parts, *totals
     )

time: 52.8 us -> 52.1 us (0.987)
  transfers between devices with their start and end apart: 7 -> 7, of which waited for: 5 -> 5; matrix products, arithmetic and copies ran while one was open for 0% -> 0% of each run, Pallas kernels for 6% -> 5%
where the time goes in v4:
time: 52.1 us; the launch traced here: 51.9 us
  blocking collectives  19.3 us (37%)
  Pallas kernels  12.5 us (24%)
  starting transfers between devices  11.1 us (21%)
  waiting for transfers between devices  7.61 us (15%)
  between operations  1.33 us (3%)
    all_to_all x2, blocking collectives, commands(): return lax.all_to_all(partial, ('case', 'mod'), 0, 0, tiled=True)  19.3 us
    pallas_call x7, Pallas kernels, call(): pl.pallas_call(kernel, out_shape=outs, in_specs=in_specs, out_specs=out_s...  12.5 us
    all_to_all x1, starting transfers between devices, body(): lax.all_to_all(angles, 'mod', 0, 0, tiled=True).reshape(count, LANES)  7.25 us
    ppermute x6, starting transfers between devices, commands(): lax.ppermute(signal, 'case', [(i, i ^ j) for i in range(cases)])  3.88 us
    all_to_all x1, waiting for transfers between devices, body(): lax.all_to_all(angles, 'mod', 0, 0, tiled=True).reshape(count, LANES)  3.82 us
    ppermute x6, waiting for transfers between devices, commands(): lax.ppermute(signal, 'case', [(i, i ^ j) for i in range(cases)])  3.79 us
  transfers between devices with their start and end apart: 7, of which 5 were waited for; matrix products, arithmetic and copies ran while one was open for 0% of the time, Pallas kernels for 5%

profile of v4, /device:TPU:0, one launch (start us, length us, event | category | flops | bytes accessed | tf_op | source)
XLA Modules:
  0.0 51.9 jit_solution(7781315429720986006)
XLA Ops:
  1.3 0.6 %spread.1 = f32[8,1,128]{2,1,0:T(1,128)} custom-call(s32[1]{0:T(128)S(6)} %copy.13.point_ref), custom_call_target="tpu_custom_call" | custom-call | tf_op jit(solution)/shard_map/modulation_angles/spread/pallas_call | solution.py:326
  1.9 7.3 %all-to-all-start = ((f32[8,1,128]{2,1,0:T(1,128)}), f32[8,1,128]{2,1,0:T(1,128)S(1)}, u32[]{:S(2)}, u32[]{:S(2)}) async-start(f32[8,1,128]{2,1,0:T(1,128)} %spread.1), calls=%async_computation | async-start | bytes 8192 | tf_op jit(solution)/shard_map/modulation_angles/all_to_all | solution.py:358
  9.1 2.6 %prepare.1 = (bf16[256,512]{1,0:T(8,128)(2,1)S(1)}, f32[64,512]{1,0:T(8,128)S(1)}, bf16[512,1024]{1,0:T(8,128)(2,1)S(1)}, s32[64,128]{1,0:T(8,128)S(1)}, bf16[25...) custom-call(f32[256,256]{1,0:T(8,128)} %bitcast.8, f32[256,256]{1,0:T(8,128)} %amp_hbm.3, s32[40,128]{1,0:T(8,128)} %bitcast.12, ...), custom_call_target="tpu_custom_call" | custom-call | tf_op jit(solution)/shard_map/prepare/pallas_call | solution.py:326
  11.7 3.8 %all-to-all-done = f32[8,1,128]{2,1,0:T(1,128)S(1)} async-done(((f32[8,1,128]{2,1,0:T(1,128)}), f32[8,1,128]{2,1,0:T(1,128)S(1)}, u32[]{:S(2)}, u32[]{:S(2)}) %all-to-all-start) | async-done | bytes 4128 | tf_op jit(solution)/shard_map/modulation_angles/all_to_all | solution.py:358
  15.5 2.7 %first_frame.1 = (f32[8,128]{1,0:T(8,128)S(1)}, bf16[512,512]{1,0:T(8,128)(2,1)}, f32[16,256]{1,0:T(8,128)S(1)}, bf16[1280,1024]{1,0:T(8,128)(2,1)S(1)}) custom-call(f32[8,128]{1,0:T(8,128)S(1)} %bitcast.7, bf16[256,512]{1,0:T(8,128)(2,1)S(1)} %get-tuple-element.15.field_ref, f32[64,512]{1,0:T(8,128)S(1)} %get-tuple-element.16.rows_ref, ...), custom_call_target="tpu_custom_call" | custom-call | tf_op jit(solution)/shard_map/first_frame/pallas_call | solution.py:326
  18.2 0.1 collective-permute-start.2
  18.3 1.6 %collective-permute-start.1 = (f32[8,128]{1,0:T(8,128)S(1)}, f32[8,128]{1,0:T(8,128)S(1)}, u32[]{:S(2)}, u32[]{:S(2)}) collective-permute-start(f32[8,128]{1,0:T(8,128)S(1)} %get-tuple-element.18.refs_0_), channel_id=1, source_target_pairs={{0,16},{8,24},{16,0},{24,8},{1,17},{9,25},{17,1},{25,9},{2,18},{10... | collective-permute-start | bytes 12296 | tf_op jit(solution)/shard_map/ppermute | solution.py:387
  19.9 0.3 collective-permute-start
  20.1 1.2 %collective-permute-done.2.refs_3_ = f32[8,128]{1,0:T(8,128)S(1)} collective-permute-done((f32[8,128]{1,0:T(8,128)S(1)}, f32[8,128]{1,0:T(8,128)S(1)}, u32[]{:S(2)}, u32[]{:S(2)}) %collective-permute-start.2) | collective-permute-done | bytes 4128 | tf_op jit(solution)/shard_map/ppermute | solution.py:387
  21.3 0.7 %collective-permute-done.1.refs_2_ = f32[8,128]{1,0:T(8,128)S(1)} collective-permute-done((f32[8,128]{1,0:T(8,128)S(1)}, f32[8,128]{1,0:T(8,128)S(1)}, u32[]{:S(2)}, u32[]{:S(2)}) %collective-permute-start.1) | collective-permute-done | bytes 4128 | tf_op jit(solution)/shard_map/ppermute | solution.py:387
  21.9 0.0 collective-permute-done.refs_1_
  22.0 0.8 %commands.2 = bf16[32,2,640]{2,1,0:T(2,128)(2,1)S(1)} custom-call(f32[8,128]{1,0:T(8,128)S(1)} %get-tuple-element.18.refs_0_, f32[8,128]{1,0:T(8,128)S(1)} %collective-permute-done.refs_1_, f32[8,128]{1,0:T(8,128)S(1)} %collective-permute-done.1.refs_2_, f32[8,128]{1,0:T(8,128)S(1)} %collective-permute-done.2.refs_3_, ...), custom_call_target="tpu_custom_call" | custom-call | tf_op jit(solution)/shard_map/commands/pallas_call | solution.py:326
  22.8 9.5 %all_to_all.15.parts_ref = bf16[32,2,640]{2,1,0:T(2,128)(2,1)S(1)} all-to-all(bf16[32,2,640]{2,1,0:T(2,128)(2,1)S(1)} %commands.2), channel_id=1, replica_groups=mesh['case'=4,'mod'=8] {'case','mod'}, dimensions={0} | all-to-all | bytes 163840 | tf_op jit(solution)/shard_map/all_to_all | solution.py:392
  32.3 4.4 %next_frame.1 = (f32[64,512]{1,0:T(8,128)}, f32[8,128]{1,0:T(8,128)S(1)}, f32[4,2,640]{2,1,0:T(2,128)S(1)}) custom-call(bf16[32,2,640]{2,1,0:T(2,128)(2,1)S(1)} %all_to_all.15.parts_ref, f32[16,256]{1,0:T(8,128)S(1)} %get-tuple-element.20.tilt_ref, s32[64,128]{1,0:T(8,128)S(1)} %get-tuple-element.21.cells_ref, ...), custom_call_target="tpu_custom_call" | custom-call | tf_op jit(solution)/shard_map/next_frame/pallas_call | solution.py:326
  36.6 0.3 collective-permute-start.5
  37.0 1.5 %collective-permute-start.4 = (f32[8,128]{1,0:T(8,128)S(1)}, f32[8,128]{1,0:T(8,128)S(1)}, u32[]{:S(2)}, u32[]{:S(2)}) collective-permute-start(f32[8,128]{1,0:T(8,128)S(1)} %get-tuple-element.25.refs_0_), channel_id=1, source_target_pairs={{0,16},{8,24},{16,0},{24,8},{1,17},{9,25},{17,1},{25,9},{2,18},{10... | collective-permute-start | bytes 12296 | tf_op jit(solution)/shard_map/ppermute | solution.py:387
  38.4 0.1 collective-permute-start.3
  38.6 1.1 %collective-permute-done.5.refs_3_ = f32[8,128]{1,0:T(8,128)S(1)} collective-permute-done((f32[8,128]{1,0:T(8,128)S(1)}, f32[8,128]{1,0:T(8,128)S(1)}, u32[]{:S(2)}, u32[]{:S(2)}) %collective-permute-start.5) | collective-permute-done | bytes 4128 | tf_op jit(solution)/shard_map/ppermute | solution.py:387
  39.7 0.8 %collective-permute-done.4.refs_2_ = f32[8,128]{1,0:T(8,128)S(1)} collective-permute-done((f32[8,128]{1,0:T(8,128)S(1)}, f32[8,128]{1,0:T(8,128)S(1)}, u32[]{:S(2)}, u32[]{:S(2)}) %collective-permute-start.4) | collective-permute-done | bytes 4128 | tf_op jit(solution)/shard_map/ppermute | solution.py:387
  40.6 0.0 collective-permute-done.3.refs_1_
  40.6 0.8 %commands.3 = bf16[32,2,640]{2,1,0:T(2,128)(2,1)S(1)} custom-call(f32[8,128]{1,0:T(8,128)S(1)} %get-tuple-element.25.refs_0_, f32[8,128]{1,0:T(8,128)S(1)} %collective-permute-done.3.refs_1_, f32[8,128]{1,0:T(8,128)S(1)} %collective-permute-done.4.refs_2_, f32[8,128]{1,0:T(8,128)S(1)} %collective-permute-done.5.refs_3_, ...), custom_call_target="tpu_custom_call" | custom-call | tf_op jit(solution)/shard_map/commands/pallas_call | solution.py:326
  41.4 9.8 %all_to_all.16.parts_ref = bf16[32,2,640]{2,1,0:T(2,128)(2,1)S(1)} all-to-all(bf16[32,2,640]{2,1,0:T(2,128)(2,1)S(1)} %commands.3), channel_id=1, replica_groups=mesh['case'=4,'mod'=8] {'case','mod'}, dimensions={0} | all-to-all | bytes 163840 | tf_op jit(solution)/shard_map/all_to_all | solution.py:392
  51.2 0.7 %total.1 = f32[1,5120]{1,0:T(1,128)} custom-call(bf16[32,2,640]{2,1,0:T(2,128)(2,1)S(1)} %all_to_all.16.parts_ref, f32[4,2,640]{2,1,0:T(2,128)S(1)} %get-tuple-element.26.total_ref), custom_call_target="tpu_custom_call" | custom-call | tf_op jit(solution)/shard_map/total/pallas_call | solution.py:326
Async XLA Ops:
  1.9 13.6 %all-to-all-start = ((f32[8,1,128]{2,1,0:T(1,128)}), f32[8,1,128]{2,1,0:T(1,128)S(1)}, u32[]{:S(2)}, u32[]{:S(2)}) async-start(f32[8,1,128]{2,1,0:T(1,128)} %spread.1), calls=%async_computation | async-start | bytes 8192 | tf_op jit(solution)/shard_map/modulation_angles/all_to_all | solution.py:358
  18.2 3.1 %collective-permute-start.2 = (f32[8,128]{1,0:T(8,128)S(1)}, f32[8,128]{1,0:T(8,128)S(1)}, u32[]{:S(2)}, u32[]{:S(2)}) collective-permute-start(f32[8,128]{1,0:T(8,128)S(1)} %get-tuple-element.18.refs_0_), channel_id=1, source_target_pairs={{0,24},{8,16},{16,8},{24,0},{1,25},{9,17},{17,9},{25,1},{2,26},{10... | collective-permute-start | bytes 12296 | tf_op jit(solution)/shard_map/ppermute | solution.py:387
  18.3 3.7 %collective-permute-start.1 = (f32[8,128]{1,0:T(8,128)S(1)}, f32[8,128]{1,0:T(8,128)S(1)}, u32[]{:S(2)}, u32[]{:S(2)}) collective-permute-start(f32[8,128]{1,0:T(8,128)S(1)} %get-tuple-element.18.refs_0_), channel_id=1, source_target_pairs={{0,16},{8,24},{16,0},{24,8},{1,17},{9,25},{17,1},{25,9},{2,18},{10... | collective-permute-start | bytes 12296 | tf_op jit(solution)/shard_map/ppermute | solution.py:387
  19.9 2.1 %collective-permute-start = (f32[8,128]{1,0:T(8,128)S(1)}, f32[8,128]{1,0:T(8,128)S(1)}, u32[]{:S(2)}, u32[]{:S(2)}) collective-permute-start(f32[8,128]{1,0:T(8,128)S(1)} %get-tuple-element.18.refs_0_), channel_id=1, source_target_pairs={{0,8},{8,0},{16,24},{24,16},{1,9},{9,1},{17,25},{25,17},{2,10},{10... | collective-permute-start | bytes 12296 | tf_op jit(solution)/shard_map/ppermute | solution.py:387
  36.6 3.1 %collective-permute-start.5 = (f32[8,128]{1,0:T(8,128)S(1)}, f32[8,128]{1,0:T(8,128)S(1)}, u32[]{:S(2)}, u32[]{:S(2)}) collective-permute-start(f32[8,128]{1,0:T(8,128)S(1)} %get-tuple-element.25.refs_0_), channel_id=1, source_target_pairs={{0,24},{8,16},{16,8},{24,0},{1,25},{9,17},{17,9},{25,1},{2,26},{10... | collective-permute-start | bytes 12296 | tf_op jit(solution)/shard_map/ppermute | solution.py:387
  37.0 3.6 %collective-permute-start.4 = (f32[8,128]{1,0:T(8,128)S(1)}, f32[8,128]{1,0:T(8,128)S(1)}, u32[]{:S(2)}, u32[]{:S(2)}) collective-permute-start(f32[8,128]{1,0:T(8,128)S(1)} %get-tuple-element.25.refs_0_), channel_id=1, source_target_pairs={{0,16},{8,24},{16,0},{24,8},{1,17},{9,25},{17,1},{25,9},{2,18},{10... | collective-permute-start | bytes 12296 | tf_op jit(solution)/shard_map/ppermute | solution.py:387
  38.4 2.1 %collective-permute-start.3 = (f32[8,128]{1,0:T(8,128)S(1)}, f32[8,128]{1,0:T(8,128)S(1)}, u32[]{:S(2)}, u32[]{:S(2)}) collective-permute-start(f32[8,128]{1,0:T(8,128)S(1)} %get-tuple-element.25.refs_0_), channel_id=1, source_target_pairs={{0,8},{8,0},{16,24},{24,16},{1,9},{9,1},{17,25},{25,17},{2,10},{10... | collective-permute-start | bytes 12296 | tf_op jit(solution)/shard_map/ppermute | solution.py:387

commit v5 on v4

v5 whole, which is shorter than its diff:
```python
import functools
import math

import jax
import jax.numpy as jnp
import numpy as np
from jax import lax
from jax.experimental import pallas as pl
from jax.experimental.pallas import tpu as pltpu
from jax.sharding import PartitionSpec as P

STEPS = 2


loop_gain = 0.5
radius_pixels = 6.0
point_count = 256
LANES = 128
VMEM_LIMIT = 16 * 1024 * 1024


def rounded_table(angle, length, sign):
    scale = 1.0 / math.sqrt(length)
    real = (np.cos(angle) * scale).astype(np.float32).astype(jnp.bfloat16).astype(np.float64)
    imag = (sign * np.sin(angle) * scale).astype(np.float32).astype(jnp.bfloat16).astype(np.float64)
    return real + 1j * imag


def pyramid_table(pupil_size, length):
    centred = np.arange(length) - length // 2
    forward = np.mod(centred[:, None] * np.arange(pupil_size)[None, :], length) * (2.0 * math.pi / length)
    inverse = np.mod(np.arange(length)[:, None] * centred[None, :], length) * (2.0 * math.pi / length)
    mask = np.array([1, 1j, -1, -1j])[np.abs(centred) % 4]
    return rounded_table(inverse, length, 1.0) @ (mask[:, None] * rounded_table(forward, length, -1.0))


def half_angle(angle):
    turns = angle * (0.5 / math.pi)
    rest = turns - jnp.floor(turns + 0.5)
    square = rest * rest
    sine = rest * polynomial(square, (4.442867756, -7.307443618, 3.594788074, -0.784373999))
    cosine = polynomial(square, (1.414213538, -6.978850841, 5.739460945, -1.883563042, 0.310698181))
    return sine, cosine


def sin_cos(angle):
    sine, cosine = half_angle(angle)
    return sine * cosine, 1.0 - sine * sine


def field_parts(phase, amplitude):
    sine, cosine = half_angle(phase)
    lead = amplitude * sine
    return (amplitude - lead * sine).astype(jnp.bfloat16), (lead * cosine).astype(jnp.bfloat16)


def polynomial(x, coefficients):
    value = coefficients[-1]
    for coefficient in coefficients[-2::-1]:
        value = value * x + coefficient
    return value


def field_matrix(real, imag):
    return jnp.concatenate([jnp.concatenate([real, imag], 1), jnp.concatenate([-imag, real], 1)], 0)


def halves(values):
    high = values.astype(jnp.bfloat16)
    low = (values - high.astype(jnp.float32)).astype(jnp.bfloat16)
    return high, low


def look_up(count, row, index):
    blocks = []
    for start in range(0, index.shape[0], 8):
        block = index[start : start + 8]
        high = block >> 7
        low = block & (LANES - 1)
        sums = [jnp.zeros(block.shape, jnp.float32) for _ in range(2)]
        for i in range(count):
            spread = jnp.broadcast_to(row(i), block.shape)
            picked = jnp.take_along_axis(spread, low, axis=1, mode="promise_in_bounds")
            sums[i % 2] = jnp.where(high == i, picked, sums[i % 2])
        blocks.append(sums[0] + sums[1])
    return jnp.concatenate(blocks, 0) if len(blocks) > 1 else blocks[0]


def runs(ref):
    per_row = ref.shape[1] // LANES

    def row(i):
        column = (i % per_row) * LANES
        return ref[i // per_row : i // per_row + 1, column : column + LANES]

    return ref.shape[0] * per_row, row


def copies(pairs, semaphores):
    started = [pltpu.make_async_copy(*pair, semaphores.at[i]) for i, pair in enumerate(pairs)]
    for copy in started:
        copy.start()
    return started


def own_rows(rows_hbm, row_count):
    start = pl.multiple_of(lax.axis_index("mod") * row_count, row_count)
    return rows_hbm.at[pl.ds(start, row_count)]


def spread_kernel(point_ref, angles_ref):
    angle = point_ref[0].astype(jnp.float32) * (2.0 * math.pi / point_count)
    angles_ref[...] = jnp.full(angles_ref.shape, angle, jnp.float32)


def prepare_kernel(
    phase_hbm, amp_hbm, map_hbm, gxt_hbm, gyt_hbm, rows_hbm, full_hbm, recon_hbm,
    field_ref, rows_ref, full_ref, cells_ref, gx_ref, gy_ref, recon_ref,
    phase_ref, amp_ref, map_ref, gxt_ref, gyt_ref, floats, semaphores,
):
    actuators, gxt, gyt, phase, amp, rows, full, recon = copies(
        [
            (map_hbm, map_ref), (gxt_hbm, gxt_ref), (gyt_hbm, gyt_ref), (phase_hbm, phase_ref), (amp_hbm, amp_ref),
            (own_rows(rows_hbm, rows_ref.shape[0]), rows_ref), (full_hbm, full_ref),
            (recon_hbm.at[: recon_ref.shape[0]], recon_ref),
        ],
        semaphores,
    )
    grid_rows, grid_columns = gxt_ref.shape[0], gyt_ref.shape[0]
    packed = cells_ref.shape[0]
    actuators.wait()
    floats[...] = map_ref[...].astype(jnp.float32)
    lane = lax.broadcasted_iota(jnp.int32, cells_ref.shape, 1)
    cell = (lane % grid_rows) * grid_columns + (lane // grid_rows) * packed
    cell = cell + lax.broadcasted_iota(jnp.int32, cells_ref.shape, 0)
    cells_ref[...] = look_up(*runs(floats), cell).astype(jnp.int32)
    gxt.wait()
    high, low = halves(gxt_ref[...].T)
    gx_ref[...] = jnp.concatenate([high, low, high, jnp.zeros_like(high)], 1)
    gyt.wait()
    high, low = halves(gyt_ref[...].T)
    gy_ref[...] = jnp.concatenate([high, low, high], 1)
    phase.wait()
    amp.wait()
    field_ref[...] = jnp.concatenate(field_parts(phase_ref[...], amp_ref[...]), 1)
    rows.wait()
    full.wait()
    recon.wait()


def mirror_surface(grid, gx_ref, gy_ref):
    f32 = jnp.float32
    lanes_used = gx_ref.shape[1] // 4
    if lanes_used == LANES:
        spread = [grid]
    else:
        lane = lax.broadcasted_iota(jnp.int32, grid.shape, 1)
        other = pltpu.roll(grid, lanes_used, 1)
        spread = [jnp.where(lane < lanes_used, grid, other), jnp.where(lane < lanes_used, other, grid)]
    transposed = jnp.concatenate(spread, 0)
    high = transposed.astype(jnp.bfloat16).astype(f32)
    parts = jnp.concatenate([high, high, transposed - high], 0).astype(jnp.bfloat16)
    high, low = halves(jnp.dot(gy_ref[...], parts, preferred_element_type=f32))
    return lax.dot_general(
        gx_ref[...], jnp.concatenate([high, low], 1), (((1,), (1,)), ((), ())), preferred_element_type=f32
    )


def tilt_factors(angles_ref, pupil, length):
    sin_a, cos_a = sin_cos(angles_ref[...])
    spread = pupil // LANES
    sin_a = jnp.concatenate([sin_a] * spread, 1)
    cos_a = jnp.concatenate([cos_a] * spread, 1)
    place = (lax.broadcasted_iota(jnp.int32, sin_a.shape, 1) - pupil // 2).astype(jnp.float32)
    place = place * (2.0 * math.pi * radius_pixels / length)
    return sin_cos(place * cos_a) + sin_cos(place * sin_a)


def turned(real, imag, sine, cosine):
    sine, cosine = sine[:, None, :], cosine[:, None, :]
    return real * cosine - imag * sine, real * sine + imag * cosine


def left_rows(rows, sine, cosine):
    count, pupil = sine.shape
    left = jnp.concatenate(turned(rows[None, :, :pupil], rows[None, :, pupil:], sine, cosine), 2)
    return left.reshape(count * rows.shape[0], 2 * pupil).astype(jnp.bfloat16)


def half_way(left, field, sine, cosine):
    count, pupil = sine.shape
    rows = left.shape[0]
    half = jnp.dot(left, field, preferred_element_type=jnp.float32)
    half = half.reshape(count, rows // count, 2 * pupil)
    real, imag = turned(half[:, :, :pupil], half[:, :, pupil:], sine, cosine)
    real = real.reshape(rows, pupil).astype(jnp.bfloat16)
    imag = imag.reshape(rows, pupil).astype(jnp.bfloat16)
    return jnp.concatenate([jnp.concatenate([real, -imag], 1), jnp.concatenate([imag, real], 1)], 0)


def detector_part(both, table, count):
    detector = jnp.dot(both, table, preferred_element_type=jnp.float32)
    squares = (detector * detector).reshape(2 * count, both.shape[0] // (2 * count), detector.shape[1])
    return jnp.sum(squares, 0) * (1.0 / count)


def detect(both, full_ref, pixels_ref, frame_ref, count):
    row_count, length = frame_ref.shape
    pixels = pixels_ref[...] - lax.axis_index("mod") * (row_count * length)
    high, low = pixels >> 7, pixels & (LANES - 1)
    per_row = length // LANES
    total = jnp.zeros(pixels.shape, jnp.float32)
    step = length // 2
    for start in range(0, length, step):
        columns = pl.ds(start, step)
        frame_ref[:, columns] = detector_part(both, full_ref[:, columns], count)
        for i in range(row_count):
            for j in range(start // LANES, (start + step) // LANES):
                spread = jnp.broadcast_to(frame_ref[i : i + 1, j * LANES : (j + 1) * LANES], pixels.shape)
                picked = jnp.take_along_axis(spread, low, axis=1, mode="promise_in_bounds")
                total = jnp.where(high == i * per_row + j, picked, total)
    return total.astype(jnp.bfloat16).astype(jnp.float32)


def first_kernel(
    angles_ref, field_ref, rows_ref, full_ref, pixels_hbm, recon_hbm, signal_ref, tilt_ref, left_ref, recon_ref,
    pixels_ref, frame_ref, semaphores,
):
    length = frame_ref.shape[1]
    pupil = length // 2
    pixels, recon = copies(
        [(pixels_hbm, pixels_ref), (recon_hbm.at[recon_hbm.shape[0] - recon_ref.shape[0] :], recon_ref)], semaphores
    )
    tilts = tilt_factors(angles_ref, pupil, length)
    tilt_ref[0], tilt_ref[1] = tilts[2:]
    left = left_rows(rows_ref[...], *tilts[:2])
    left_ref[...] = left
    field = field_matrix(field_ref[:, :pupil], field_ref[:, pupil:])
    both = half_way(left, field, *tilts[2:])
    pixels.wait()
    signal_ref[...] = detect(both, full_ref, pixels_ref, frame_ref, angles_ref.shape[0])
    recon.wait()


def add_commands(parts_ref, total_ref, out_ref):
    cases = out_ref.shape[0]
    each = parts_ref.shape[0] // cases
    for case in range(cases):
        sums = jnp.sum(parts_ref[case * each : (case + 1) * each].astype(jnp.float32), 0)
        out_ref[case] = loop_gain * sums if total_ref is None else total_ref[case] + loop_gain * sums


def later_kernel(
    parts_ref, tilt_ref, cells_ref, gx_ref, gy_ref, left_ref, full_ref, phase_hbm, amp_hbm, pixels_hbm, recon_hbm,
    *refs
):
    old_total, refs = (None, refs) if len(refs) == 8 else (refs[0], refs[1:])
    frame_ref, signal_ref, new_total_ref, recon_ref, phase_ref, amp_ref, pixels_ref, semaphores = refs
    phase, amp, pixels, recon = copies(
        [
            (phase_hbm, phase_ref), (amp_hbm, amp_ref), (pixels_hbm, pixels_ref),
            (recon_hbm.at[recon_hbm.shape[0] - recon_ref.shape[0] :], recon_ref),
        ],
        semaphores,
    )
    add_commands(parts_ref, old_total, new_total_ref)
    cases, pieces, width = new_total_ref.shape
    per_piece = width // LANES

    def row(i):
        column = (i % per_piece) * LANES
        piece = i // per_piece
        return new_total_ref[piece // pieces, piece % pieces : piece % pieces + 1, column : column + LANES]

    grid = look_up(cases * pieces * per_piece, row, cells_ref[...])
    surface = mirror_surface(grid, gx_ref, gy_ref)
    phase.wait()
    amp.wait()
    field = field_matrix(*field_parts(phase_ref[...] - surface, amp_ref[...]))

    both = half_way(left_ref[...], field, tilt_ref[0], tilt_ref[1])
    pixels.wait()
    signal_ref[...] = detect(both, full_ref, pixels_ref, frame_ref, tilt_ref.shape[1])
    recon.wait()


def command_kernel(cases, *refs):
    signal_refs, recon_refs, refs = refs[:cases], refs[cases : cases + 2], refs[cases + 2 :]
    out_ref = refs[0] if len(refs) == 1 else refs[1]
    frame_out = None if len(refs) == 1 else copies([(refs[0], refs[2])], refs[3])[0]
    own_case = lax.axis_index("case")
    received = [ref[...] for ref in signal_refs]
    ordered = []
    for case in range(cases):
        values = received[0]
        for j in range(1, cases):
            values = jnp.where((own_case ^ j) == case, received[j], values)
        ordered.append(values)
    groups = received[0].shape[0]
    signals = jnp.concatenate(
        [jnp.concatenate([values[g : g + 1] for values in ordered], 0) for g in range(groups)], 1
    ).astype(jnp.bfloat16)
    partial = jnp.concatenate(
        [
            lax.dot_general(signals, ref[...], (((1,), (1,)), ((), ())), preferred_element_type=jnp.float32)
            for ref in recon_refs
        ],
        1,
    )
    messages, pieces, width = out_ref.shape
    copies_each = messages // cases
    for case in range(cases):
        message = jnp.concatenate(
            [partial[case : case + 1, i * width : (i + 1) * width] for i in range(pieces)], 0
        ).astype(jnp.bfloat16)
        for i in range(copies_each):
            out_ref[case * copies_each + i] = message
    if frame_out is not None:
        frame_out.wait()


def last_kernel(parts_ref, total_ref, out_ref, sums_ref):
    add_commands(parts_ref, total_ref, sums_ref)
    cases, pieces, width = sums_ref.shape
    for case in range(cases):
        for i in range(pieces):
            start = (case * pieces + i) * width
            out_ref[:, start : start + width] = sums_ref[case, i : i + 1, :]


def body(turbulence, pupil_amp, mod_points, valid_pix, recon, gx, gy, act_map):
    pupil = pupil_amp.shape[0]
    length = 2 * pupil
    cases = lax.axis_size("case")
    devices_mod = lax.axis_size("mod")
    count = devices_mod * mod_points.shape[0]
    row_count = length // devices_mod
    block = recon.shape[0]
    pieces = 2
    width = block // pieces
    signal_rows = valid_pix.shape[0] // LANES
    grid_rows, grid_columns = gx.shape[1], gy.shape[1]
    packed = grid_columns * grid_rows // LANES
    screen = turbulence[0]
    pixels = valid_pix.reshape(signal_rows, LANES)
    f32, bf16 = jnp.float32, jnp.bfloat16
    shape = jax.ShapeDtypeStruct
    hbm = pl.BlockSpec(memory_space=pltpu.HBM)
    vmem = pl.BlockSpec(memory_space=pltpu.VMEM)
    smem = pl.BlockSpec(memory_space=pltpu.SMEM)

    def call(kernel, name, outs, out_specs, in_specs, scratch, *operands):
        operands = [
            pltpu.with_memory_space_constraint(operand, pltpu.HBM) if spec is hbm else operand
            for operand, spec in zip(operands, in_specs)
        ]
        if isinstance(outs, tuple):
            outs = tuple(
                pltpu.HBM(out.shape, out.dtype) if spec is hbm else out for out, spec in zip(outs, out_specs)
            )
        return pl.pallas_call(
            kernel,
            out_shape=outs,
            in_specs=in_specs,
            out_specs=out_specs,
            scratch_shapes=scratch,
            compiler_params=pltpu.CompilerParams(vmem_limit_bytes=VMEM_LIMIT),
            name=name,
        )(*operands)

    def like(*arrays):
        return [pltpu.VMEM(array.shape, array.dtype) for array in arrays]

    def done(count):
        return pltpu.SemaphoreType.DMA((count,))

    table = pyramid_table(pupil, length)
    rows_table = jnp.asarray(np.concatenate([table.real, table.imag], 1).astype(np.float32))
    full_table = jnp.asarray(np.concatenate([table.real.T, table.imag.T], 0).astype(jnp.bfloat16))

    with jax.named_scope("modulation_angles"):
        angles = call(
            spread_kernel, "spread", shape((devices_mod, 1, LANES), f32), vmem, [smem], [], mod_points
        )
        angles = lax.all_to_all(angles, "mod", 0, 0, tiled=True).reshape(count, LANES)

    recon_early = block // LANES * 6 // 10 * LANES
    late_shape = shape((block - recon_early, recon.shape[1]), bf16)
    map_shape = (act_map.shape[0] // LANES, LANES)
    field, rows, full, cells, gx_parts, gy_parts, recon_first = call(
        prepare_kernel,
        "prepare",
        (
            shape((pupil, 2 * pupil), bf16),
            shape((row_count, 2 * pupil), f32),
            shape(full_table.shape, bf16),
            shape((packed, LANES), jnp.int32),
            shape((pupil, 4 * grid_rows), bf16),
            shape((pupil, 3 * grid_columns), bf16),
            shape((recon_early, recon.shape[1]), bf16),
        ),
        (vmem,) * 7,
        [hbm] * 8,
        like(screen, pupil_amp)
        + [
            pltpu.VMEM(map_shape, jnp.int32),
            pltpu.VMEM(gx.shape[::-1], f32),
            pltpu.VMEM(gy.shape[::-1], f32),
            pltpu.VMEM(map_shape, f32),
            done(8),
        ],
        screen, pupil_amp, act_map.reshape(map_shape), gx.T, gy.T, rows_table, full_table, recon,
    )

    def commands(signal, recon_late, frame=None):
        signals = [signal]
        for j in range(1, cases):
            signals.append(lax.ppermute(signal, "case", [(i, i ^ j) for i in range(cases)]))
        messages = shape((cases * devices_mod, pieces, width), bf16)
        kernel = functools.partial(command_kernel, cases)
        operands = (*signals, recon_first, recon_late)
        if frame is None:
            partial = call(kernel, "commands", messages, vmem, [vmem] * (cases + 2), [], *operands)
            return lax.all_to_all(partial, ("case", "mod"), 0, 0, tiled=True)
        partial, frame = call(
            kernel, "last_commands", (messages, frame), (vmem, hbm), [vmem] * (cases + 3), [done(1)], *operands, frame
        )
        return lax.all_to_all(partial, ("case", "mod"), 0, 0, tiled=True), frame

    frame_shape = shape((row_count, length), f32)
    signal_shape = shape((signal_rows, LANES), f32)
    total_shape = shape((cases, pieces, width), f32)
    left_shape = shape((count * row_count, 2 * pupil), bf16)
    signal, tilts, left, recon_late = call(
        first_kernel,
        "first_frame",
        (signal_shape, shape((2, count, pupil), f32), left_shape, late_shape),
        (vmem, vmem, vmem, vmem),
        [vmem, vmem, vmem, vmem, hbm, hbm],
        like(pixels, frame_shape) + [done(2)],
        angles, field, rows, full, pixels, recon,
    )
    totals = ()
    for iteration in range(1, STEPS):
        parts = commands(signal, recon_late)
        held = (screen, pupil_amp, pixels)
        frame, signal, *totals, recon_late = call(
            later_kernel,
            "next_frame",
            (frame_shape, signal_shape, total_shape, late_shape),
            (vmem, vmem, vmem, vmem),
            [vmem] * 7 + [hbm] * 4 + [vmem] * len(totals),
            like(*held) + [done(4)],
            parts, tilts, cells, gx_parts, gy_parts, left, full, *held, recon, *totals,
        )
    parts, frame = commands(signal, recon_late, frame)
    command_total = call(
        last_kernel, "total", shape((1, cases * block), f32), vmem, [vmem, vmem], like(total_shape), parts, *totals
    )
    return (command_total, frame[None])


def solution(mesh):
    return jax.shard_map(
        body,
        mesh=mesh,
        in_specs=(P("case", None, None), P(), P("mod"), P("mod"), P("case", "mod"), P(), P(), P()),
        out_specs=(P("case", None), P("case", "mod", None)),
        check_vma=False,
    )
```

time: 52.1 us -> 50.3 us (0.965)
  Pallas kernels: 12.5 us -> 10.4 us
  waiting for transfers between devices: 7.61 us -> 8.23 us
    all_to_all x2 -> x1, blocking collectives: 19.3 us -> 9.15 us  [commands(): return lax.all_to_all(partial, ('case', 'mod'), 0, 0, tiled=True)]
    all_to_all x0 -> x1, blocking collectives: none -> 9.77 us  [commands(): return (lax.all_to_all(partial, ('case', 'mod'), 0, 0, tiled=True), frame)]
    pallas_call x7, Pallas kernels: 12.5 us -> 10.4 us  [call(): pl.pallas_call(kernel, out_shape=outs, in_specs=in_specs, out_specs=out_s...]
    all_to_all x1, waiting for transfers between devices: 3.82 us -> 4.45 us  [body(): lax.all_to_all(angles, 'mod', 0, 0, tiled=True).reshape(count, LANES)]
  transfers between devices with their start and end apart: 7 -> 7, of which waited for: 5 -> 5; matrix products, arithmetic and copies ran while one was open for 0% -> 0% of each run, Pallas kernels for 5% -> 4%
where the time goes in v5:
time: 50.3 us; the launch traced here: 50 us
  blocking collectives  18.9 us (38%)
  starting transfers between devices  11.1 us (22%)
  Pallas kernels  10.4 us (21%)
  waiting for transfers between devices  8.23 us (16%)
  between operations  1.33 us (3%)
    pallas_call x7, Pallas kernels, call(): pl.pallas_call(kernel, out_shape=outs, in_specs=in_specs, out_specs=out_s...  10.4 us
    all_to_all x1, blocking collectives, commands(): return (lax.all_to_all(partial, ('case', 'mod'), 0, 0, tiled=True), frame)  9.77 us
    all_to_all x1, blocking collectives, commands(): return lax.all_to_all(partial, ('case', 'mod'), 0, 0, tiled=True)  9.15 us
    all_to_all x1, starting transfers between devices, body(): lax.all_to_all(angles, 'mod', 0, 0, tiled=True).reshape(count, LANES)  7.25 us
    all_to_all x1, waiting for transfers between devices, body(): lax.all_to_all(angles, 'mod', 0, 0, tiled=True).reshape(count, LANES)  4.45 us
    ppermute x6, starting transfers between devices, commands(): lax.ppermute(signal, 'case', [(i, i ^ j) for i in range(cases)])  3.88 us
    ppermute x6, waiting for transfers between devices, commands(): lax.ppermute(signal, 'case', [(i, i ^ j) for i in range(cases)])  3.79 us
  transfers between devices with their start and end apart: 7, of which 5 were waited for; matrix products, arithmetic and copies ran while one was open for 0% of the time, Pallas kernels for 4%

profile of v5, /device:TPU:0, one launch (start us, length us, event | category | flops | bytes accessed | tf_op | source)
XLA Modules:
  0.0 50.0 jit_solution(1299880329982269545)
XLA Ops:
  1.3 0.6 %spread.1 = f32[8,1,128]{2,1,0:T(1,128)} custom-call(s32[1]{0:T(128)S(6)} %copy.13.point_ref), custom_call_target="tpu_custom_call" | custom-call | tf_op jit(solution)/shard_map/modulation_angles/spread/pallas_call | solution.py:361
  1.9 7.3 %all-to-all-start = ((f32[8,1,128]{2,1,0:T(1,128)}), f32[8,1,128]{2,1,0:T(1,128)S(1)}, u32[]{:S(2)}, u32[]{:S(2)}) async-start(f32[8,1,128]{2,1,0:T(1,128)} %spread.1), calls=%async_computation | async-start | bytes 8192 | tf_op jit(solution)/shard_map/modulation_angles/all_to_all | solution.py:385
  9.1 1.9 %prepare.1 = (bf16[256,512]{1,0:T(8,128)(2,1)S(1)}, f32[64,512]{1,0:T(8,128)S(1)}, bf16[512,512]{1,0:T(8,128)(2,1)S(1)}, s32[40,128]{1,0:T(8,128)S(1)}, bf16[256...) custom-call(f32[256,256]{1,0:T(8,128)} %bitcast.8, f32[256,256]{1,0:T(8,128)} %amp_hbm.3, ...), custom_call_target="tpu_custom_call" | custom-call | tf_op jit(solution)/shard_map/prepare/pallas_call | solution.py:361
  11.1 4.4 %all-to-all-done = f32[8,1,128]{2,1,0:T(1,128)S(1)} async-done(((f32[8,1,128]{2,1,0:T(1,128)}), f32[8,1,128]{2,1,0:T(1,128)S(1)}, u32[]{:S(2)}, u32[]{:S(2)}) %all-to-all-start) | async-done | bytes 4128 | tf_op jit(solution)/shard_map/modulation_angles/all_to_all | solution.py:385
  15.5 1.9 %first_frame.1 = (f32[8,128]{1,0:T(8,128)S(1)}, f32[2,8,256]{2,1,0:T(8,128)S(1)}, bf16[512,512]{1,0:T(8,128)(2,1)S(1)}, bf16[512,1024]{1,0:T(8,128)(2,1)S(1)}) custom-call(f32[8,128]{1,0:T(8,128)S(1)} %bitcast.7, bf16[256,512]{1,0:T(8,128)(2,1)S(1)} %get-tuple-element.19.field_ref, f32[64,512]{1,0:T(8,128)S(1)} %get-tuple-element.20.rows_ref, ...), custom_call_target="tpu_custom_call" | custom-call | tf_op jit(solution)/shard_map/first_frame/pallas_call | solution.py:361
  17.4 0.1 collective-permute-start.2
  17.5 1.6 %collective-permute-start.1 = (f32[8,128]{1,0:T(8,128)S(1)}, f32[8,128]{1,0:T(8,128)S(1)}, u32[]{:S(2)}, u32[]{:S(2)}) collective-permute-start(f32[8,128]{1,0:T(8,128)S(1)} %get-tuple-element.22.refs_0_), channel_id=1, source_target_pairs={{0,16},{8,24},{16,0},{24,8},{1,17},{9,25},{17,1},{25,9},{2,18},{10... | collective-permute-start | bytes 12296 | tf_op jit(solution)/shard_map/ppermute | solution.py:418
  19.1 0.3 collective-permute-start
  19.4 1.2 %collective-permute-done.2.refs_3_ = f32[8,128]{1,0:T(8,128)S(1)} collective-permute-done((f32[8,128]{1,0:T(8,128)S(1)}, f32[8,128]{1,0:T(8,128)S(1)}, u32[]{:S(2)}, u32[]{:S(2)}) %collective-permute-start.2) | collective-permute-done | bytes 4128 | tf_op jit(solution)/shard_map/ppermute | solution.py:418
  20.5 0.7 %collective-permute-done.1.refs_2_ = f32[8,128]{1,0:T(8,128)S(1)} collective-permute-done((f32[8,128]{1,0:T(8,128)S(1)}, f32[8,128]{1,0:T(8,128)S(1)}, u32[]{:S(2)}, u32[]{:S(2)}) %collective-permute-start.1) | collective-permute-done | bytes 4128 | tf_op jit(solution)/shard_map/ppermute | solution.py:418
  21.2 0.0 collective-permute-done.refs_1_
  21.2 0.8 %commands.1 = bf16[32,2,640]{2,1,0:T(2,128)(2,1)S(1)} custom-call(f32[8,128]{1,0:T(8,128)S(1)} %get-tuple-element.22.refs_0_, f32[8,128]{1,0:T(8,128)S(1)} %collective-permute-done.refs_1_, f32[8,128]{1,0:T(8,128)S(1)} %collective-permute-done.1.refs_2_, f32[8,128]{1,0:T(8,128)S(1)} %collective-permute-done.2.refs_3_, ...), custom_call_target="tpu_custom_call" | custom-call | tf_op jit(solution)/shard_map/commands/pallas_call | solution.py:361
  22.0 9.1 %all_to_all.15.parts_ref = bf16[32,2,640]{2,1,0:T(2,128)(2,1)S(1)} all-to-all(bf16[32,2,640]{2,1,0:T(2,128)(2,1)S(1)} %commands.1), channel_id=1, replica_groups=mesh['case'=4,'mod'=8] {'case','mod'}, dimensions={0} | all-to-all | bytes 163840 | tf_op jit(solution)/shard_map/all_to_all | solution.py:424
  31.1 3.2 %next_frame.1 = (f32[64,512]{1,0:T(8,128)S(1)}, f32[8,128]{1,0:T(8,128)S(1)}, f32[4,2,640]{2,1,0:T(2,128)S(1)}, bf16[512,1024]{1,0:T(8,128)(2,1)S(1)}) custom-call(bf16[32,2,640]{2,1,0:T(2,128)(2,1)S(1)} %all_to_all.15.parts_ref, f32[2,8,256]{2,1,0:T(8,128)S(1)} %get-tuple-element.25.tilt_ref, s32[40,128]{1,0:T(8,128)S(1)} %get-tuple-element.26.cells_ref, ...), custom_call_target="tpu_custom_call" | custom-call | tf_op jit(solution)/shard_map/next_frame/pallas_call | solution.py:361
  34.3 0.3 collective-permute-start.5
  34.7 1.5 %collective-permute-start.4 = (f32[8,128]{1,0:T(8,128)S(1)}, f32[8,128]{1,0:T(8,128)S(1)}, u32[]{:S(2)}, u32[]{:S(2)}) collective-permute-start(f32[8,128]{1,0:T(8,128)S(1)} %get-tuple-element.30.refs_0_), channel_id=1, source_target_pairs={{0,16},{8,24},{16,0},{24,8},{1,17},{9,25},{17,1},{25,9},{2,18},{10... | collective-permute-start | bytes 12296 | tf_op jit(solution)/shard_map/ppermute | solution.py:418
  36.2 0.1 collective-permute-start.3
  36.3 1.1 %collective-permute-done.5.refs_3_ = f32[8,128]{1,0:T(8,128)S(1)} collective-permute-done((f32[8,128]{1,0:T(8,128)S(1)}, f32[8,128]{1,0:T(8,128)S(1)}, u32[]{:S(2)}, u32[]{:S(2)}) %collective-permute-start.5) | collective-permute-done | bytes 4128 | tf_op jit(solution)/shard_map/ppermute | solution.py:418
  37.4 0.8 %collective-permute-done.4.refs_2_ = f32[8,128]{1,0:T(8,128)S(1)} collective-permute-done((f32[8,128]{1,0:T(8,128)S(1)}, f32[8,128]{1,0:T(8,128)S(1)}, u32[]{:S(2)}, u32[]{:S(2)}) %collective-permute-start.4) | collective-permute-done | bytes 4128 | tf_op jit(solution)/shard_map/ppermute | solution.py:418
  38.3 0.0 collective-permute-done.3.refs_1_
  38.3 1.3 %last_commands.1 = (bf16[32,2,640]{2,1,0:T(2,128)(2,1)S(1)}, f32[64,512]{1,0:T(8,128)}) custom-call(f32[8,128]{1,0:T(8,128)S(1)} %get-tuple-element.30.refs_0_, f32[8,128]{1,0:T(8,128)S(1)} %collective-permute-done.3.refs_1_, f32[8,128]{1,0:T(8,128)S(1)} %collective-permute-done.4.refs_2_, f32[8,128]{1,0:T(8,128)S(1)} %collective-permute-done.5.refs_3_, ...), custom_call_target="tpu_custom_call" | custom-call | tf_op jit(solution)/shard_map/last_commands/pallas_call | solution.py:361
  39.6 9.8 %all_to_all.16.parts_ref = bf16[32,2,640]{2,1,0:T(2,128)(2,1)S(1)} all-to-all(bf16[32,2,640]{2,1,0:T(2,128)(2,1)S(1)} %get-tuple-element.33), channel_id=1, replica_groups=mesh['case'=4,'mod'=8] {'case','mod'}, dimensions={0} | all-to-all | bytes 163840 | tf_op jit(solution)/shard_map/all_to_all | solution.py:428
  49.3 0.7 %total.1 = f32[1,5120]{1,0:T(1,128)} custom-call(bf16[32,2,640]{2,1,0:T(2,128)(2,1)S(1)} %all_to_all.16.parts_ref, f32[4,2,640]{2,1,0:T(2,128)S(1)} %get-tuple-element.34.total_ref), custom_call_target="tpu_custom_call" | custom-call | tf_op jit(solution)/shard_map/total/pallas_call | solution.py:361
Async XLA Ops:
  1.9 13.6 %all-to-all-start = ((f32[8,1,128]{2,1,0:T(1,128)}), f32[8,1,128]{2,1,0:T(1,128)S(1)}, u32[]{:S(2)}, u32[]{:S(2)}) async-start(f32[8,1,128]{2,1,0:T(1,128)} %spread.1), calls=%async_computation | async-start | bytes 8192 | tf_op jit(solution)/shard_map/modulation_angles/all_to_all | solution.py:385
  17.4 3.1 %collective-permute-start.2 = (f32[8,128]{1,0:T(8,128)S(1)}, f32[8,128]{1,0:T(8,128)S(1)}, u32[]{:S(2)}, u32[]{:S(2)}) collective-permute-start(f32[8,128]{1,0:T(8,128)S(1)} %get-tuple-element.22.refs_0_), channel_id=1, source_target_pairs={{0,24},{8,16},{16,8},{24,0},{1,25},{9,17},{17,9},{25,1},{2,26},{10... | collective-permute-start | bytes 12296 | tf_op jit(solution)/shard_map/ppermute | solution.py:418
  17.5 3.7 %collective-permute-start.1 = (f32[8,128]{1,0:T(8,128)S(1)}, f32[8,128]{1,0:T(8,128)S(1)}, u32[]{:S(2)}, u32[]{:S(2)}) collective-permute-start(f32[8,128]{1,0:T(8,128)S(1)} %get-tuple-element.22.refs_0_), channel_id=1, source_target_pairs={{0,16},{8,24},{16,0},{24,8},{1,17},{9,25},{17,1},{25,9},{2,18},{10... | collective-permute-start | bytes 12296 | tf_op jit(solution)/shard_map/ppermute | solution.py:418
  19.1 2.1 %collective-permute-start = (f32[8,128]{1,0:T(8,128)S(1)}, f32[8,128]{1,0:T(8,128)S(1)}, u32[]{:S(2)}, u32[]{:S(2)}) collective-permute-start(f32[8,128]{1,0:T(8,128)S(1)} %get-tuple-element.22.refs_0_), channel_id=1, source_target_pairs={{0,8},{8,0},{16,24},{24,16},{1,9},{9,1},{17,25},{25,17},{2,10},{10... | collective-permute-start | bytes 12296 | tf_op jit(solution)/shard_map/ppermute | solution.py:418
  34.3 3.1 %collective-permute-start.5 = (f32[8,128]{1,0:T(8,128)S(1)}, f32[8,128]{1,0:T(8,128)S(1)}, u32[]{:S(2)}, u32[]{:S(2)}) collective-permute-start(f32[8,128]{1,0:T(8,128)S(1)} %get-tuple-element.30.refs_0_), channel_id=1, source_target_pairs={{0,24},{8,16},{16,8},{24,0},{1,25},{9,17},{17,9},{25,1},{2,26},{10... | collective-permute-start | bytes 12296 | tf_op jit(solution)/shard_map/ppermute | solution.py:418
  34.7 3.6 %collective-permute-start.4 = (f32[8,128]{1,0:T(8,128)S(1)}, f32[8,128]{1,0:T(8,128)S(1)}, u32[]{:S(2)}, u32[]{:S(2)}) collective-permute-start(f32[8,128]{1,0:T(8,128)S(1)} %get-tuple-element.30.refs_0_), channel_id=1, source_target_pairs={{0,16},{8,24},{16,0},{24,8},{1,17},{9,25},{17,1},{25,9},{2,18},{10... | collective-permute-start | bytes 12296 | tf_op jit(solution)/shard_map/ppermute | solution.py:418
  36.2 2.1 %collective-permute-start.3 = (f32[8,128]{1,0:T(8,128)S(1)}, f32[8,128]{1,0:T(8,128)S(1)}, u32[]{:S(2)}, u32[]{:S(2)}) collective-permute-start(f32[8,128]{1,0:T(8,128)S(1)} %get-tuple-element.30.refs_0_), channel_id=1, source_target_pairs={{0,8},{8,0},{16,24},{24,16},{1,9},{9,1},{17,25},{25,17},{2,10},{10... | collective-permute-start | bytes 12296 | tf_op jit(solution)/shard_map/ppermute | solution.py:418

commit v6 on v5

--- a/solution.py
+++ b/solution.py
@@ -1,4 +1,3 @@
-import functools
 import math
 
 import jax
@@ -198,27 +197,32 @@
     return jnp.concatenate([jnp.concatenate([real, -imag], 1), jnp.concatenate([imag, real], 1)], 0)
 
 
-def detector_part(both, table, count):
-    detector = jnp.dot(both, table, preferred_element_type=jnp.float32)
-    squares = (detector * detector).reshape(2 * count, both.shape[0] // (2 * count), detector.shape[1])
-    return jnp.sum(squares, 0) * (1.0 / count)
-
-
-def detect(both, full_ref, pixels_ref, frame_ref, count):
+def detect(left, field, full_ref, sine, cosine, frame_ref):
     row_count, length = frame_ref.shape
-    pixels = pixels_ref[...] - lax.axis_index("mod") * (row_count * length)
-    high, low = pixels >> 7, pixels & (LANES - 1)
+    count = sine.shape[0]
+    both = half_way(left, field, sine, cosine)
+    detector = jnp.dot(both, full_ref[...], preferred_element_type=jnp.float32)
+    squares = (detector * detector).reshape(2 * count, row_count, length)
+    frame_ref[...] = jnp.sum(squares, 0) * (1.0 / count)
+
+
+def read_signals(frame_ref, pixels):
+    row_count, length = frame_ref.shape
     per_row = length // LANES
+    own = pixels - lax.axis_index("mod") * (row_count * length)
+    low = own & (LANES - 1)
+    run = (own >> 7) & (per_row - 1)
+    row = own >> (per_row * LANES).bit_length() - 1
+    bits = [(run >> i) & 1 == 1 for i in range(per_row.bit_length() - 1)]
     total = jnp.zeros(pixels.shape, jnp.float32)
-    step = length // 2
-    for start in range(0, length, step):
-        columns = pl.ds(start, step)
-        frame_ref[:, columns] = detector_part(both, full_ref[:, columns], count)
-        for i in range(row_count):
-            for j in range(start // LANES, (start + step) // LANES):
-                spread = jnp.broadcast_to(frame_ref[i : i + 1, j * LANES : (j + 1) * LANES], pixels.shape)
-                picked = jnp.take_along_axis(spread, low, axis=1, mode="promise_in_bounds")
-                total = jnp.where(high == i * per_row + j, picked, total)
+    for i in range(row_count):
+        picked = []
+        for j in range(per_row):
+            spread = jnp.broadcast_to(frame_ref[i : i + 1, j * LANES : (j + 1) * LANES], pixels.shape)
+            picked.append(jnp.take_along_axis(spread, low, axis=1, mode="promise_in_bounds"))
+        for bit in bits:
+            picked = [jnp.where(bit, picked[j + 1], picked[j]) for j in range(0, len(picked), 2)]
+        total = jnp.where(row == i, picked[0], total)
     return total.astype(jnp.bfloat16).astype(jnp.float32)
 
 
@@ -236,9 +240,9 @@
     left = left_rows(rows_ref[...], *tilts[:2])
     left_ref[...] = left
     field = field_matrix(field_ref[:, :pupil], field_ref[:, pupil:])
-    both = half_way(left, field, *tilts[2:])
+    detect(left, field, full_ref, *tilts[2:], frame_ref)
     pixels.wait()
-    signal_ref[...] = detect(both, full_ref, pixels_ref, frame_ref, angles_ref.shape[0])
+    signal_ref[...] = read_signals(frame_ref, pixels_ref[...])
     recon.wait()
 
 
@@ -278,16 +282,15 @@
     amp.wait()
     field = field_matrix(*field_parts(phase_ref[...] - surface, amp_ref[...]))
 
-    both = half_way(left_ref[...], field, tilt_ref[0], tilt_ref[1])
+    detect(left_ref[...], field, full_ref, tilt_ref[0], tilt_ref[1], frame_ref)
     pixels.wait()
-    signal_ref[...] = detect(both, full_ref, pixels_ref, frame_ref, tilt_ref.shape[1])
+    signal_ref[...] = read_signals(frame_ref, pixels_ref[...])
     recon.wait()
 
 
-def command_kernel(cases, *refs):
-    signal_refs, recon_refs, refs = refs[:cases], refs[cases : cases + 2], refs[cases + 2 :]
-    out_ref = refs[0] if len(refs) == 1 else refs[1]
-    frame_out = None if len(refs) == 1 else copies([(refs[0], refs[2])], refs[3])[0]
+def command_kernel(*refs):
+    signal_refs, recon_refs, out_ref = refs[:-3], refs[-3:-1], refs[-1]
+    cases = len(signal_refs)
     own_case = lax.axis_index("case")
     received = [ref[...] for ref in signal_refs]
     ordered = []
@@ -315,17 +318,21 @@
         ).astype(jnp.bfloat16)
         for i in range(copies_each):
             out_ref[case * copies_each + i] = message
-    if frame_out is not None:
-        frame_out.wait()
-
-
-def last_kernel(parts_ref, total_ref, out_ref, sums_ref):
+
+
+def last_kernel(parts_ref, total_ref, frame_ref, total_hbm, frame_hbm, sums_ref, out_ref, semaphores):
+    frame_out = pltpu.make_async_copy(frame_ref, frame_hbm, semaphores.at[0])
+    frame_out.start()
     add_commands(parts_ref, total_ref, sums_ref)
     cases, pieces, width = sums_ref.shape
     for case in range(cases):
         for i in range(pieces):
             start = (case * pieces + i) * width
             out_ref[:, start : start + width] = sums_ref[case, i : i + 1, :]
+    total_out = pltpu.make_async_copy(out_ref, total_hbm, semaphores.at[1])
+    total_out.start()
+    frame_out.wait()
+    total_out.wait()
 
 
 def body(turbulence, pupil_amp, mod_points, valid_pix, recon, gx, gy, act_map):
@@ -412,20 +419,15 @@
         screen, pupil_amp, act_map.reshape(map_shape), gx.T, gy.T, rows_table, full_table, recon,
     )
 
-    def commands(signal, recon_late, frame=None):
+    def commands(signal, recon_late):
         signals = [signal]
         for j in range(1, cases):
             signals.append(lax.ppermute(signal, "case", [(i, i ^ j) for i in range(cases)]))
-        messages = shape((cases * devices_mod, pieces, width), bf16)
-        kernel = functools.partial(command_kernel, cases)
-        operands = (*signals, recon_first, recon_late)
-        if frame is None:
-            partial = call(kernel, "commands", messages, vmem, [vmem] * (cases + 2), [], *operands)
-            return lax.all_to_all(partial, ("case", "mod"), 0, 0, tiled=True)
-        partial, frame = call(
-            kernel, "last_commands", (messages, frame), (vmem, hbm), [vmem] * (cases + 3), [done(1)], *operands, frame
+        partial = call(
+            command_kernel, "commands", shape((cases * devices_mod, pieces, width), bf16), vmem,
+            [vmem] * (cases + 2), [], *signals, recon_first, recon_late,
         )
-        return lax.all_to_all(partial, ("case", "mod"), 0, 0, tiled=True), frame
+        return lax.all_to_all(partial, ("case", "mod"), 0, 0, tiled=True)
 
     frame_shape = shape((row_count, length), f32)
     signal_shape = shape((signal_rows, LANES), f32)
@@ -453,9 +455,16 @@
             like(*held) + [done(4)],
             parts, tilts, cells, gx_parts, gy_parts, left, full, *held, recon, *totals,
         )
-    parts, frame = commands(signal, recon_late, frame)
-    command_total = call(
-        last_kernel, "total", shape((1, cases * block), f32), vmem, [vmem, vmem], like(total_shape), parts, *totals
+    parts = commands(signal, recon_late)
+    command_shape = shape((1, cases * block), f32)
+    command_total, frame = call(
+        last_kernel,
+        "total",
+        (command_shape, frame_shape),
+        (hbm, hbm),
+        [vmem, vmem, vmem],
+        like(total_shape, command_shape) + [done(2)],
+        parts, *totals, frame,
     )
     return (command_total, frame[None])
 

time: 50.3 us -> 49.6 us (0.986)
  Pallas kernels: 10.4 us -> 9.64 us
    all_to_all x1 -> x2, blocking collectives: 9.15 us -> 18.9 us  [commands(): return lax.all_to_all(partial, ('case', 'mod'), 0, 0, tiled=True)]
    all_to_all x1 -> x0, blocking collectives: 9.77 us -> none  [commands(): return (lax.all_to_all(partial, ('case', 'mod'), 0, 0, tiled=True), frame)]
    pallas_call x7, Pallas kernels: 10.4 us -> 9.64 us  [call(): pl.pallas_call(kernel, out_shape=outs, in_specs=in_specs, out_specs=out_s...]
where the time goes in v6:
time: 49.6 us; the launch traced here: 49.3 us
  blocking collectives  18.9 us (38%)
  starting transfers between devices  11.1 us (22%)
  Pallas kernels  9.64 us (19%)
  waiting for transfers between devices  8.23 us (17%)
  between operations  1.33 us (3%)
    all_to_all x2, blocking collectives, commands(): return lax.all_to_all(partial, ('case', 'mod'), 0, 0, tiled=True)  18.9 us
    pallas_call x7, Pallas kernels, call(): pl.pallas_call(kernel, out_shape=outs, in_specs=in_specs, out_specs=out_s...  9.64 us
    all_to_all x1, starting transfers between devices, body(): lax.all_to_all(angles, 'mod', 0, 0, tiled=True).reshape(count, LANES)  7.25 us
    all_to_all x1, waiting for transfers between devices, body(): lax.all_to_all(angles, 'mod', 0, 0, tiled=True).reshape(count, LANES)  4.45 us
    ppermute x6, starting transfers between devices, commands(): lax.ppermute(signal, 'case', [(i, i ^ j) for i in range(cases)])  3.88 us
    ppermute x6, waiting for transfers between devices, commands(): lax.ppermute(signal, 'case', [(i, i ^ j) for i in range(cases)])  3.79 us
  transfers between devices with their start and end apart: 7, of which 5 were waited for; matrix products, arithmetic and copies ran while one was open for 0% of the time, Pallas kernels for 4%

profile of v6, /device:TPU:0, one launch (start us, length us, event | category | flops | bytes accessed | tf_op | source)
XLA Modules:
  0.0 49.3 jit_solution(13699702623444057704)
XLA Ops:
  1.3 0.6 %spread.1 = f32[8,1,128]{2,1,0:T(1,128)} custom-call(s32[1]{0:T(128)S(6)} %copy.13.point_ref), custom_call_target="tpu_custom_call" | custom-call | tf_op jit(solution)/shard_map/modulation_angles/spread/pallas_call | solution.py:368
  1.9 7.3 %all-to-all-start = ((f32[8,1,128]{2,1,0:T(1,128)}), f32[8,1,128]{2,1,0:T(1,128)S(1)}, u32[]{:S(2)}, u32[]{:S(2)}) async-start(f32[8,1,128]{2,1,0:T(1,128)} %spread.1), calls=%async_computation | async-start | bytes 8192 | tf_op jit(solution)/shard_map/modulation_angles/all_to_all | solution.py:392
  9.1 1.9 %prepare.1 = (bf16[256,512]{1,0:T(8,128)(2,1)S(1)}, f32[64,512]{1,0:T(8,128)S(1)}, bf16[512,512]{1,0:T(8,128)(2,1)S(1)}, s32[40,128]{1,0:T(8,128)S(1)}, bf16[256...) custom-call(f32[256,256]{1,0:T(8,128)} %bitcast.8, f32[256,256]{1,0:T(8,128)} %amp_hbm.3, ...), custom_call_target="tpu_custom_call" | custom-call | tf_op jit(solution)/shard_map/prepare/pallas_call | solution.py:368
  11.1 4.4 %all-to-all-done = f32[8,1,128]{2,1,0:T(1,128)S(1)} async-done(((f32[8,1,128]{2,1,0:T(1,128)}), f32[8,1,128]{2,1,0:T(1,128)S(1)}, u32[]{:S(2)}, u32[]{:S(2)}) %all-to-all-start) | async-done | bytes 4128 | tf_op jit(solution)/shard_map/modulation_angles/all_to_all | solution.py:392
  15.5 1.7 %first_frame.1 = (f32[8,128]{1,0:T(8,128)S(1)}, f32[2,8,256]{2,1,0:T(8,128)S(1)}, bf16[512,512]{1,0:T(8,128)(2,1)S(1)}, bf16[512,1024]{1,0:T(8,128)(2,1)S(1)}) custom-call(f32[8,128]{1,0:T(8,128)S(1)} %bitcast.7, bf16[256,512]{1,0:T(8,128)(2,1)S(1)} %get-tuple-element.19.field_ref, f32[64,512]{1,0:T(8,128)S(1)} %get-tuple-element.20.rows_ref, ...), custom_call_target="tpu_custom_call" | custom-call | tf_op jit(solution)/shard_map/first_frame/pallas_call | solution.py:368
  17.3 0.1 collective-permute-start.2
  17.3 1.6 %collective-permute-start.1 = (f32[8,128]{1,0:T(8,128)S(1)}, f32[8,128]{1,0:T(8,128)S(1)}, u32[]{:S(2)}, u32[]{:S(2)}) collective-permute-start(f32[8,128]{1,0:T(8,128)S(1)} %get-tuple-element.22.refs_0_), channel_id=1, source_target_pairs={{0,16},{8,24},{16,0},{24,8},{1,17},{9,25},{17,1},{25,9},{2,18},{10... | collective-permute-start | bytes 12296 | tf_op jit(solution)/shard_map/ppermute | solution.py:425
  18.9 0.3 collective-permute-start
  19.2 1.2 %collective-permute-done.2.refs_3_ = f32[8,128]{1,0:T(8,128)S(1)} collective-permute-done((f32[8,128]{1,0:T(8,128)S(1)}, f32[8,128]{1,0:T(8,128)S(1)}, u32[]{:S(2)}, u32[]{:S(2)}) %collective-permute-start.2) | collective-permute-done | bytes 4128 | tf_op jit(solution)/shard_map/ppermute | solution.py:425
  20.4 0.7 %collective-permute-done.1.refs_2_ = f32[8,128]{1,0:T(8,128)S(1)} collective-permute-done((f32[8,128]{1,0:T(8,128)S(1)}, f32[8,128]{1,0:T(8,128)S(1)}, u32[]{:S(2)}, u32[]{:S(2)}) %collective-permute-start.1) | collective-permute-done | bytes 4128 | tf_op jit(solution)/shard_map/ppermute | solution.py:425
  21.0 0.0 collective-permute-done.refs_1_
  21.0 0.8 %commands.2 = bf16[32,2,640]{2,1,0:T(2,128)(2,1)S(1)} custom-call(f32[8,128]{1,0:T(8,128)S(1)} %get-tuple-element.22.refs_0_, f32[8,128]{1,0:T(8,128)S(1)} %collective-permute-done.refs_1_, f32[8,128]{1,0:T(8,128)S(1)} %collective-permute-done.1.refs_2_, f32[8,128]{1,0:T(8,128)S(1)} %collective-permute-done.2.refs_3_, ...), custom_call_target="tpu_custom_call" | custom-call | tf_op jit(solution)/shard_map/commands/pallas_call | solution.py:368
  21.8 9.1 %all_to_all.15.parts_ref = bf16[32,2,640]{2,1,0:T(2,128)(2,1)S(1)} all-to-all(bf16[32,2,640]{2,1,0:T(2,128)(2,1)S(1)} %commands.2), channel_id=1, replica_groups=mesh['case'=4,'mod'=8] {'case','mod'}, dimensions={0} | all-to-all | bytes 163840 | tf_op jit(solution)/shard_map/all_to_all | solution.py:430
  31.0 3.0 %next_frame.1 = (f32[64,512]{1,0:T(8,128)S(1)}, f32[8,128]{1,0:T(8,128)S(1)}, f32[4,2,640]{2,1,0:T(2,128)S(1)}, bf16[512,1024]{1,0:T(8,128)(2,1)S(1)}) custom-call(bf16[32,2,640]{2,1,0:T(2,128)(2,1)S(1)} %all_to_all.15.parts_ref, f32[2,8,256]{2,1,0:T(8,128)S(1)} %get-tuple-element.25.tilt_ref, s32[40,128]{1,0:T(8,128)S(1)} %get-tuple-element.26.cells_ref, ...), custom_call_target="tpu_custom_call" | custom-call | tf_op jit(solution)/shard_map/next_frame/pallas_call | solution.py:368
  34.0 0.3 collective-permute-start.5
  34.3 1.5 %collective-permute-start.4 = (f32[8,128]{1,0:T(8,128)S(1)}, f32[8,128]{1,0:T(8,128)S(1)}, u32[]{:S(2)}, u32[]{:S(2)}) collective-permute-start(f32[8,128]{1,0:T(8,128)S(1)} %get-tuple-element.30.refs_0_), channel_id=1, source_target_pairs={{0,16},{8,24},{16,0},{24,8},{1,17},{9,25},{17,1},{25,9},{2,18},{10... | collective-permute-start | bytes 12296 | tf_op jit(solution)/shard_map/ppermute | solution.py:425
  35.8 0.1 collective-permute-start.3
  36.0 1.1 %collective-permute-done.5.refs_3_ = f32[8,128]{1,0:T(8,128)S(1)} collective-permute-done((f32[8,128]{1,0:T(8,128)S(1)}, f32[8,128]{1,0:T(8,128)S(1)}, u32[]{:S(2)}, u32[]{:S(2)}) %collective-permute-start.5) | collective-permute-done | bytes 4128 | tf_op jit(solution)/shard_map/ppermute | solution.py:425
  37.1 0.8 %collective-permute-done.4.refs_2_ = f32[8,128]{1,0:T(8,128)S(1)} collective-permute-done((f32[8,128]{1,0:T(8,128)S(1)}, f32[8,128]{1,0:T(8,128)S(1)}, u32[]{:S(2)}, u32[]{:S(2)}) %collective-permute-start.4) | collective-permute-done | bytes 4128 | tf_op jit(solution)/shard_map/ppermute | solution.py:425
  38.0 0.0 collective-permute-done.3.refs_1_
  38.0 0.8 %commands.3 = bf16[32,2,640]{2,1,0:T(2,128)(2,1)S(1)} custom-call(f32[8,128]{1,0:T(8,128)S(1)} %get-tuple-element.30.refs_0_, f32[8,128]{1,0:T(8,128)S(1)} %collective-permute-done.3.refs_1_, f32[8,128]{1,0:T(8,128)S(1)} %collective-permute-done.4.refs_2_, f32[8,128]{1,0:T(8,128)S(1)} %collective-permute-done.5.refs_3_, ...), custom_call_target="tpu_custom_call" | custom-call | tf_op jit(solution)/shard_map/commands/pallas_call | solution.py:368
  38.8 9.8 %all_to_all.16.parts_ref = bf16[32,2,640]{2,1,0:T(2,128)(2,1)S(1)} all-to-all(bf16[32,2,640]{2,1,0:T(2,128)(2,1)S(1)} %commands.3), channel_id=1, replica_groups=mesh['case'=4,'mod'=8] {'case','mod'}, dimensions={0} | all-to-all | bytes 163840 | tf_op jit(solution)/shard_map/all_to_all | solution.py:430
  48.5 0.7 %total.1 = (f32[1,5120]{1,0:T(1,128)}, f32[64,512]{1,0:T(8,128)}) custom-call(bf16[32,2,640]{2,1,0:T(2,128)(2,1)S(1)} %all_to_all.16.parts_ref, f32[4,2,640]{2,1,0:T(2,128)S(1)} %get-tuple-element.32.total_ref, f32[64,512]{1,0:T(8,128)S(1)} %get-tuple-element.33.frame_ref), custom_call_target="tpu_custom_call" | custom-call | tf_op jit(solution)/shard_map/total/pallas_call | solution.py:368
Async XLA Ops:
  1.9 13.6 %all-to-all-start = ((f32[8,1,128]{2,1,0:T(1,128)}), f32[8,1,128]{2,1,0:T(1,128)S(1)}, u32[]{:S(2)}, u32[]{:S(2)}) async-start(f32[8,1,128]{2,1,0:T(1,128)} %spread.1), calls=%async_computation | async-start | bytes 8192 | tf_op jit(solution)/shard_map/modulation_angles/all_to_all | solution.py:392
  17.3 3.1 %collective-permute-start.2 = (f32[8,128]{1,0:T(8,128)S(1)}, f32[8,128]{1,0:T(8,128)S(1)}, u32[]{:S(2)}, u32[]{:S(2)}) collective-permute-start(f32[8,128]{1,0:T(8,128)S(1)} %get-tuple-element.22.refs_0_), channel_id=1, source_target_pairs={{0,24},{8,16},{16,8},{24,0},{1,25},{9,17},{17,9},{25,1},{2,26},{10... | collective-permute-start | bytes 12296 | tf_op jit(solution)/shard_map/ppermute | solution.py:425
  17.3 3.7 %collective-permute-start.1 = (f32[8,128]{1,0:T(8,128)S(1)}, f32[8,128]{1,0:T(8,128)S(1)}, u32[]{:S(2)}, u32[]{:S(2)}) collective-permute-start(f32[8,128]{1,0:T(8,128)S(1)} %get-tuple-element.22.refs_0_), channel_id=1, source_target_pairs={{0,16},{8,24},{16,0},{24,8},{1,17},{9,25},{17,1},{25,9},{2,18},{10... | collective-permute-start | bytes 12296 | tf_op jit(solution)/shard_map/ppermute | solution.py:425
  18.9 2.1 %collective-permute-start = (f32[8,128]{1,0:T(8,128)S(1)}, f32[8,128]{1,0:T(8,128)S(1)}, u32[]{:S(2)}, u32[]{:S(2)}) collective-permute-start(f32[8,128]{1,0:T(8,128)S(1)} %get-tuple-element.22.refs_0_), channel_id=1, source_target_pairs={{0,8},{8,0},{16,24},{24,16},{1,9},{9,1},{17,25},{25,17},{2,10},{10... | collective-permute-start | bytes 12296 | tf_op jit(solution)/shard_map/ppermute | solution.py:425
  34.0 3.1 %collective-permute-start.5 = (f32[8,128]{1,0:T(8,128)S(1)}, f32[8,128]{1,0:T(8,128)S(1)}, u32[]{:S(2)}, u32[]{:S(2)}) collective-permute-start(f32[8,128]{1,0:T(8,128)S(1)} %get-tuple-element.30.refs_0_), channel_id=1, source_target_pairs={{0,24},{8,16},{16,8},{24,0},{1,25},{9,17},{17,9},{25,1},{2,26},{10... | collective-permute-start | bytes 12296 | tf_op jit(solution)/shard_map/ppermute | solution.py:425
  34.3 3.6 %collective-permute-start.4 = (f32[8,128]{1,0:T(8,128)S(1)}, f32[8,128]{1,0:T(8,128)S(1)}, u32[]{:S(2)}, u32[]{:S(2)}) collective-permute-start(f32[8,128]{1,0:T(8,128)S(1)} %get-tuple-element.30.refs_0_), channel_id=1, source_target_pairs={{0,16},{8,24},{16,0},{24,8},{1,17},{9,25},{17,1},{25,9},{2,18},{10... | collective-permute-start | bytes 12296 | tf_op jit(solution)/shard_map/ppermute | solution.py:425
  35.8 2.1 %collective-permute-start.3 = (f32[8,128]{1,0:T(8,128)S(1)}, f32[8,128]{1,0:T(8,128)S(1)}, u32[]{:S(2)}, u32[]{:S(2)}) collective-permute-start(f32[8,128]{1,0:T(8,128)S(1)} %get-tuple-element.30.refs_0_), channel_id=1, source_target_pairs={{0,8},{8,0},{16,24},{24,16},{1,9},{9,1},{17,25},{25,17},{2,10},{10... | collective-permute-start | bytes 12296 | tf_op jit(solution)/shard_map/ppermute | solution.py:425

commit v7 on v6

--- a/solution.py
+++ b/solution.py
@@ -70,18 +70,26 @@
     return high, low
 
 
+def choose(picked, index):
+    while len(picked) > 1:
+        odd = index & 1 == 1
+        rest = picked[len(picked) - 1 :] if len(picked) % 2 else []
+        picked = [jnp.where(odd, picked[j + 1], picked[j]) for j in range(0, len(picked) - 1, 2)] + rest
+        index = index >> 1
+    return picked[0]
+
+
 def look_up(count, row, index):
     blocks = []
     for start in range(0, index.shape[0], 8):
         block = index[start : start + 8]
         high = block >> 7
         low = block & (LANES - 1)
-        sums = [jnp.zeros(block.shape, jnp.float32) for _ in range(2)]
+        picked = []
         for i in range(count):
             spread = jnp.broadcast_to(row(i), block.shape)
-            picked = jnp.take_along_axis(spread, low, axis=1, mode="promise_in_bounds")
-            sums[i % 2] = jnp.where(high == i, picked, sums[i % 2])
-        blocks.append(sums[0] + sums[1])
+            picked.append(jnp.take_along_axis(spread, low, axis=1, mode="promise_in_bounds"))
+        blocks.append(choose(picked, high))
     return jnp.concatenate(blocks, 0) if len(blocks) > 1 else blocks[0]
 
 
@@ -213,16 +221,14 @@
     low = own & (LANES - 1)
     run = (own >> 7) & (per_row - 1)
     row = own >> (per_row * LANES).bit_length() - 1
-    bits = [(run >> i) & 1 == 1 for i in range(per_row.bit_length() - 1)]
-    total = jnp.zeros(pixels.shape, jnp.float32)
+    rows = []
     for i in range(row_count):
         picked = []
         for j in range(per_row):
             spread = jnp.broadcast_to(frame_ref[i : i + 1, j * LANES : (j + 1) * LANES], pixels.shape)
             picked.append(jnp.take_along_axis(spread, low, axis=1, mode="promise_in_bounds"))
-        for bit in bits:
-            picked = [jnp.where(bit, picked[j + 1], picked[j]) for j in range(0, len(picked), 2)]
-        total = jnp.where(row == i, picked[0], total)
+        rows.append(choose(picked, run))
+    total = choose(rows, row)
     return total.astype(jnp.bfloat16).astype(jnp.float32)
 
 

time: 49.6 us -> 49 us (0.988)
  Pallas kernels: 9.64 us -> 9.14 us
    pallas_call x7, Pallas kernels: 9.64 us -> 9.14 us  [call(): pl.pallas_call(kernel, out_shape=outs, in_specs=in_specs, out_specs=out_s...]
where the time goes in v7:
time: 49 us; the launch traced here: 48.7 us
  blocking collectives  18.9 us (39%)
  starting transfers between devices  11.1 us (23%)
  Pallas kernels  9.14 us (19%)
  waiting for transfers between devices  8.24 us (17%)
  between operations  1.33 us (3%)
    all_to_all x2, blocking collectives, commands(): return lax.all_to_all(partial, ('case', 'mod'), 0, 0, tiled=True)  18.9 us
    pallas_call x7, Pallas kernels, call(): pl.pallas_call(kernel, out_shape=outs, in_specs=in_specs, out_specs=out_s...  9.14 us
    all_to_all x1, starting transfers between devices, body(): lax.all_to_all(angles, 'mod', 0, 0, tiled=True).reshape(count, LANES)  7.25 us
    all_to_all x1, waiting for transfers between devices, body(): lax.all_to_all(angles, 'mod', 0, 0, tiled=True).reshape(count, LANES)  4.45 us
    ppermute x6, starting transfers between devices, commands(): lax.ppermute(signal, 'case', [(i, i ^ j) for i in range(cases)])  3.88 us
    ppermute x6, waiting for transfers between devices, commands(): lax.ppermute(signal, 'case', [(i, i ^ j) for i in range(cases)])  3.79 us
  transfers between devices with their start and end apart: 7, of which 5 were waited for; matrix products, arithmetic and copies ran while one was open for 0% of the time, Pallas kernels for 4%

profile of v7, /device:TPU:0, one launch (start us, length us, event | category | flops | bytes accessed | tf_op | source)
XLA Modules:
  0.0 48.7 jit_solution(11564467378956088104)
XLA Ops:
  1.3 0.6 %spread.1 = f32[8,1,128]{2,1,0:T(1,128)} custom-call(s32[1]{0:T(128)S(6)} %copy.13.point_ref), custom_call_target="tpu_custom_call" | custom-call | tf_op jit(solution)/shard_map/modulation_angles/spread/pallas_call | solution.py:374
  1.9 7.3 %all-to-all-start = ((f32[8,1,128]{2,1,0:T(1,128)}), f32[8,1,128]{2,1,0:T(1,128)S(1)}, u32[]{:S(2)}, u32[]{:S(2)}) async-start(f32[8,1,128]{2,1,0:T(1,128)} %spread.1), calls=%async_computation | async-start | bytes 8192 | tf_op jit(solution)/shard_map/modulation_angles/all_to_all | solution.py:398
  9.1 1.9 %prepare.1 = (bf16[256,512]{1,0:T(8,128)(2,1)S(1)}, f32[64,512]{1,0:T(8,128)S(1)}, bf16[512,512]{1,0:T(8,128)(2,1)S(1)}, s32[40,128]{1,0:T(8,128)S(1)}, bf16[256...) custom-call(f32[256,256]{1,0:T(8,128)} %bitcast.8, f32[256,256]{1,0:T(8,128)} %amp_hbm.3, ...), custom_call_target="tpu_custom_call" | custom-call | tf_op jit(solution)/shard_map/prepare/pallas_call | solution.py:374
  11.1 4.4 %all-to-all-done = f32[8,1,128]{2,1,0:T(1,128)S(1)} async-done(((f32[8,1,128]{2,1,0:T(1,128)}), f32[8,1,128]{2,1,0:T(1,128)S(1)}, u32[]{:S(2)}, u32[]{:S(2)}) %all-to-all-start) | async-done | bytes 4128 | tf_op jit(solution)/shard_map/modulation_angles/all_to_all | solution.py:398
  15.5 1.7 %first_frame.1 = (f32[8,128]{1,0:T(8,128)S(1)}, f32[2,8,256]{2,1,0:T(8,128)S(1)}, bf16[512,512]{1,0:T(8,128)(2,1)S(1)}, bf16[512,1024]{1,0:T(8,128)(2,1)S(1)}) custom-call(f32[8,128]{1,0:T(8,128)S(1)} %bitcast.7, bf16[256,512]{1,0:T(8,128)(2,1)S(1)} %get-tuple-element.19.field_ref, f32[64,512]{1,0:T(8,128)S(1)} %get-tuple-element.20.rows_ref, ...), custom_call_target="tpu_custom_call" | custom-call | tf_op jit(solution)/shard_map/first_frame/pallas_call | solution.py:374
  17.3 0.1 collective-permute-start.2
  17.3 1.6 %collective-permute-start.1 = (f32[8,128]{1,0:T(8,128)S(1)}, f32[8,128]{1,0:T(8,128)S(1)}, u32[]{:S(2)}, u32[]{:S(2)}) collective-permute-start(f32[8,128]{1,0:T(8,128)S(1)} %get-tuple-element.22.refs_0_), channel_id=1, source_target_pairs={{0,16},{8,24},{16,0},{24,8},{1,17},{9,25},{17,1},{25,9},{2,18},{10... | collective-permute-start | bytes 12296 | tf_op jit(solution)/shard_map/ppermute | solution.py:431
  18.9 0.3 collective-permute-start
  19.2 1.2 %collective-permute-done.2.refs_3_ = f32[8,128]{1,0:T(8,128)S(1)} collective-permute-done((f32[8,128]{1,0:T(8,128)S(1)}, f32[8,128]{1,0:T(8,128)S(1)}, u32[]{:S(2)}, u32[]{:S(2)}) %collective-permute-start.2) | collective-permute-done | bytes 4128 | tf_op jit(solution)/shard_map/ppermute | solution.py:431
  20.4 0.7 %collective-permute-done.1.refs_2_ = f32[8,128]{1,0:T(8,128)S(1)} collective-permute-done((f32[8,128]{1,0:T(8,128)S(1)}, f32[8,128]{1,0:T(8,128)S(1)}, u32[]{:S(2)}, u32[]{:S(2)}) %collective-permute-start.1) | collective-permute-done | bytes 4128 | tf_op jit(solution)/shard_map/ppermute | solution.py:431
  21.0 0.0 collective-permute-done.refs_1_
  21.0 0.8 %commands.2 = bf16[32,2,640]{2,1,0:T(2,128)(2,1)S(1)} custom-call(f32[8,128]{1,0:T(8,128)S(1)} %get-tuple-element.22.refs_0_, f32[8,128]{1,0:T(8,128)S(1)} %collective-permute-done.refs_1_, f32[8,128]{1,0:T(8,128)S(1)} %collective-permute-done.1.refs_2_, f32[8,128]{1,0:T(8,128)S(1)} %collective-permute-done.2.refs_3_, ...), custom_call_target="tpu_custom_call" | custom-call | tf_op jit(solution)/shard_map/commands/pallas_call | solution.py:374
  21.8 9.1 %all_to_all.15.parts_ref = bf16[32,2,640]{2,1,0:T(2,128)(2,1)S(1)} all-to-all(bf16[32,2,640]{2,1,0:T(2,128)(2,1)S(1)} %commands.2), channel_id=1, replica_groups=mesh['case'=4,'mod'=8] {'case','mod'}, dimensions={0} | all-to-all | bytes 163840 | tf_op jit(solution)/shard_map/all_to_all | solution.py:436
  31.0 2.5 %next_frame.1 = (f32[64,512]{1,0:T(8,128)S(1)}, f32[8,128]{1,0:T(8,128)S(1)}, f32[4,2,640]{2,1,0:T(2,128)S(1)}, bf16[512,1024]{1,0:T(8,128)(2,1)S(1)}) custom-call(bf16[32,2,640]{2,1,0:T(2,128)(2,1)S(1)} %all_to_all.15.parts_ref, f32[2,8,256]{2,1,0:T(8,128)S(1)} %get-tuple-element.25.tilt_ref, s32[40,128]{1,0:T(8,128)S(1)} %get-tuple-element.26.cells_ref, ...), custom_call_target="tpu_custom_call" | custom-call | tf_op jit(solution)/shard_map/next_frame/pallas_call | solution.py:374
  33.5 0.3 collective-permute-start.5
  33.8 1.5 %collective-permute-start.4 = (f32[8,128]{1,0:T(8,128)S(1)}, f32[8,128]{1,0:T(8,128)S(1)}, u32[]{:S(2)}, u32[]{:S(2)}) collective-permute-start(f32[8,128]{1,0:T(8,128)S(1)} %get-tuple-element.30.refs_0_), channel_id=1, source_target_pairs={{0,16},{8,24},{16,0},{24,8},{1,17},{9,25},{17,1},{25,9},{2,18},{10... | collective-permute-start | bytes 12296 | tf_op jit(solution)/shard_map/ppermute | solution.py:431
  35.3 0.1 collective-permute-start.3
  35.5 1.1 %collective-permute-done.5.refs_3_ = f32[8,128]{1,0:T(8,128)S(1)} collective-permute-done((f32[8,128]{1,0:T(8,128)S(1)}, f32[8,128]{1,0:T(8,128)S(1)}, u32[]{:S(2)}, u32[]{:S(2)}) %collective-permute-start.5) | collective-permute-done | bytes 4128 | tf_op jit(solution)/shard_map/ppermute | solution.py:431
  36.6 0.8 %collective-permute-done.4.refs_2_ = f32[8,128]{1,0:T(8,128)S(1)} collective-permute-done((f32[8,128]{1,0:T(8,128)S(1)}, f32[8,128]{1,0:T(8,128)S(1)}, u32[]{:S(2)}, u32[]{:S(2)}) %collective-permute-start.4) | collective-permute-done | bytes 4128 | tf_op jit(solution)/shard_map/ppermute | solution.py:431
  37.4 0.0 collective-permute-done.3.refs_1_
  37.5 0.8 %commands.3 = bf16[32,2,640]{2,1,0:T(2,128)(2,1)S(1)} custom-call(f32[8,128]{1,0:T(8,128)S(1)} %get-tuple-element.30.refs_0_, f32[8,128]{1,0:T(8,128)S(1)} %collective-permute-done.3.refs_1_, f32[8,128]{1,0:T(8,128)S(1)} %collective-permute-done.4.refs_2_, f32[8,128]{1,0:T(8,128)S(1)} %collective-permute-done.5.refs_3_, ...), custom_call_target="tpu_custom_call" | custom-call | tf_op jit(solution)/shard_map/commands/pallas_call | solution.py:374
  38.3 9.8 %all_to_all.16.parts_ref = bf16[32,2,640]{2,1,0:T(2,128)(2,1)S(1)} all-to-all(bf16[32,2,640]{2,1,0:T(2,128)(2,1)S(1)} %commands.3), channel_id=1, replica_groups=mesh['case'=4,'mod'=8] {'case','mod'}, dimensions={0} | all-to-all | bytes 163840 | tf_op jit(solution)/shard_map/all_to_all | solution.py:436
  48.0 0.7 %total.1 = (f32[1,5120]{1,0:T(1,128)}, f32[64,512]{1,0:T(8,128)}) custom-call(bf16[32,2,640]{2,1,0:T(2,128)(2,1)S(1)} %all_to_all.16.parts_ref, f32[4,2,640]{2,1,0:T(2,128)S(1)} %get-tuple-element.32.total_ref, f32[64,512]{1,0:T(8,128)S(1)} %get-tuple-element.33.frame_ref), custom_call_target="tpu_custom_call" | custom-call | tf_op jit(solution)/shard_map/total/pallas_call | solution.py:374
Async XLA Ops:
  1.9 13.6 %all-to-all-start = ((f32[8,1,128]{2,1,0:T(1,128)}), f32[8,1,128]{2,1,0:T(1,128)S(1)}, u32[]{:S(2)}, u32[]{:S(2)}) async-start(f32[8,1,128]{2,1,0:T(1,128)} %spread.1), calls=%async_computation | async-start | bytes 8192 | tf_op jit(solution)/shard_map/modulation_angles/all_to_all | solution.py:398
  17.3 3.1 %collective-permute-start.2 = (f32[8,128]{1,0:T(8,128)S(1)}, f32[8,128]{1,0:T(8,128)S(1)}, u32[]{:S(2)}, u32[]{:S(2)}) collective-permute-start(f32[8,128]{1,0:T(8,128)S(1)} %get-tuple-element.22.refs_0_), channel_id=1, source_target_pairs={{0,24},{8,16},{16,8},{24,0},{1,25},{9,17},{17,9},{25,1},{2,26},{10... | collective-permute-start | bytes 12296 | tf_op jit(solution)/shard_map/ppermute | solution.py:431
  17.3 3.7 %collective-permute-start.1 = (f32[8,128]{1,0:T(8,128)S(1)}, f32[8,128]{1,0:T(8,128)S(1)}, u32[]{:S(2)}, u32[]{:S(2)}) collective-permute-start(f32[8,128]{1,0:T(8,128)S(1)} %get-tuple-element.22.refs_0_), channel_id=1, source_target_pairs={{0,16},{8,24},{16,0},{24,8},{1,17},{9,25},{17,1},{25,9},{2,18},{10... | collective-permute-start | bytes 12296 | tf_op jit(solution)/shard_map/ppermute | solution.py:431
  18.9 2.1 %collective-permute-start = (f32[8,128]{1,0:T(8,128)S(1)}, f32[8,128]{1,0:T(8,128)S(1)}, u32[]{:S(2)}, u32[]{:S(2)}) collective-permute-start(f32[8,128]{1,0:T(8,128)S(1)} %get-tuple-element.22.refs_0_), channel_id=1, source_target_pairs={{0,8},{8,0},{16,24},{24,16},{1,9},{9,1},{17,25},{25,17},{2,10},{10... | collective-permute-start | bytes 12296 | tf_op jit(solution)/shard_map/ppermute | solution.py:431
  33.5 3.1 %collective-permute-start.5 = (f32[8,128]{1,0:T(8,128)S(1)}, f32[8,128]{1,0:T(8,128)S(1)}, u32[]{:S(2)}, u32[]{:S(2)}) collective-permute-start(f32[8,128]{1,0:T(8,128)S(1)} %get-tuple-element.30.refs_0_), channel_id=1, source_target_pairs={{0,24},{8,16},{16,8},{24,0},{1,25},{9,17},{17,9},{25,1},{2,26},{10... | collective-permute-start | bytes 12296 | tf_op jit(solution)/shard_map/ppermute | solution.py:431
  33.8 3.6 %collective-permute-start.4 = (f32[8,128]{1,0:T(8,128)S(1)}, f32[8,128]{1,0:T(8,128)S(1)}, u32[]{:S(2)}, u32[]{:S(2)}) collective-permute-start(f32[8,128]{1,0:T(8,128)S(1)} %get-tuple-element.30.refs_0_), channel_id=1, source_target_pairs={{0,16},{8,24},{16,0},{24,8},{1,17},{9,25},{17,1},{25,9},{2,18},{10... | collective-permute-start | bytes 12296 | tf_op jit(solution)/shard_map/ppermute | solution.py:431
  35.3 2.1 %collective-permute-start.3 = (f32[8,128]{1,0:T(8,128)S(1)}, f32[8,128]{1,0:T(8,128)S(1)}, u32[]{:S(2)}, u32[]{:S(2)}) collective-permute-start(f32[8,128]{1,0:T(8,128)S(1)} %get-tuple-element.30.refs_0_), channel_id=1, source_target_pairs={{0,8},{8,0},{16,24},{24,16},{1,9},{9,1},{17,25},{25,17},{2,10},{10... | collective-permute-start | bytes 12296 | tf_op jit(solution)/shard_map/ppermute | solution.py:431

commit v8 on v7

--- a/solution.py
+++ b/solution.py
@@ -122,8 +122,8 @@
 
 def prepare_kernel(
     phase_hbm, amp_hbm, map_hbm, gxt_hbm, gyt_hbm, rows_hbm, full_hbm, recon_hbm,
-    field_ref, rows_ref, full_ref, cells_ref, gx_ref, gy_ref, recon_ref,
-    phase_ref, amp_ref, map_ref, gxt_ref, gyt_ref, floats, semaphores,
+    field_ref, rows_ref, full_ref, cells_ref, gx_ref, gy_ref, recon_ref, phase_ref, amp_ref,
+    map_ref, gxt_ref, gyt_ref, floats, semaphores,
 ):
     actuators, gxt, gyt, phase, amp, rows, full, recon = copies(
         [
@@ -253,43 +253,30 @@
 
 
 def add_commands(parts_ref, total_ref, out_ref):
-    cases = out_ref.shape[0]
-    each = parts_ref.shape[0] // cases
-    for case in range(cases):
-        sums = jnp.sum(parts_ref[case * each : (case + 1) * each].astype(jnp.float32), 0)
-        out_ref[case] = loop_gain * sums if total_ref is None else total_ref[case] + loop_gain * sums
+    messages, pieces, _ = parts_ref.shape
+    cases = out_ref.shape[0] // pieces
+    each = messages // cases
+    sums = [jnp.sum(parts_ref[i * each : (i + 1) * each].astype(jnp.float32), 0) for i in range(cases)]
+    sums = loop_gain * jnp.concatenate(sums, 0)
+    out_ref[...] = sums if total_ref is None else total_ref[...] + sums
 
 
 def later_kernel(
-    parts_ref, tilt_ref, cells_ref, gx_ref, gy_ref, left_ref, full_ref, phase_hbm, amp_hbm, pixels_hbm, recon_hbm,
+    parts_ref, tilt_ref, cells_ref, gx_ref, gy_ref, left_ref, full_ref, phase_ref, amp_ref, pixels_hbm, recon_hbm,
     *refs
 ):
-    old_total, refs = (None, refs) if len(refs) == 8 else (refs[0], refs[1:])
-    frame_ref, signal_ref, new_total_ref, recon_ref, phase_ref, amp_ref, pixels_ref, semaphores = refs
-    phase, amp, pixels, recon = copies(
-        [
-            (phase_hbm, phase_ref), (amp_hbm, amp_ref), (pixels_hbm, pixels_ref),
-            (recon_hbm.at[recon_hbm.shape[0] - recon_ref.shape[0] :], recon_ref),
-        ],
-        semaphores,
+    old_total, refs = (None, refs) if len(refs) == 6 else (refs[0], refs[1:])
+    frame_ref, signal_ref, new_total_ref, recon_ref, pixels_ref, semaphores = refs
+    pixels, recon = copies(
+        [(pixels_hbm, pixels_ref), (recon_hbm.at[recon_hbm.shape[0] - recon_ref.shape[0] :], recon_ref)], semaphores
     )
     add_commands(parts_ref, old_total, new_total_ref)
-    cases, pieces, width = new_total_ref.shape
-    per_piece = width // LANES
-
-    def row(i):
-        column = (i % per_piece) * LANES
-        piece = i // per_piece
-        return new_total_ref[piece // pieces, piece % pieces : piece % pieces + 1, column : column + LANES]
-
-    grid = look_up(cases * pieces * per_piece, row, cells_ref[...])
+    grid = look_up(*runs(new_total_ref), cells_ref[...])
     surface = mirror_surface(grid, gx_ref, gy_ref)
-    phase.wait()
-    amp.wait()
+    pixels.wait()
     field = field_matrix(*field_parts(phase_ref[...] - surface, amp_ref[...]))
 
     detect(left_ref[...], field, full_ref, tilt_ref[0], tilt_ref[1], frame_ref)
-    pixels.wait()
     signal_ref[...] = read_signals(frame_ref, pixels_ref[...])
     recon.wait()
 
@@ -330,11 +317,9 @@
     frame_out = pltpu.make_async_copy(frame_ref, frame_hbm, semaphores.at[0])
     frame_out.start()
     add_commands(parts_ref, total_ref, sums_ref)
-    cases, pieces, width = sums_ref.shape
-    for case in range(cases):
-        for i in range(pieces):
-            start = (case * pieces + i) * width
-            out_ref[:, start : start + width] = sums_ref[case, i : i + 1, :]
+    rows, width = sums_ref.shape
+    for i in range(rows):
+        out_ref[:, i * width : (i + 1) * width] = sums_ref[i : i + 1, :]
     total_out = pltpu.make_async_copy(out_ref, total_hbm, semaphores.at[1])
     total_out.start()
     frame_out.wait()
@@ -400,7 +385,7 @@
     recon_early = block // LANES * 6 // 10 * LANES
     late_shape = shape((block - recon_early, recon.shape[1]), bf16)
     map_shape = (act_map.shape[0] // LANES, LANES)
-    field, rows, full, cells, gx_parts, gy_parts, recon_first = call(
+    field, rows, full, cells, gx_parts, gy_parts, recon_first, phase, amplitude = call(
         prepare_kernel,
         "prepare",
         (
@@ -411,11 +396,12 @@
             shape((pupil, 4 * grid_rows), bf16),
             shape((pupil, 3 * grid_columns), bf16),
             shape((recon_early, recon.shape[1]), bf16),
+            shape(screen.shape, f32),
+            shape(pupil_amp.shape, f32),
         ),
-        (vmem,) * 7,
+        (vmem,) * 9,
         [hbm] * 8,
-        like(screen, pupil_amp)
-        + [
+        [
             pltpu.VMEM(map_shape, jnp.int32),
             pltpu.VMEM(gx.shape[::-1], f32),
             pltpu.VMEM(gy.shape[::-1], f32),
@@ -437,7 +423,7 @@
 
     frame_shape = shape((row_count, length), f32)
     signal_shape = shape((signal_rows, LANES), f32)
-    total_shape = shape((cases, pieces, width), f32)
+    total_shape = shape((cases * pieces, width), f32)
     left_shape = shape((count * row_count, 2 * pupil), bf16)
     signal, tilts, left, recon_late = call(
         first_kernel,
@@ -451,15 +437,14 @@
     totals = ()
     for iteration in range(1, STEPS):
         parts = commands(signal, recon_late)
-        held = (screen, pupil_amp, pixels)
         frame, signal, *totals, recon_late = call(
             later_kernel,
             "next_frame",
             (frame_shape, signal_shape, total_shape, late_shape),
             (vmem, vmem, vmem, vmem),
-            [vmem] * 7 + [hbm] * 4 + [vmem] * len(totals),
-            like(*held) + [done(4)],
-            parts, tilts, cells, gx_parts, gy_parts, left, full, *held, recon, *totals,
+            [vmem] * 9 + [hbm] * 2 + [vmem] * len(totals),
+            like(pixels) + [done(2)],
+            parts, tilts, cells, gx_parts, gy_parts, left, full, phase, amplitude, pixels, recon, *totals,
         )
     parts = commands(signal, recon_late)
     command_shape = shape((1, cases * block), f32)

time: 49 us -> 48.8 us (level)
  no operation moved by 1% of the time
where the time goes in v8:
time: 48.8 us; the launch traced here: 48.6 us
  blocking collectives  18.9 us (39%)
  starting transfers between devices  11.1 us (23%)
  Pallas kernels  8.94 us (18%)
  waiting for transfers between devices  8.23 us (17%)
  between operations  1.33 us (3%)
    all_to_all x2, blocking collectives, commands(): return lax.all_to_all(partial, ('case', 'mod'), 0, 0, tiled=True)  18.9 us
    pallas_call x7, Pallas kernels, call(): pl.pallas_call(kernel, out_shape=outs, in_specs=in_specs, out_specs=out_s...  8.94 us
    all_to_all x1, starting transfers between devices, body(): lax.all_to_all(angles, 'mod', 0, 0, tiled=True).reshape(count, LANES)  7.25 us
    all_to_all x1, waiting for transfers between devices, body(): lax.all_to_all(angles, 'mod', 0, 0, tiled=True).reshape(count, LANES)  4.45 us
    ppermute x6, starting transfers between devices, commands(): lax.ppermute(signal, 'case', [(i, i ^ j) for i in range(cases)])  3.88 us
    ppermute x6, waiting for transfers between devices, commands(): lax.ppermute(signal, 'case', [(i, i ^ j) for i in range(cases)])  3.79 us
  transfers between devices with their start and end apart: 7, of which 5 were waited for; matrix products, arithmetic and copies ran while one was open for 0% of the time, Pallas kernels for 4%

profile of v8, /device:TPU:0, one launch (start us, length us, event | category | flops | bytes accessed | tf_op | source)
XLA Modules:
  0.0 48.6 jit_solution(9452883756232420785)
XLA Ops:
  1.3 0.6 %spread.1 = f32[8,1,128]{2,1,0:T(1,128)} custom-call(s32[1]{0:T(128)S(6)} %copy.13.point_ref), custom_call_target="tpu_custom_call" | custom-call | tf_op jit(solution)/shard_map/modulation_angles/spread/pallas_call | solution.py:359
  1.9 7.3 %all-to-all-start = ((f32[8,1,128]{2,1,0:T(1,128)}), f32[8,1,128]{2,1,0:T(1,128)S(1)}, u32[]{:S(2)}, u32[]{:S(2)}) async-start(f32[8,1,128]{2,1,0:T(1,128)} %spread.1), calls=%async_computation | async-start | bytes 8192 | tf_op jit(solution)/shard_map/modulation_angles/all_to_all | solution.py:383
  9.1 1.9 %prepare.1 = (bf16[256,512]{1,0:T(8,128)(2,1)S(1)}, f32[64,512]{1,0:T(8,128)S(1)}, bf16[512,512]{1,0:T(8,128)(2,1)S(1)}, s32[40,128]{1,0:T(8,128)S(1)}, bf16[256...) custom-call(f32[256,256]{1,0:T(8,128)} %bitcast.8, ...), custom_call_target="tpu_custom_call" | custom-call | tf_op jit(solution)/shard_map/prepare/pallas_call | solution.py:359
  11.1 4.4 %all-to-all-done = f32[8,1,128]{2,1,0:T(1,128)S(1)} async-done(((f32[8,1,128]{2,1,0:T(1,128)}), f32[8,1,128]{2,1,0:T(1,128)S(1)}, u32[]{:S(2)}, u32[]{:S(2)}) %all-to-all-start) | async-done | bytes 4128 | tf_op jit(solution)/shard_map/modulation_angles/all_to_all | solution.py:383
  15.5 1.7 %first_frame.1 = (f32[8,128]{1,0:T(8,128)S(1)}, f32[2,8,256]{2,1,0:T(8,128)S(1)}, bf16[512,512]{1,0:T(8,128)(2,1)S(1)}, bf16[512,1024]{1,0:T(8,128)(2,1)S(1)}) custom-call(f32[8,128]{1,0:T(8,128)S(1)} %bitcast.7, bf16[256,512]{1,0:T(8,128)(2,1)S(1)} %get-tuple-element.21.field_ref, f32[64,512]{1,0:T(8,128)S(1)} %get-tuple-element.22.rows_ref, ...), custom_call_target="tpu_custom_call" | custom-call | tf_op jit(solution)/shard_map/first_frame/pallas_call | solution.py:359
  17.3 0.1 collective-permute-start.2
  17.3 1.6 %collective-permute-start.1 = (f32[8,128]{1,0:T(8,128)S(1)}, f32[8,128]{1,0:T(8,128)S(1)}, u32[]{:S(2)}, u32[]{:S(2)}) collective-permute-start(f32[8,128]{1,0:T(8,128)S(1)} %get-tuple-element.24.refs_0_), channel_id=1, source_target_pairs={{0,16},{8,24},{16,0},{24,8},{1,17},{9,25},{17,1},{25,9},{2,18},{10... | collective-permute-start | bytes 12296 | tf_op jit(solution)/shard_map/ppermute | solution.py:417
  18.9 0.3 collective-permute-start
  19.2 1.2 %collective-permute-done.2.refs_3_ = f32[8,128]{1,0:T(8,128)S(1)} collective-permute-done((f32[8,128]{1,0:T(8,128)S(1)}, f32[8,128]{1,0:T(8,128)S(1)}, u32[]{:S(2)}, u32[]{:S(2)}) %collective-permute-start.2) | collective-permute-done | bytes 4128 | tf_op jit(solution)/shard_map/ppermute | solution.py:417
  20.4 0.7 %collective-permute-done.1.refs_2_ = f32[8,128]{1,0:T(8,128)S(1)} collective-permute-done((f32[8,128]{1,0:T(8,128)S(1)}, f32[8,128]{1,0:T(8,128)S(1)}, u32[]{:S(2)}, u32[]{:S(2)}) %collective-permute-start.1) | collective-permute-done | bytes 4128 | tf_op jit(solution)/shard_map/ppermute | solution.py:417
  21.0 0.0 collective-permute-done.refs_1_
  21.0 0.8 %commands.2 = bf16[32,2,640]{2,1,0:T(2,128)(2,1)S(1)} custom-call(f32[8,128]{1,0:T(8,128)S(1)} %get-tuple-element.24.refs_0_, f32[8,128]{1,0:T(8,128)S(1)} %collective-permute-done.refs_1_, f32[8,128]{1,0:T(8,128)S(1)} %collective-permute-done.1.refs_2_, f32[8,128]{1,0:T(8,128)S(1)} %collective-permute-done.2.refs_3_, ...), custom_call_target="tpu_custom_call" | custom-call | tf_op jit(solution)/shard_map/commands/pallas_call | solution.py:359
  21.8 9.1 %all_to_all.15.parts_ref = bf16[32,2,640]{2,1,0:T(2,128)(2,1)S(1)} all-to-all(bf16[32,2,640]{2,1,0:T(2,128)(2,1)S(1)} %commands.2), channel_id=1, replica_groups=mesh['case'=4,'mod'=8] {'case','mod'}, dimensions={0} | all-to-all | bytes 163840 | tf_op jit(solution)/shard_map/all_to_all | solution.py:422
  31.0 2.3 %next_frame.1 = (f32[64,512]{1,0:T(8,128)S(1)}, f32[8,128]{1,0:T(8,128)S(1)}, f32[8,640]{1,0:T(8,128)S(1)}, bf16[512,1024]{1,0:T(8,128)(2,1)S(1)}) custom-call(bf16[32,2,640]{2,1,0:T(2,128)(2,1)S(1)} %all_to_all.15.parts_ref, f32[2,8,256]{2,1,0:T(8,128)S(1)} %get-tuple-element.27.tilt_ref, s32[40,128]{1,0:T(8,128)S(1)} %get-tuple-element.28.cells_ref, ...), custom_call_target="tpu_custom_call" | custom-call | tf_op jit(solution)/shard_map/next_frame/pallas_call | solution.py:359
  33.3 0.3 collective-permute-start.5
  33.6 1.5 %collective-permute-start.4 = (f32[8,128]{1,0:T(8,128)S(1)}, f32[8,128]{1,0:T(8,128)S(1)}, u32[]{:S(2)}, u32[]{:S(2)}) collective-permute-start(f32[8,128]{1,0:T(8,128)S(1)} %get-tuple-element.34.refs_0_), channel_id=1, source_target_pairs={{0,16},{8,24},{16,0},{24,8},{1,17},{9,25},{17,1},{25,9},{2,18},{10... | collective-permute-start | bytes 12296 | tf_op jit(solution)/shard_map/ppermute | solution.py:417
  35.1 0.1 collective-permute-start.3
  35.3 1.1 %collective-permute-done.5.refs_3_ = f32[8,128]{1,0:T(8,128)S(1)} collective-permute-done((f32[8,128]{1,0:T(8,128)S(1)}, f32[8,128]{1,0:T(8,128)S(1)}, u32[]{:S(2)}, u32[]{:S(2)}) %collective-permute-start.5) | collective-permute-done | bytes 4128 | tf_op jit(solution)/shard_map/ppermute | solution.py:417
  36.4 0.8 %collective-permute-done.4.refs_2_ = f32[8,128]{1,0:T(8,128)S(1)} collective-permute-done((f32[8,128]{1,0:T(8,128)S(1)}, f32[8,128]{1,0:T(8,128)S(1)}, u32[]{:S(2)}, u32[]{:S(2)}) %collective-permute-start.4) | collective-permute-done | bytes 4128 | tf_op jit(solution)/shard_map/ppermute | solution.py:417
  37.2 0.0 collective-permute-done.3.refs_1_
  37.3 0.8 %commands.3 = bf16[32,2,640]{2,1,0:T(2,128)(2,1)S(1)} custom-call(f32[8,128]{1,0:T(8,128)S(1)} %get-tuple-element.34.refs_0_, f32[8,128]{1,0:T(8,128)S(1)} %collective-permute-done.3.refs_1_, f32[8,128]{1,0:T(8,128)S(1)} %collective-permute-done.4.refs_2_, f32[8,128]{1,0:T(8,128)S(1)} %collective-permute-done.5.refs_3_, ...), custom_call_target="tpu_custom_call" | custom-call | tf_op jit(solution)/shard_map/commands/pallas_call | solution.py:359
  38.1 9.8 %all_to_all.16.parts_ref = bf16[32,2,640]{2,1,0:T(2,128)(2,1)S(1)} all-to-all(bf16[32,2,640]{2,1,0:T(2,128)(2,1)S(1)} %commands.3), channel_id=1, replica_groups=mesh['case'=4,'mod'=8] {'case','mod'}, dimensions={0} | all-to-all | bytes 163840 | tf_op jit(solution)/shard_map/all_to_all | solution.py:422
  47.8 0.7 %total.1 = (f32[1,5120]{1,0:T(1,128)}, f32[64,512]{1,0:T(8,128)}) custom-call(bf16[32,2,640]{2,1,0:T(2,128)(2,1)S(1)} %all_to_all.16.parts_ref, f32[8,640]{1,0:T(8,128)S(1)} %get-tuple-element.36.total_ref, f32[64,512]{1,0:T(8,128)S(1)} %get-tuple-element.37.frame_ref), custom_call_target="tpu_custom_call" | custom-call | tf_op jit(solution)/shard_map/total/pallas_call | solution.py:359
Async XLA Ops:
  1.9 13.6 %all-to-all-start = ((f32[8,1,128]{2,1,0:T(1,128)}), f32[8,1,128]{2,1,0:T(1,128)S(1)}, u32[]{:S(2)}, u32[]{:S(2)}) async-start(f32[8,1,128]{2,1,0:T(1,128)} %spread.1), calls=%async_computation | async-start | bytes 8192 | tf_op jit(solution)/shard_map/modulation_angles/all_to_all | solution.py:383
  17.3 3.1 %collective-permute-start.2 = (f32[8,128]{1,0:T(8,128)S(1)}, f32[8,128]{1,0:T(8,128)S(1)}, u32[]{:S(2)}, u32[]{:S(2)}) collective-permute-start(f32[8,128]{1,0:T(8,128)S(1)} %get-tuple-element.24.refs_0_), channel_id=1, source_target_pairs={{0,24},{8,16},{16,8},{24,0},{1,25},{9,17},{17,9},{25,1},{2,26},{10... | collective-permute-start | bytes 12296 | tf_op jit(solution)/shard_map/ppermute | solution.py:417
  17.3 3.7 %collective-permute-start.1 = (f32[8,128]{1,0:T(8,128)S(1)}, f32[8,128]{1,0:T(8,128)S(1)}, u32[]{:S(2)}, u32[]{:S(2)}) collective-permute-start(f32[8,128]{1,0:T(8,128)S(1)} %get-tuple-element.24.refs_0_), channel_id=1, source_target_pairs={{0,16},{8,24},{16,0},{24,8},{1,17},{9,25},{17,1},{25,9},{2,18},{10... | collective-permute-start | bytes 12296 | tf_op jit(solution)/shard_map/ppermute | solution.py:417
  18.9 2.1 %collective-permute-start = (f32[8,128]{1,0:T(8,128)S(1)}, f32[8,128]{1,0:T(8,128)S(1)}, u32[]{:S(2)}, u32[]{:S(2)}) collective-permute-start(f32[8,128]{1,0:T(8,128)S(1)} %get-tuple-element.24.refs_0_), channel_id=1, source_target_pairs={{0,8},{8,0},{16,24},{24,16},{1,9},{9,1},{17,25},{25,17},{2,10},{10... | collective-permute-start | bytes 12296 | tf_op jit(solution)/shard_map/ppermute | solution.py:417
  33.3 3.1 %collective-permute-start.5 = (f32[8,128]{1,0:T(8,128)S(1)}, f32[8,128]{1,0:T(8,128)S(1)}, u32[]{:S(2)}, u32[]{:S(2)}) collective-permute-start(f32[8,128]{1,0:T(8,128)S(1)} %get-tuple-element.34.refs_0_), channel_id=1, source_target_pairs={{0,24},{8,16},{16,8},{24,0},{1,25},{9,17},{17,9},{25,1},{2,26},{10... | collective-permute-start | bytes 12296 | tf_op jit(solution)/shard_map/ppermute | solution.py:417
  33.6 3.6 %collective-permute-start.4 = (f32[8,128]{1,0:T(8,128)S(1)}, f32[8,128]{1,0:T(8,128)S(1)}, u32[]{:S(2)}, u32[]{:S(2)}) collective-permute-start(f32[8,128]{1,0:T(8,128)S(1)} %get-tuple-element.34.refs_0_), channel_id=1, source_target_pairs={{0,16},{8,24},{16,0},{24,8},{1,17},{9,25},{17,1},{25,9},{2,18},{10... | collective-permute-start | bytes 12296 | tf_op jit(solution)/shard_map/ppermute | solution.py:417
  35.1 2.1 %collective-permute-start.3 = (f32[8,128]{1,0:T(8,128)S(1)}, f32[8,128]{1,0:T(8,128)S(1)}, u32[]{:S(2)}, u32[]{:S(2)}) collective-permute-start(f32[8,128]{1,0:T(8,128)S(1)} %get-tuple-element.34.refs_0_), channel_id=1, source_target_pairs={{0,8},{8,0},{16,24},{24,16},{1,9},{9,1},{17,25},{25,17},{2,10},{10... | collective-permute-start | bytes 12296 | tf_op jit(solution)/shard_map/ppermute | solution.py:417

commit v9 on v8

--- a/solution.py
+++ b/solution.py
@@ -233,14 +233,12 @@
 
 
 def first_kernel(
-    angles_ref, field_ref, rows_ref, full_ref, pixels_hbm, recon_hbm, signal_ref, tilt_ref, left_ref, recon_ref,
+    angles_ref, field_ref, rows_ref, full_ref, pixels_hbm, signal_ref, tilt_ref, left_ref,
     pixels_ref, frame_ref, semaphores,
 ):
     length = frame_ref.shape[1]
     pupil = length // 2
-    pixels, recon = copies(
-        [(pixels_hbm, pixels_ref), (recon_hbm.at[recon_hbm.shape[0] - recon_ref.shape[0] :], recon_ref)], semaphores
-    )
+    (pixels,) = copies([(pixels_hbm, pixels_ref)], semaphores)
     tilts = tilt_factors(angles_ref, pupil, length)
     tilt_ref[0], tilt_ref[1] = tilts[2:]
     left = left_rows(rows_ref[...], *tilts[:2])
@@ -249,7 +247,10 @@
     detect(left, field, full_ref, *tilts[2:], frame_ref)
     pixels.wait()
     signal_ref[...] = read_signals(frame_ref, pixels_ref[...])
-    recon.wait()
+
+
+def fetch_kernel(tilt_ref, recon_hbm, recon_ref, semaphores):
+    copies([(recon_hbm.at[recon_hbm.shape[0] - recon_ref.shape[0] :], recon_ref)], semaphores)[0].wait()
 
 
 def add_commands(parts_ref, total_ref, out_ref):
@@ -347,7 +348,7 @@
     vmem = pl.BlockSpec(memory_space=pltpu.VMEM)
     smem = pl.BlockSpec(memory_space=pltpu.SMEM)
 
-    def call(kernel, name, outs, out_specs, in_specs, scratch, *operands):
+    def call(kernel, name, outs, out_specs, in_specs, scratch, *operands, cost=None):
         operands = [
             pltpu.with_memory_space_constraint(operand, pltpu.HBM) if spec is hbm else operand
             for operand, spec in zip(operands, in_specs)
@@ -363,6 +364,7 @@
             out_specs=out_specs,
             scratch_shapes=scratch,
             compiler_params=pltpu.CompilerParams(vmem_limit_bytes=VMEM_LIMIT),
+            cost_estimate=cost,
             name=name,
         )(*operands)
 
@@ -425,15 +427,16 @@
     signal_shape = shape((signal_rows, LANES), f32)
     total_shape = shape((cases * pieces, width), f32)
     left_shape = shape((count * row_count, 2 * pupil), bf16)
-    signal, tilts, left, recon_late = call(
+    signal, tilts, left = call(
         first_kernel,
         "first_frame",
-        (signal_shape, shape((2, count, pupil), f32), left_shape, late_shape),
-        (vmem, vmem, vmem, vmem),
-        [vmem, vmem, vmem, vmem, hbm, hbm],
-        like(pixels, frame_shape) + [done(2)],
-        angles, field, rows, full, pixels, recon,
-    )
+        (signal_shape, shape((2, count, pupil), f32), left_shape),
+        (vmem, vmem, vmem),
+        [vmem, vmem, vmem, vmem, hbm],
+        like(pixels, frame_shape) + [done(1)],
+        angles, field, rows, full, pixels,
+    )
+    recon_late = call(fetch_kernel, "fetch", late_shape, vmem, [vmem, hbm], [done(1)], tilts, recon, cost=pl.CostEstimate(flops=0, bytes_accessed=late_shape.size * 4, transcendentals=0))
     totals = ()
     for iteration in range(1, STEPS):
         parts = commands(signal, recon_late)

time: 48.8 us -> 48.5 us (level)
  waiting for transfers between devices: 8.23 us -> 6.99 us
  Pallas kernels: 8.94 us -> 9.83 us
    ppermute x6, waiting for transfers between devices: 3.79 us -> 2.54 us  [commands(): lax.ppermute(signal, 'case', [(i, i ^ j) for i in range(cases)])]
    pallas_call x7 -> x8, Pallas kernels: 8.94 us -> 9.83 us  [call(): pl.pallas_call(kernel, out_shape=outs, in_specs=in_specs, out_specs=out_s...]
  transfers between devices with their start and end apart: 7 -> 7, of which waited for: 5 -> 4; matrix products, arithmetic and copies ran while one was open for 0% -> 0% of each run, Pallas kernels for 4% -> 7%
where the time goes in v9:
time: 48.5 us; the launch traced here: 48.2 us
  blocking collectives  18.9 us (39%)
  starting transfers between devices  11.1 us (23%)
  Pallas kernels  9.83 us (20%)
  waiting for transfers between devices  6.99 us (14%)
  between operations  1.35 us (3%)
    all_to_all x2, blocking collectives, commands(): return lax.all_to_all(partial, ('case', 'mod'), 0, 0, tiled=True)  18.9 us
    pallas_call x8, Pallas kernels, call(): pl.pallas_call(kernel, out_shape=outs, in_specs=in_specs, out_specs=out_s...  9.83 us
    all_to_all x1, starting transfers between devices, body(): lax.all_to_all(angles, 'mod', 0, 0, tiled=True).reshape(count, LANES)  7.25 us
    all_to_all x1, waiting for transfers between devices, body(): lax.all_to_all(angles, 'mod', 0, 0, tiled=True).reshape(count, LANES)  4.45 us
    ppermute x6, starting transfers between devices, commands(): lax.ppermute(signal, 'case', [(i, i ^ j) for i in range(cases)])  3.88 us
    ppermute x6, waiting for transfers between devices, commands(): lax.ppermute(signal, 'case', [(i, i ^ j) for i in range(cases)])  2.54 us
  transfers between devices with their start and end apart: 7, of which 4 were waited for; matrix products, arithmetic and copies ran while one was open for 0% of the time, Pallas kernels for 7%

profile of v9, /device:TPU:0, one launch (start us, length us, event | category | flops | bytes accessed | tf_op | source)
XLA Modules:
  0.0 48.2 jit_solution(16012326187067457090)
XLA Ops:
  1.3 0.6 %spread.1 = f32[8,1,128]{2,1,0:T(1,128)} custom-call(s32[1]{0:T(128)S(6)} %copy.13.point_ref), custom_call_target="tpu_custom_call" | custom-call | tf_op jit(solution)/shard_map/modulation_angles/spread/pallas_call | solution.py:360
  1.9 7.3 %all-to-all-start = ((f32[8,1,128]{2,1,0:T(1,128)}), f32[8,1,128]{2,1,0:T(1,128)S(1)}, u32[]{:S(2)}, u32[]{:S(2)}) async-start(f32[8,1,128]{2,1,0:T(1,128)} %spread.1), calls=%async_computation | async-start | bytes 8192 | tf_op jit(solution)/shard_map/modulation_angles/all_to_all | solution.py:385
  9.1 1.9 %prepare.1 = (bf16[256,512]{1,0:T(8,128)(2,1)S(1)}, f32[64,512]{1,0:T(8,128)S(1)}, bf16[512,512]{1,0:T(8,128)(2,1)S(1)}, s32[40,128]{1,0:T(8,128)S(1)}, bf16[256...) custom-call(f32[256,256]{1,0:T(8,128)} %bitcast.8, ...), custom_call_target="tpu_custom_call" | custom-call | tf_op jit(solution)/shard_map/prepare/pallas_call | solution.py:360
  11.1 4.4 %all-to-all-done = f32[8,1,128]{2,1,0:T(1,128)S(1)} async-done(((f32[8,1,128]{2,1,0:T(1,128)}), f32[8,1,128]{2,1,0:T(1,128)S(1)}, u32[]{:S(2)}, u32[]{:S(2)}) %all-to-all-start) | async-done | bytes 4128 | tf_op jit(solution)/shard_map/modulation_angles/all_to_all | solution.py:385
  15.5 1.4 %first_frame.1 = (f32[8,128]{1,0:T(8,128)S(1)}, f32[2,8,256]{2,1,0:T(8,128)S(1)}, bf16[512,512]{1,0:T(8,128)(2,1)S(1)}) custom-call(f32[8,128]{1,0:T(8,128)S(1)} %bitcast.7, bf16[256,512]{1,0:T(8,128)(2,1)S(1)} %get-tuple-element.20.field_ref, f32[64,512]{1,0:T(8,128)S(1)} %get-tuple-element.21.rows_ref, bf16[512,512]{1,0:T(8,128)(2,1)S(1)} %get-tuple-element.22.full_ref, ...), custom_call_target="tpu_custom_call" | custom-call | tf_op jit(solution)/shard_map/first_frame/pallas_call | solution.py:360
  16.9 0.1 collective-permute-start.2
  17.0 1.6 %collective-permute-start.1 = (f32[8,128]{1,0:T(8,128)S(1)}, f32[8,128]{1,0:T(8,128)S(1)}, u32[]{:S(2)}, u32[]{:S(2)}) collective-permute-start(f32[8,128]{1,0:T(8,128)S(1)} %get-tuple-element.23.refs_0_), channel_id=1, source_target_pairs={{0,16},{8,24},{16,0},{24,8},{1,17},{9,25},{17,1},{25,9},{2,18},{10... | collective-permute-start | bytes 12296 | tf_op jit(solution)/shard_map/ppermute | solution.py:419
  18.6 0.3 collective-permute-start
  18.8 1.2 %fetch.1.refs_5_ = bf16[512,1024]{1,0:T(8,128)(2,1)S(1)} custom-call(f32[2,8,256]{2,1,0:T(8,128)S(1)} %get-tuple-element.25.tilt_ref, bf16[1280,1024]{1,0:T(8,128)(2,1)} %recon_hbm.5), custom_call_target="tpu_custom_call" | custom-call | bytes 2097152 | tf_op jit(solution)/shard_map/fetch/pallas_call | solution.py:360
  20.1 0.0 collective-permute-done.2.refs_3_
  20.1 0.6 %collective-permute-done.1.refs_2_ = f32[8,128]{1,0:T(8,128)S(1)} collective-permute-done((f32[8,128]{1,0:T(8,128)S(1)}, f32[8,128]{1,0:T(8,128)S(1)}, u32[]{:S(2)}, u32[]{:S(2)}) %collective-permute-start.1) | collective-permute-done | bytes 4128 | tf_op jit(solution)/shard_map/ppermute | solution.py:419
  20.7 0.0 collective-permute-done.refs_1_
  20.7 0.8 %commands.2 = bf16[32,2,640]{2,1,0:T(2,128)(2,1)S(1)} custom-call(f32[8,128]{1,0:T(8,128)S(1)} %get-tuple-element.23.refs_0_, f32[8,128]{1,0:T(8,128)S(1)} %collective-permute-done.refs_1_, f32[8,128]{1,0:T(8,128)S(1)} %collective-permute-done.1.refs_2_, f32[8,128]{1,0:T(8,128)S(1)} %collective-permute-done.2.refs_3_, ...), custom_call_target="tpu_custom_call" | custom-call | tf_op jit(solution)/shard_map/commands/pallas_call | solution.py:360
  21.5 9.1 %all_to_all.15.parts_ref = bf16[32,2,640]{2,1,0:T(2,128)(2,1)S(1)} all-to-all(bf16[32,2,640]{2,1,0:T(2,128)(2,1)S(1)} %commands.2), channel_id=1, replica_groups=mesh['case'=4,'mod'=8] {'case','mod'}, dimensions={0} | all-to-all | bytes 163840 | tf_op jit(solution)/shard_map/all_to_all | solution.py:424
  30.6 2.3 %next_frame.1 = (f32[64,512]{1,0:T(8,128)S(1)}, f32[8,128]{1,0:T(8,128)S(1)}, f32[8,640]{1,0:T(8,128)S(1)}, bf16[512,1024]{1,0:T(8,128)(2,1)S(1)}) custom-call(bf16[32,2,640]{2,1,0:T(2,128)(2,1)S(1)} %all_to_all.15.parts_ref, f32[2,8,256]{2,1,0:T(8,128)S(1)} %get-tuple-element.25.tilt_ref, s32[40,128]{1,0:T(8,128)S(1)} %get-tuple-element.26.cells_ref, ...), custom_call_target="tpu_custom_call" | custom-call | tf_op jit(solution)/shard_map/next_frame/pallas_call | solution.py:360
  33.0 0.3 collective-permute-start.5
  33.3 1.5 %collective-permute-start.4 = (f32[8,128]{1,0:T(8,128)S(1)}, f32[8,128]{1,0:T(8,128)S(1)}, u32[]{:S(2)}, u32[]{:S(2)}) collective-permute-start(f32[8,128]{1,0:T(8,128)S(1)} %get-tuple-element.32.refs_0_), channel_id=1, source_target_pairs={{0,16},{8,24},{16,0},{24,8},{1,17},{9,25},{17,1},{25,9},{2,18},{10... | collective-permute-start | bytes 12296 | tf_op jit(solution)/shard_map/ppermute | solution.py:419
  34.8 0.1 collective-permute-start.3
  34.9 1.1 %collective-permute-done.5.refs_3_ = f32[8,128]{1,0:T(8,128)S(1)} collective-permute-done((f32[8,128]{1,0:T(8,128)S(1)}, f32[8,128]{1,0:T(8,128)S(1)}, u32[]{:S(2)}, u32[]{:S(2)}) %collective-permute-start.5) | collective-permute-done | bytes 4128 | tf_op jit(solution)/shard_map/ppermute | solution.py:419
  36.1 0.8 %collective-permute-done.4.refs_2_ = f32[8,128]{1,0:T(8,128)S(1)} collective-permute-done((f32[8,128]{1,0:T(8,128)S(1)}, f32[8,128]{1,0:T(8,128)S(1)}, u32[]{:S(2)}, u32[]{:S(2)}) %collective-permute-start.4) | collective-permute-done | bytes 4128 | tf_op jit(solution)/shard_map/ppermute | solution.py:419
  36.9 0.0 collective-permute-done.3.refs_1_
  36.9 0.8 %commands.3 = bf16[32,2,640]{2,1,0:T(2,128)(2,1)S(1)} custom-call(f32[8,128]{1,0:T(8,128)S(1)} %get-tuple-element.32.refs_0_, f32[8,128]{1,0:T(8,128)S(1)} %collective-permute-done.3.refs_1_, f32[8,128]{1,0:T(8,128)S(1)} %collective-permute-done.4.refs_2_, f32[8,128]{1,0:T(8,128)S(1)} %collective-permute-done.5.refs_3_, ...), custom_call_target="tpu_custom_call" | custom-call | tf_op jit(solution)/shard_map/commands/pallas_call | solution.py:360
  37.7 9.8 %all_to_all.16.parts_ref = bf16[32,2,640]{2,1,0:T(2,128)(2,1)S(1)} all-to-all(bf16[32,2,640]{2,1,0:T(2,128)(2,1)S(1)} %commands.3), channel_id=1, replica_groups=mesh['case'=4,'mod'=8] {'case','mod'}, dimensions={0} | all-to-all | bytes 163840 | tf_op jit(solution)/shard_map/all_to_all | solution.py:424
  47.5 0.7 %total.1 = (f32[1,5120]{1,0:T(1,128)}, f32[64,512]{1,0:T(8,128)}) custom-call(bf16[32,2,640]{2,1,0:T(2,128)(2,1)S(1)} %all_to_all.16.parts_ref, f32[8,640]{1,0:T(8,128)S(1)} %get-tuple-element.34.total_ref, f32[64,512]{1,0:T(8,128)S(1)} %get-tuple-element.35.frame_ref), custom_call_target="tpu_custom_call" | custom-call | tf_op jit(solution)/shard_map/total/pallas_call | solution.py:360
Async XLA Ops:
  1.9 13.6 %all-to-all-start = ((f32[8,1,128]{2,1,0:T(1,128)}), f32[8,1,128]{2,1,0:T(1,128)S(1)}, u32[]{:S(2)}, u32[]{:S(2)}) async-start(f32[8,1,128]{2,1,0:T(1,128)} %spread.1), calls=%async_computation | async-start | bytes 8192 | tf_op jit(solution)/shard_map/modulation_angles/all_to_all | solution.py:385
  16.9 3.2 %collective-permute-start.2 = (f32[8,128]{1,0:T(8,128)S(1)}, f32[8,128]{1,0:T(8,128)S(1)}, u32[]{:S(2)}, u32[]{:S(2)}) collective-permute-start(f32[8,128]{1,0:T(8,128)S(1)} %get-tuple-element.23.refs_0_), channel_id=1, source_target_pairs={{0,24},{8,16},{16,8},{24,0},{1,25},{9,17},{17,9},{25,1},{2,26},{10... | collective-permute-start | bytes 12296 | tf_op jit(solution)/shard_map/ppermute | solution.py:419
  17.0 3.7 %collective-permute-start.1 = (f32[8,128]{1,0:T(8,128)S(1)}, f32[8,128]{1,0:T(8,128)S(1)}, u32[]{:S(2)}, u32[]{:S(2)}) collective-permute-start(f32[8,128]{1,0:T(8,128)S(1)} %get-tuple-element.23.refs_0_), channel_id=1, source_target_pairs={{0,16},{8,24},{16,0},{24,8},{1,17},{9,25},{17,1},{25,9},{2,18},{10... | collective-permute-start | bytes 12296 | tf_op jit(solution)/shard_map/ppermute | solution.py:419
  18.6 2.1 %collective-permute-start = (f32[8,128]{1,0:T(8,128)S(1)}, f32[8,128]{1,0:T(8,128)S(1)}, u32[]{:S(2)}, u32[]{:S(2)}) collective-permute-start(f32[8,128]{1,0:T(8,128)S(1)} %get-tuple-element.23.refs_0_), channel_id=1, source_target_pairs={{0,8},{8,0},{16,24},{24,16},{1,9},{9,1},{17,25},{25,17},{2,10},{10... | collective-permute-start | bytes 12296 | tf_op jit(solution)/shard_map/ppermute | solution.py:419
  33.0 3.1 %collective-permute-start.5 = (f32[8,128]{1,0:T(8,128)S(1)}, f32[8,128]{1,0:T(8,128)S(1)}, u32[]{:S(2)}, u32[]{:S(2)}) collective-permute-start(f32[8,128]{1,0:T(8,128)S(1)} %get-tuple-element.32.refs_0_), channel_id=1, source_target_pairs={{0,24},{8,16},{16,8},{24,0},{1,25},{9,17},{17,9},{25,1},{2,26},{10... | collective-permute-start | bytes 12296 | tf_op jit(solution)/shard_map/ppermute | solution.py:419
  33.3 3.6 %collective-permute-start.4 = (f32[8,128]{1,0:T(8,128)S(1)}, f32[8,128]{1,0:T(8,128)S(1)}, u32[]{:S(2)}, u32[]{:S(2)}) collective-permute-start(f32[8,128]{1,0:T(8,128)S(1)} %get-tuple-element.32.refs_0_), channel_id=1, source_target_pairs={{0,16},{8,24},{16,0},{24,8},{1,17},{9,25},{17,1},{25,9},{2,18},{10... | collective-permute-start | bytes 12296 | tf_op jit(solution)/shard_map/ppermute | solution.py:419
  34.8 2.1 %collective-permute-start.3 = (f32[8,128]{1,0:T(8,128)S(1)}, f32[8,128]{1,0:T(8,128)S(1)}, u32[]{:S(2)}, u32[]{:S(2)}) collective-permute-start(f32[8,128]{1,0:T(8,128)S(1)} %get-tuple-element.32.refs_0_), channel_id=1, source_target_pairs={{0,8},{8,0},{16,24},{24,16},{1,9},{9,1},{17,25},{25,17},{2,10},{10... | collective-permute-start | bytes 12296 | tf_op jit(solution)/shard_map/ppermute | solution.py:419

commit v10 on v9

--- a/solution.py
+++ b/solution.py
@@ -167,10 +167,16 @@
     transposed = jnp.concatenate(spread, 0)
     high = transposed.astype(jnp.bfloat16).astype(f32)
     parts = jnp.concatenate([high, high, transposed - high], 0).astype(jnp.bfloat16)
-    high, low = halves(jnp.dot(gy_ref[...], parts, preferred_element_type=f32))
-    return lax.dot_general(
-        gx_ref[...], jnp.concatenate([high, low], 1), (((1,), (1,)), ((), ())), preferred_element_type=f32
-    )
+    out = []
+    step = gy_ref.shape[0] // 2
+    for start in range(0, gy_ref.shape[0], step):
+        high, low = halves(jnp.dot(gy_ref[start : start + step, :], parts, preferred_element_type=f32))
+        out.append(
+            lax.dot_general(
+                gx_ref[...], jnp.concatenate([high, low], 1), (((1,), (1,)), ((), ())), preferred_element_type=f32
+            )
+        )
+    return jnp.concatenate(out, 1)
 
 
 def tilt_factors(angles_ref, pupil, length):

time: 48.5 us -> 48.4 us (level)
  no operation moved by 1% of the time
where the time goes in v10:
time: 48.4 us; the launch traced here: 48.1 us
  blocking collectives  18.9 us (39%)
  starting transfers between devices  11.1 us (23%)
  Pallas kernels  9.73 us (20%)
  waiting for transfers between devices  6.99 us (14%)
  between operations  1.35 us (3%)
    all_to_all x2, blocking collectives, commands(): return lax.all_to_all(partial, ('case', 'mod'), 0, 0, tiled=True)  18.9 us
    pallas_call x8, Pallas kernels, call(): pl.pallas_call(kernel, out_shape=outs, in_specs=in_specs, out_specs=out_s...  9.73 us
    all_to_all x1, starting transfers between devices, body(): lax.all_to_all(angles, 'mod', 0, 0, tiled=True).reshape(count, LANES)  7.25 us
    all_to_all x1, waiting for transfers between devices, body(): lax.all_to_all(angles, 'mod', 0, 0, tiled=True).reshape(count, LANES)  4.45 us
    ppermute x6, starting transfers between devices, commands(): lax.ppermute(signal, 'case', [(i, i ^ j) for i in range(cases)])  3.88 us
    ppermute x6, waiting for transfers between devices, commands(): lax.ppermute(signal, 'case', [(i, i ^ j) for i in range(cases)])  2.54 us
  transfers between devices with their start and end apart: 7, of which 4 were waited for; matrix products, arithmetic and copies ran while one was open for 0% of the time, Pallas kernels for 7%

profile of v10, /device:TPU:0, one launch (start us, length us, event | category | flops | bytes accessed | tf_op | source)
XLA Modules:
  0.0 48.1 jit_solution(8064093180901083564)
XLA Ops:
  1.3 0.6 %spread.1 = f32[8,1,128]{2,1,0:T(1,128)} custom-call(s32[1]{0:T(128)S(6)} %copy.13.point_ref), custom_call_target="tpu_custom_call" | custom-call | tf_op jit(solution)/shard_map/modulation_angles/spread/pallas_call | solution.py:366
  1.9 7.3 %all-to-all-start = ((f32[8,1,128]{2,1,0:T(1,128)}), f32[8,1,128]{2,1,0:T(1,128)S(1)}, u32[]{:S(2)}, u32[]{:S(2)}) async-start(f32[8,1,128]{2,1,0:T(1,128)} %spread.1), calls=%async_computation | async-start | bytes 8192 | tf_op jit(solution)/shard_map/modulation_angles/all_to_all | solution.py:391
  9.1 1.9 %prepare.1 = (bf16[256,512]{1,0:T(8,128)(2,1)S(1)}, f32[64,512]{1,0:T(8,128)S(1)}, bf16[512,512]{1,0:T(8,128)(2,1)S(1)}, s32[40,128]{1,0:T(8,128)S(1)}, bf16[256...) custom-call(f32[256,256]{1,0:T(8,128)} %bitcast.8, ...), custom_call_target="tpu_custom_call" | custom-call | tf_op jit(solution)/shard_map/prepare/pallas_call | solution.py:366
  11.1 4.4 %all-to-all-done = f32[8,1,128]{2,1,0:T(1,128)S(1)} async-done(((f32[8,1,128]{2,1,0:T(1,128)}), f32[8,1,128]{2,1,0:T(1,128)S(1)}, u32[]{:S(2)}, u32[]{:S(2)}) %all-to-all-start) | async-done | bytes 4128 | tf_op jit(solution)/shard_map/modulation_angles/all_to_all | solution.py:391
  15.5 1.4 %first_frame.1 = (f32[8,128]{1,0:T(8,128)S(1)}, f32[2,8,256]{2,1,0:T(8,128)S(1)}, bf16[512,512]{1,0:T(8,128)(2,1)S(1)}) custom-call(f32[8,128]{1,0:T(8,128)S(1)} %bitcast.7, bf16[256,512]{1,0:T(8,128)(2,1)S(1)} %get-tuple-element.20.field_ref, f32[64,512]{1,0:T(8,128)S(1)} %get-tuple-element.21.rows_ref, bf16[512,512]{1,0:T(8,128)(2,1)S(1)} %get-tuple-element.22.full_ref, ...), custom_call_target="tpu_custom_call" | custom-call | tf_op jit(solution)/shard_map/first_frame/pallas_call | solution.py:366
  16.9 0.1 collective-permute-start.2
  17.0 1.6 %collective-permute-start.1 = (f32[8,128]{1,0:T(8,128)S(1)}, f32[8,128]{1,0:T(8,128)S(1)}, u32[]{:S(2)}, u32[]{:S(2)}) collective-permute-start(f32[8,128]{1,0:T(8,128)S(1)} %get-tuple-element.23.refs_0_), channel_id=1, source_target_pairs={{0,16},{8,24},{16,0},{24,8},{1,17},{9,25},{17,1},{25,9},{2,18},{10... | collective-permute-start | bytes 12296 | tf_op jit(solution)/shard_map/ppermute | solution.py:425
  18.6 0.3 collective-permute-start
  18.8 1.2 %fetch.1.refs_5_ = bf16[512,1024]{1,0:T(8,128)(2,1)S(1)} custom-call(f32[2,8,256]{2,1,0:T(8,128)S(1)} %get-tuple-element.25.tilt_ref, bf16[1280,1024]{1,0:T(8,128)(2,1)} %recon_hbm.5), custom_call_target="tpu_custom_call" | custom-call | bytes 2097152 | tf_op jit(solution)/shard_map/fetch/pallas_call | solution.py:366
  20.1 0.0 collective-permute-done.2.refs_3_
  20.1 0.6 %collective-permute-done.1.refs_2_ = f32[8,128]{1,0:T(8,128)S(1)} collective-permute-done((f32[8,128]{1,0:T(8,128)S(1)}, f32[8,128]{1,0:T(8,128)S(1)}, u32[]{:S(2)}, u32[]{:S(2)}) %collective-permute-start.1) | collective-permute-done | bytes 4128 | tf_op jit(solution)/shard_map/ppermute | solution.py:425
  20.7 0.0 collective-permute-done.refs_1_
  20.7 0.8 %commands.2 = bf16[32,2,640]{2,1,0:T(2,128)(2,1)S(1)} custom-call(f32[8,128]{1,0:T(8,128)S(1)} %get-tuple-element.23.refs_0_, f32[8,128]{1,0:T(8,128)S(1)} %collective-permute-done.refs_1_, f32[8,128]{1,0:T(8,128)S(1)} %collective-permute-done.1.refs_2_, f32[8,128]{1,0:T(8,128)S(1)} %collective-permute-done.2.refs_3_, ...), custom_call_target="tpu_custom_call" | custom-call | tf_op jit(solution)/shard_map/commands/pallas_call | solution.py:366
  21.5 9.1 %all_to_all.15.parts_ref = bf16[32,2,640]{2,1,0:T(2,128)(2,1)S(1)} all-to-all(bf16[32,2,640]{2,1,0:T(2,128)(2,1)S(1)} %commands.2), channel_id=1, replica_groups=mesh['case'=4,'mod'=8] {'case','mod'}, dimensions={0} | all-to-all | bytes 163840 | tf_op jit(solution)/shard_map/all_to_all | solution.py:430
  30.6 2.2 %next_frame.1 = (f32[64,512]{1,0:T(8,128)S(1)}, f32[8,128]{1,0:T(8,128)S(1)}, f32[8,640]{1,0:T(8,128)S(1)}, bf16[512,1024]{1,0:T(8,128)(2,1)S(1)}) custom-call(bf16[32,2,640]{2,1,0:T(2,128)(2,1)S(1)} %all_to_all.15.parts_ref, f32[2,8,256]{2,1,0:T(8,128)S(1)} %get-tuple-element.25.tilt_ref, s32[40,128]{1,0:T(8,128)S(1)} %get-tuple-element.26.cells_ref, ...), custom_call_target="tpu_custom_call" | custom-call | tf_op jit(solution)/shard_map/next_frame/pallas_call | solution.py:366
  32.9 0.3 collective-permute-start.5
  33.2 1.5 %collective-permute-start.4 = (f32[8,128]{1,0:T(8,128)S(1)}, f32[8,128]{1,0:T(8,128)S(1)}, u32[]{:S(2)}, u32[]{:S(2)}) collective-permute-start(f32[8,128]{1,0:T(8,128)S(1)} %get-tuple-element.32.refs_0_), channel_id=1, source_target_pairs={{0,16},{8,24},{16,0},{24,8},{1,17},{9,25},{17,1},{25,9},{2,18},{10... | collective-permute-start | bytes 12296 | tf_op jit(solution)/shard_map/ppermute | solution.py:425
  34.7 0.1 collective-permute-start.3
  34.8 1.1 %collective-permute-done.5.refs_3_ = f32[8,128]{1,0:T(8,128)S(1)} collective-permute-done((f32[8,128]{1,0:T(8,128)S(1)}, f32[8,128]{1,0:T(8,128)S(1)}, u32[]{:S(2)}, u32[]{:S(2)}) %collective-permute-start.5) | collective-permute-done | bytes 4128 | tf_op jit(solution)/shard_map/ppermute | solution.py:425
  36.0 0.8 %collective-permute-done.4.refs_2_ = f32[8,128]{1,0:T(8,128)S(1)} collective-permute-done((f32[8,128]{1,0:T(8,128)S(1)}, f32[8,128]{1,0:T(8,128)S(1)}, u32[]{:S(2)}, u32[]{:S(2)}) %collective-permute-start.4) | collective-permute-done | bytes 4128 | tf_op jit(solution)/shard_map/ppermute | solution.py:425
  36.8 0.0 collective-permute-done.3.refs_1_
  36.8 0.8 %commands.3 = bf16[32,2,640]{2,1,0:T(2,128)(2,1)S(1)} custom-call(f32[8,128]{1,0:T(8,128)S(1)} %get-tuple-element.32.refs_0_, f32[8,128]{1,0:T(8,128)S(1)} %collective-permute-done.3.refs_1_, f32[8,128]{1,0:T(8,128)S(1)} %collective-permute-done.4.refs_2_, f32[8,128]{1,0:T(8,128)S(1)} %collective-permute-done.5.refs_3_, ...), custom_call_target="tpu_custom_call" | custom-call | tf_op jit(solution)/shard_map/commands/pallas_call | solution.py:366
  37.6 9.8 %all_to_all.16.parts_ref = bf16[32,2,640]{2,1,0:T(2,128)(2,1)S(1)} all-to-all(bf16[32,2,640]{2,1,0:T(2,128)(2,1)S(1)} %commands.3), channel_id=1, replica_groups=mesh['case'=4,'mod'=8] {'case','mod'}, dimensions={0} | all-to-all | bytes 163840 | tf_op jit(solution)/shard_map/all_to_all | solution.py:430
  47.4 0.7 %total.1 = (f32[1,5120]{1,0:T(1,128)}, f32[64,512]{1,0:T(8,128)}) custom-call(bf16[32,2,640]{2,1,0:T(2,128)(2,1)S(1)} %all_to_all.16.parts_ref, f32[8,640]{1,0:T(8,128)S(1)} %get-tuple-element.34.total_ref, f32[64,512]{1,0:T(8,128)S(1)} %get-tuple-element.35.frame_ref), custom_call_target="tpu_custom_call" | custom-call | tf_op jit(solution)/shard_map/total/pallas_call | solution.py:366
Async XLA Ops:
  1.9 13.6 %all-to-all-start = ((f32[8,1,128]{2,1,0:T(1,128)}), f32[8,1,128]{2,1,0:T(1,128)S(1)}, u32[]{:S(2)}, u32[]{:S(2)}) async-start(f32[8,1,128]{2,1,0:T(1,128)} %spread.1), calls=%async_computation | async-start | bytes 8192 | tf_op jit(solution)/shard_map/modulation_angles/all_to_all | solution.py:391
  16.9 3.2 %collective-permute-start.2 = (f32[8,128]{1,0:T(8,128)S(1)}, f32[8,128]{1,0:T(8,128)S(1)}, u32[]{:S(2)}, u32[]{:S(2)}) collective-permute-start(f32[8,128]{1,0:T(8,128)S(1)} %get-tuple-element.23.refs_0_), channel_id=1, source_target_pairs={{0,24},{8,16},{16,8},{24,0},{1,25},{9,17},{17,9},{25,1},{2,26},{10... | collective-permute-start | bytes 12296 | tf_op jit(solution)/shard_map/ppermute | solution.py:425
  17.0 3.7 %collective-permute-start.1 = (f32[8,128]{1,0:T(8,128)S(1)}, f32[8,128]{1,0:T(8,128)S(1)}, u32[]{:S(2)}, u32[]{:S(2)}) collective-permute-start(f32[8,128]{1,0:T(8,128)S(1)} %get-tuple-element.23.refs_0_), channel_id=1, source_target_pairs={{0,16},{8,24},{16,0},{24,8},{1,17},{9,25},{17,1},{25,9},{2,18},{10... | collective-permute-start | bytes 12296 | tf_op jit(solution)/shard_map/ppermute | solution.py:425
  18.6 2.1 %collective-permute-start = (f32[8,128]{1,0:T(8,128)S(1)}, f32[8,128]{1,0:T(8,128)S(1)}, u32[]{:S(2)}, u32[]{:S(2)}) collective-permute-start(f32[8,128]{1,0:T(8,128)S(1)} %get-tuple-element.23.refs_0_), channel_id=1, source_target_pairs={{0,8},{8,0},{16,24},{24,16},{1,9},{9,1},{17,25},{25,17},{2,10},{10... | collective-permute-start | bytes 12296 | tf_op jit(solution)/shard_map/ppermute | solution.py:425
  32.9 3.1 %collective-permute-start.5 = (f32[8,128]{1,0:T(8,128)S(1)}, f32[8,128]{1,0:T(8,128)S(1)}, u32[]{:S(2)}, u32[]{:S(2)}) collective-permute-start(f32[8,128]{1,0:T(8,128)S(1)} %get-tuple-element.32.refs_0_), channel_id=1, source_target_pairs={{0,24},{8,16},{16,8},{24,0},{1,25},{9,17},{17,9},{25,1},{2,26},{10... | collective-permute-start | bytes 12296 | tf_op jit(solution)/shard_map/ppermute | solution.py:425
  33.2 3.6 %collective-permute-start.4 = (f32[8,128]{1,0:T(8,128)S(1)}, f32[8,128]{1,0:T(8,128)S(1)}, u32[]{:S(2)}, u32[]{:S(2)}) collective-permute-start(f32[8,128]{1,0:T(8,128)S(1)} %get-tuple-element.32.refs_0_), channel_id=1, source_target_pairs={{0,16},{8,24},{16,0},{24,8},{1,17},{9,25},{17,1},{25,9},{2,18},{10... | collective-permute-start | bytes 12296 | tf_op jit(solution)/shard_map/ppermute | solution.py:425
  34.7 2.1 %collective-permute-start.3 = (f32[8,128]{1,0:T(8,128)S(1)}, f32[8,128]{1,0:T(8,128)S(1)}, u32[]{:S(2)}, u32[]{:S(2)}) collective-permute-start(f32[8,128]{1,0:T(8,128)S(1)} %get-tuple-element.32.refs_0_), channel_id=1, source_target_pairs={{0,8},{8,0},{16,24},{24,16},{1,9},{9,1},{17,25},{25,17},{2,10},{10... | collective-permute-start | bytes 12296 | tf_op jit(solution)/shard_map/ppermute | solution.py:425

commit v11 on v10

--- a/solution.py
+++ b/solution.py
@@ -390,7 +390,7 @@
         )
         angles = lax.all_to_all(angles, "mod", 0, 0, tiled=True).reshape(count, LANES)
 
-    recon_early = block // LANES * 6 // 10 * LANES
+    recon_early = block // LANES * 5 // 10 * LANES
     late_shape = shape((block - recon_early, recon.shape[1]), bf16)
     map_shape = (act_map.shape[0] // LANES, LANES)
     field, rows, full, cells, gx_parts, gy_parts, recon_first, phase, amplitude = call(

time: 48.4 us -> 48.4 us (level)
  no operation moved by 1% of the time
where the time goes in v11:
time: 48.4 us; the launch traced here: 48.1 us
  blocking collectives  18.9 us (39%)
  starting transfers between devices  11.1 us (23%)
  Pallas kernels  9.73 us (20%)
  waiting for transfers between devices  6.99 us (14%)
  between operations  1.35 us (3%)
    all_to_all x2, blocking collectives, commands(): return lax.all_to_all(partial, ('case', 'mod'), 0, 0, tiled=True)  18.9 us
    pallas_call x8, Pallas kernels, call(): pl.pallas_call(kernel, out_shape=outs, in_specs=in_specs, out_specs=out_s...  9.73 us
    all_to_all x1, starting transfers between devices, body(): lax.all_to_all(angles, 'mod', 0, 0, tiled=True).reshape(count, LANES)  7.25 us
    all_to_all x1, waiting for transfers between devices, body(): lax.all_to_all(angles, 'mod', 0, 0, tiled=True).reshape(count, LANES)  4.54 us
    ppermute x6, starting transfers between devices, commands(): lax.ppermute(signal, 'case', [(i, i ^ j) for i in range(cases)])  3.88 us
    ppermute x6, waiting for transfers between devices, commands(): lax.ppermute(signal, 'case', [(i, i ^ j) for i in range(cases)])  2.45 us
  transfers between devices with their start and end apart: 7, of which 4 were waited for; matrix products, arithmetic and copies ran while one was open for 0% of the time, Pallas kernels for 7%

profile of v11, /device:TPU:0, one launch (start us, length us, event | category | flops | bytes accessed | tf_op | source)
XLA Modules:
  0.0 48.1 jit_solution(17996708917050228385)
XLA Ops:
  1.3 0.6 %spread.1 = f32[8,1,128]{2,1,0:T(1,128)} custom-call(s32[1]{0:T(128)S(6)} %copy.13.point_ref), custom_call_target="tpu_custom_call" | custom-call | tf_op jit(solution)/shard_map/modulation_angles/spread/pallas_call | solution.py:366
  1.9 7.3 %all-to-all-start = ((f32[8,1,128]{2,1,0:T(1,128)}), f32[8,1,128]{2,1,0:T(1,128)S(1)}, u32[]{:S(2)}, u32[]{:S(2)}) async-start(f32[8,1,128]{2,1,0:T(1,128)} %spread.1), calls=%async_computation | async-start | bytes 8192 | tf_op jit(solution)/shard_map/modulation_angles/all_to_all | solution.py:391
  9.1 1.8 %prepare.1 = (bf16[256,512]{1,0:T(8,128)(2,1)S(1)}, f32[64,512]{1,0:T(8,128)S(1)}, bf16[512,512]{1,0:T(8,128)(2,1)S(1)}, s32[40,128]{1,0:T(8,128)S(1)}, bf16[256...) custom-call(f32[256,256]{1,0:T(8,128)} %bitcast.8, ...), custom_call_target="tpu_custom_call" | custom-call | tf_op jit(solution)/shard_map/prepare/pallas_call | solution.py:366
  11.0 4.5 %all-to-all-done = f32[8,1,128]{2,1,0:T(1,128)S(1)} async-done(((f32[8,1,128]{2,1,0:T(1,128)}), f32[8,1,128]{2,1,0:T(1,128)S(1)}, u32[]{:S(2)}, u32[]{:S(2)}) %all-to-all-start) | async-done | bytes 4128 | tf_op jit(solution)/shard_map/modulation_angles/all_to_all | solution.py:391
  15.5 1.4 %first_frame.1 = (f32[8,128]{1,0:T(8,128)S(1)}, f32[2,8,256]{2,1,0:T(8,128)S(1)}, bf16[512,512]{1,0:T(8,128)(2,1)S(1)}) custom-call(f32[8,128]{1,0:T(8,128)S(1)} %bitcast.7, bf16[256,512]{1,0:T(8,128)(2,1)S(1)} %get-tuple-element.20.field_ref, f32[64,512]{1,0:T(8,128)S(1)} %get-tuple-element.21.rows_ref, bf16[512,512]{1,0:T(8,128)(2,1)S(1)} %get-tuple-element.22.full_ref, ...), custom_call_target="tpu_custom_call" | custom-call | tf_op jit(solution)/shard_map/first_frame/pallas_call | solution.py:366
  16.9 0.1 collective-permute-start.2
  17.0 1.6 %collective-permute-start.1 = (f32[8,128]{1,0:T(8,128)S(1)}, f32[8,128]{1,0:T(8,128)S(1)}, u32[]{:S(2)}, u32[]{:S(2)}) collective-permute-start(f32[8,128]{1,0:T(8,128)S(1)} %get-tuple-element.23.refs_0_), channel_id=1, source_target_pairs={{0,16},{8,24},{16,0},{24,8},{1,17},{9,25},{17,1},{25,9},{2,18},{10... | collective-permute-start | bytes 12296 | tf_op jit(solution)/shard_map/ppermute | solution.py:425
  18.6 0.3 collective-permute-start
  18.8 1.3 %fetch.1.refs_5_ = bf16[640,1024]{1,0:T(8,128)(2,1)S(1)} custom-call(f32[2,8,256]{2,1,0:T(8,128)S(1)} %get-tuple-element.25.tilt_ref, bf16[1280,1024]{1,0:T(8,128)(2,1)} %recon_hbm.5), custom_call_target="tpu_custom_call" | custom-call | bytes 2621440 | tf_op jit(solution)/shard_map/fetch/pallas_call | solution.py:366
  20.2 0.0 collective-permute-done.2.refs_3_
  20.2 0.5 %collective-permute-done.1.refs_2_ = f32[8,128]{1,0:T(8,128)S(1)} collective-permute-done((f32[8,128]{1,0:T(8,128)S(1)}, f32[8,128]{1,0:T(8,128)S(1)}, u32[]{:S(2)}, u32[]{:S(2)}) %collective-permute-start.1) | collective-permute-done | bytes 4128 | tf_op jit(solution)/shard_map/ppermute | solution.py:425
  20.7 0.0 collective-permute-done.refs_1_
  20.7 0.8 %commands.2 = bf16[32,2,640]{2,1,0:T(2,128)(2,1)S(1)} custom-call(f32[8,128]{1,0:T(8,128)S(1)} %get-tuple-element.23.refs_0_, f32[8,128]{1,0:T(8,128)S(1)} %collective-permute-done.refs_1_, f32[8,128]{1,0:T(8,128)S(1)} %collective-permute-done.1.refs_2_, f32[8,128]{1,0:T(8,128)S(1)} %collective-permute-done.2.refs_3_, ...), custom_call_target="tpu_custom_call" | custom-call | tf_op jit(solution)/shard_map/commands/pallas_call | solution.py:366
  21.5 9.1 %all_to_all.15.parts_ref = bf16[32,2,640]{2,1,0:T(2,128)(2,1)S(1)} all-to-all(bf16[32,2,640]{2,1,0:T(2,128)(2,1)S(1)} %commands.2), channel_id=1, replica_groups=mesh['case'=4,'mod'=8] {'case','mod'}, dimensions={0} | all-to-all | bytes 163840 | tf_op jit(solution)/shard_map/all_to_all | solution.py:430
  30.6 2.2 %next_frame.1 = (f32[64,512]{1,0:T(8,128)S(1)}, f32[8,128]{1,0:T(8,128)S(1)}, f32[8,640]{1,0:T(8,128)S(1)}, bf16[640,1024]{1,0:T(8,128)(2,1)S(1)}) custom-call(bf16[32,2,640]{2,1,0:T(2,128)(2,1)S(1)} %all_to_all.15.parts_ref, f32[2,8,256]{2,1,0:T(8,128)S(1)} %get-tuple-element.25.tilt_ref, s32[40,128]{1,0:T(8,128)S(1)} %get-tuple-element.26.cells_ref, ...), custom_call_target="tpu_custom_call" | custom-call | tf_op jit(solution)/shard_map/next_frame/pallas_call | solution.py:366
  32.9 0.3 collective-permute-start.5
  33.2 1.5 %collective-permute-start.4 = (f32[8,128]{1,0:T(8,128)S(1)}, f32[8,128]{1,0:T(8,128)S(1)}, u32[]{:S(2)}, u32[]{:S(2)}) collective-permute-start(f32[8,128]{1,0:T(8,128)S(1)} %get-tuple-element.32.refs_0_), channel_id=1, source_target_pairs={{0,16},{8,24},{16,0},{24,8},{1,17},{9,25},{17,1},{25,9},{2,18},{10... | collective-permute-start | bytes 12296 | tf_op jit(solution)/shard_map/ppermute | solution.py:425
  34.7 0.1 collective-permute-start.3
  34.8 1.1 %collective-permute-done.5.refs_3_ = f32[8,128]{1,0:T(8,128)S(1)} collective-permute-done((f32[8,128]{1,0:T(8,128)S(1)}, f32[8,128]{1,0:T(8,128)S(1)}, u32[]{:S(2)}, u32[]{:S(2)}) %collective-permute-start.5) | collective-permute-done | bytes 4128 | tf_op jit(solution)/shard_map/ppermute | solution.py:425
  36.0 0.8 %collective-permute-done.4.refs_2_ = f32[8,128]{1,0:T(8,128)S(1)} collective-permute-done((f32[8,128]{1,0:T(8,128)S(1)}, f32[8,128]{1,0:T(8,128)S(1)}, u32[]{:S(2)}, u32[]{:S(2)}) %collective-permute-start.4) | collective-permute-done | bytes 4128 | tf_op jit(solution)/shard_map/ppermute | solution.py:425
  36.8 0.0 collective-permute-done.3.refs_1_
  36.8 0.8 %commands.3 = bf16[32,2,640]{2,1,0:T(2,128)(2,1)S(1)} custom-call(f32[8,128]{1,0:T(8,128)S(1)} %get-tuple-element.32.refs_0_, f32[8,128]{1,0:T(8,128)S(1)} %collective-permute-done.3.refs_1_, f32[8,128]{1,0:T(8,128)S(1)} %collective-permute-done.4.refs_2_, f32[8,128]{1,0:T(8,128)S(1)} %collective-permute-done.5.refs_3_, ...), custom_call_target="tpu_custom_call" | custom-call | tf_op jit(solution)/shard_map/commands/pallas_call | solution.py:366
  37.6 9.8 %all_to_all.16.parts_ref = bf16[32,2,640]{2,1,0:T(2,128)(2,1)S(1)} all-to-all(bf16[32,2,640]{2,1,0:T(2,128)(2,1)S(1)} %commands.3), channel_id=1, replica_groups=mesh['case'=4,'mod'=8] {'case','mod'}, dimensions={0} | all-to-all | bytes 163840 | tf_op jit(solution)/shard_map/all_to_all | solution.py:430
  47.4 0.7 %total.1 = (f32[1,5120]{1,0:T(1,128)}, f32[64,512]{1,0:T(8,128)}) custom-call(bf16[32,2,640]{2,1,0:T(2,128)(2,1)S(1)} %all_to_all.16.parts_ref, f32[8,640]{1,0:T(8,128)S(1)} %get-tuple-element.34.total_ref, f32[64,512]{1,0:T(8,128)S(1)} %get-tuple-element.35.frame_ref), custom_call_target="tpu_custom_call" | custom-call | tf_op jit(solution)/shard_map/total/pallas_call | solution.py:366
Async XLA Ops:
  1.9 13.6 %all-to-all-start = ((f32[8,1,128]{2,1,0:T(1,128)}), f32[8,1,128]{2,1,0:T(1,128)S(1)}, u32[]{:S(2)}, u32[]{:S(2)}) async-start(f32[8,1,128]{2,1,0:T(1,128)} %spread.1), calls=%async_computation | async-start | bytes 8192 | tf_op jit(solution)/shard_map/modulation_angles/all_to_all | solution.py:391
  16.9 3.3 %collective-permute-start.2 = (f32[8,128]{1,0:T(8,128)S(1)}, f32[8,128]{1,0:T(8,128)S(1)}, u32[]{:S(2)}, u32[]{:S(2)}) collective-permute-start(f32[8,128]{1,0:T(8,128)S(1)} %get-tuple-element.23.refs_0_), channel_id=1, source_target_pairs={{0,24},{8,16},{16,8},{24,0},{1,25},{9,17},{17,9},{25,1},{2,26},{10... | collective-permute-start | bytes 12296 | tf_op jit(solution)/shard_map/ppermute | solution.py:425
  17.0 3.7 %collective-permute-start.1 = (f32[8,128]{1,0:T(8,128)S(1)}, f32[8,128]{1,0:T(8,128)S(1)}, u32[]{:S(2)}, u32[]{:S(2)}) collective-permute-start(f32[8,128]{1,0:T(8,128)S(1)} %get-tuple-element.23.refs_0_), channel_id=1, source_target_pairs={{0,16},{8,24},{16,0},{24,8},{1,17},{9,25},{17,1},{25,9},{2,18},{10... | collective-permute-start | bytes 12296 | tf_op jit(solution)/shard_map/ppermute | solution.py:425
  18.6 2.1 %collective-permute-start = (f32[8,128]{1,0:T(8,128)S(1)}, f32[8,128]{1,0:T(8,128)S(1)}, u32[]{:S(2)}, u32[]{:S(2)}) collective-permute-start(f32[8,128]{1,0:T(8,128)S(1)} %get-tuple-element.23.refs_0_), channel_id=1, source_target_pairs={{0,8},{8,0},{16,24},{24,16},{1,9},{9,1},{17,25},{25,17},{2,10},{10... | collective-permute-start | bytes 12296 | tf_op jit(solution)/shard_map/ppermute | solution.py:425
  32.9 3.1 %collective-permute-start.5 = (f32[8,128]{1,0:T(8,128)S(1)}, f32[8,128]{1,0:T(8,128)S(1)}, u32[]{:S(2)}, u32[]{:S(2)}) collective-permute-start(f32[8,128]{1,0:T(8,128)S(1)} %get-tuple-element.32.refs_0_), channel_id=1, source_target_pairs={{0,24},{8,16},{16,8},{24,0},{1,25},{9,17},{17,9},{25,1},{2,26},{10... | collective-permute-start | bytes 12296 | tf_op jit(solution)/shard_map/ppermute | solution.py:425
  33.2 3.6 %collective-permute-start.4 = (f32[8,128]{1,0:T(8,128)S(1)}, f32[8,128]{1,0:T(8,128)S(1)}, u32[]{:S(2)}, u32[]{:S(2)}) collective-permute-start(f32[8,128]{1,0:T(8,128)S(1)} %get-tuple-element.32.refs_0_), channel_id=1, source_target_pairs={{0,16},{8,24},{16,0},{24,8},{1,17},{9,25},{17,1},{25,9},{2,18},{10... | collective-permute-start | bytes 12296 | tf_op jit(solution)/shard_map/ppermute | solution.py:425
  34.7 2.1 %collective-permute-start.3 = (f32[8,128]{1,0:T(8,128)S(1)}, f32[8,128]{1,0:T(8,128)S(1)}, u32[]{:S(2)}, u32[]{:S(2)}) collective-permute-start(f32[8,128]{1,0:T(8,128)S(1)} %get-tuple-element.32.refs_0_), channel_id=1, source_target_pairs={{0,8},{8,0},{16,24},{24,16},{1,9},{9,1},{17,25},{25,17},{2,10},{10... | collective-permute-start | bytes 12296 | tf_op jit(solution)/shard_map/ppermute | solution.py:425
